TPU v7x, 32 devices: a whole 2x2x4 slice. The times are simulated.
32 devices in a mesh: dp: 2 (over y), expert: 16 (over z, x, core).
Axes of the slice: x: 2, y: 2, z: 4, core: 2. Of those that a mesh axis runs over, the one named last changes fastest.
Arguments:
- tokens: bfloat16 [12288, 1024], P(('dp', 'expert')), may hold values from -6 to 6
- cotangent: bfloat16 [12288, 1024], P(('dp', 'expert')), may hold values from -6 to 6
- routes: int32 [12288, 8], P(('dp', 'expert')), may hold values from 0 to 15, all different within a row
- cont_group: int32 [32], P(('dp', 'expert')), may hold values from 0 to 1
- attn_gain: float32 [1024], P('dp'), may hold values from 0.5 to 1.5
- qkv_weight: float32 [1024, 2048], P('dp'), may hold values from -0.1875 to 0.1875
- out_weight: float32 [1024, 1024], P('dp'), may hold values from -3 to 3
- ffn_gain: float32 [1024], P('dp'), may hold values from 0.5 to 1.5
- router_weight: float32 [1024, 16], P('dp'), may hold values from -0.09375 to 0.09375
- gate_up_weight: float32 [16, 1024, 1024], P('expert', 'dp'), may hold values from -0.1875 to 0.1875
- down_weight: float32 [16, 512, 1024], P('expert', 'dp'), may hold values from -1 to 1
- mean_attn_gain: float32 [1024], P('dp'), may hold values from -0.625 to 0.625
- mean_qkv_weight: float32 [1024, 2048], P('dp'), may hold values from -0.625 to 0.625
- mean_out_weight: float32 [1024, 1024], P('dp'), may hold values from -0.625 to 0.625
- mean_ffn_gain: float32 [1024], P('dp'), may hold values from -0.625 to 0.625
- mean_router_weight: float32 [1024, 16], P('dp'), may hold values from -0.625 to 0.625
- mean_gate_up_weight: float32 [16, 1024, 1024], P('expert', 'dp'), may hold values from -0.625 to 0.625
- mean_down_weight: float32 [16, 512, 1024], P('expert', 'dp'), may hold values from -0.125 to 0.125
- square_attn_gain: float32 [1024], P('dp'), may hold values from 0.1 to 1
- square_qkv_weight: float32 [1024, 2048], P('dp'), may hold values from 0.1 to 1
- square_out_weight: float32 [1024, 1024], P('dp'), may hold values from 0.0005 to 0.005
- square_ffn_gain: float32 [1024], P('dp'), may hold values from 0.1 to 1
- square_router_weight: float32 [1024, 16], P('dp'), may hold values from 0.1 to 1
- square_gate_up_weight: float32 [16, 1024, 1024], P('expert', 'dp'), may hold values from 0.002 to 0.02
- square_down_weight: float32 [16, 512, 1024], P('expert', 'dp'), may hold values from 5e-05 to 0.0005
Outputs:
- output: bfloat16 [12288, 1024], P(('dp', 'expert'))
- input_grad: float32 [12288, 1024], P(('dp', 'expert'))
- update_attn_gain: float32 [1024], replicated
- update_qkv_weight: float32 [1024, 2048], replicated
- update_out_weight: float32 [1024, 1024], replicated
- update_ffn_gain: float32 [1024], replicated
- update_router_weight: float32 [1024, 16], replicated
- update_gate_up_weight: float32 [16, 1024, 1024], P('expert')
- update_down_weight: float32 [16, 512, 1024], P('expert')
- new_mean_attn_gain: float32 [1024], P('dp')
- new_mean_qkv_weight: float32 [1024, 2048], P('dp')
- new_mean_out_weight: float32 [1024, 1024], P('dp')
- new_mean_ffn_gain: float32 [1024], P('dp')
- new_mean_router_weight: float32 [1024, 16], P('dp')
- new_mean_gate_up_weight: float32 [16, 1024, 1024], P('expert', 'dp')
- new_mean_down_weight: float32 [16, 512, 1024], P('expert', 'dp')
- new_square_attn_gain: float32 [1024], P('dp')
- new_square_qkv_weight: float32 [1024, 2048], P('dp')
- new_square_out_weight: float32 [1024, 1024], P('dp')
- new_square_ffn_gain: float32 [1024], P('dp')
- new_square_router_weight: float32 [1024, 16], P('dp')
- new_square_gate_up_weight: float32 [16, 1024, 1024], P('expert', 'dp')
- new_square_down_weight: float32 [16, 512, 1024], P('expert', 'dp')
Inputs may be any that keep to these rules, and one draw needn't show every extreme that they name: `routes`: each row names 8 different experts.
All inputs are finite; a program needn't handle non-finite values.
Results may differ from a plain program's by a relative error of at most 0.04.
Values may be sent and summed in bfloat16 or wider, within the bound.
No kernel may reach another device: no remote copies, remote signals or barrier semaphores. Data moves between devices by JAX's collectives and lax.ppermute only.
A program may use at most 320 MiB of HBM per device.

v0:
```python
import math

import jax
import jax.numpy as jnp
from jax import lax
from jax.sharding import PartitionSpec as P

HEADS = 16
KV_HEADS = 8
HEAD_DIM = 64
EXP_FF = 512
TOPK = 8
NPROMPT = 2
PROMPT_DEV = 128
CLEN = 128


norm_eps = 1e-05
masked_score = -1e30
decay_rate = 0.1
adam_eps = 1e-08
bias_first = 0.999973438601112
bias_second = 0.99407947078


def rotate(values, cosine, sine_part):
    half_dim = values.shape[-1] // 2
    first_half = values[..., :half_dim]
    second_half = values[..., half_dim:]
    return jnp.concatenate(
        [
            first_half * cosine - second_half * sine_part,
            second_half * cosine + first_half * sine_part,
        ],
        axis=-1,
    )


def norm_back(values, scale_rows, gain_row, grad_rows):
    normed = values * scale_rows
    grad_normed = grad_rows * gain_row
    grad_values = scale_rows * (
        grad_normed - normed * jnp.mean(grad_normed * normed, axis=-1, keepdims=True)
    )
    return (grad_values, jnp.sum(grad_rows * normed, axis=0))


def online_step(carried, scores, allowed, value_heads, pattern):
    running_max, running_sum, running_acc = carried
    scores = jnp.where(allowed, scores, masked_score)
    new_max = jnp.maximum(running_max, jnp.max(scores, axis=-1))
    factor = jnp.exp(running_max - new_max)
    weights = jnp.where(allowed, jnp.exp(scores - new_max[..., None]), 0.0)
    new_sum = running_sum * factor + jnp.sum(weights, axis=-1)
    new_acc = running_acc * factor[..., None] + jnp.einsum(
        pattern, weights.astype(jnp.bfloat16), value_heads, preferred_element_type=jnp.float32
    )
    return (new_max, new_sum, new_acc)


def adamw(weight, mean_in, square_in, gradient, grad_scale, decay_factor):
    scaled = gradient * grad_scale
    mean_out = 0.9 * mean_in + 0.1 * scaled
    square_out = 0.95 * square_in + 0.05 * scaled * scaled
    update = mean_out / bias_first / (jnp.sqrt(square_out / bias_second) + adam_eps)
    return (update + decay_factor * weight, mean_out, square_out)


def per_device(
    tokens,
    cotangent,
    routes,
    cont_group,
    attn_gain,
    qkv_weight,
    out_weight,
    ffn_gain,
    router_weight,
    gate_up_weight,
    down_weight,
    mean_attn_gain,
    mean_qkv_weight,
    mean_out_weight,
    mean_ffn_gain,
    mean_router_weight,
    mean_gate_up_weight,
    mean_down_weight,
    square_attn_gain,
    square_qkv_weight,
    square_out_weight,
    square_ffn_gain,
    square_router_weight,
    square_gate_up_weight,
    square_down_weight,
):
    members = lax.axis_size("expert")
    groups_dp = lax.axis_size("dp")
    member = lax.axis_index("expert")
    tok_count = tokens.shape[0]
    model_width = tokens.shape[1]
    experts = router_weight.shape[1]
    local_experts = gate_up_weight.shape[0]
    capacity = 5 * tok_count * TOPK // (4 * experts)
    pair_count = tok_count * TOPK
    prompt_rows = NPROMPT * PROMPT_DEV
    prompt_len = PROMPT_DEV * members
    repeat = HEADS // KV_HEADS
    query_width = HEADS * HEAD_DIM
    key_width = KV_HEADS * HEAD_DIM
    score_scale = HEAD_DIM ** (-0.5)
    gathered = (
        lax.all_gather(attn_gain.astype(jnp.bfloat16), "dp", axis=0, tiled=True),
        lax.all_gather(qkv_weight.astype(jnp.bfloat16), "dp", axis=0, tiled=True),
        lax.all_gather(out_weight.astype(jnp.bfloat16), "dp", axis=0, tiled=True),
        lax.all_gather(ffn_gain.astype(jnp.bfloat16), "dp", axis=0, tiled=True),
        lax.all_gather(router_weight.astype(jnp.bfloat16), "dp", axis=0, tiled=True),
        lax.all_gather(gate_up_weight.astype(jnp.bfloat16), "dp", axis=1, tiled=True),
        lax.all_gather(down_weight.astype(jnp.bfloat16), "dp", axis=1, tiled=True),
    )
    gain_attn, proj_qkv, proj_out, gain_ffn, proj_router, proj_gate_up, proj_down = gathered
    tok_float = tokens.astype(jnp.float32)
    scale_attn = lax.rsqrt(jnp.mean(tok_float * tok_float, axis=-1, keepdims=True) + norm_eps)
    gain_attn_float = gain_attn.astype(jnp.float32)
    attn_in = (tok_float * scale_attn * gain_attn_float).astype(jnp.bfloat16)
    projected = jnp.dot(attn_in, proj_qkv, preferred_element_type=jnp.float32)
    row_index = jnp.arange(tok_count, dtype=jnp.int32)
    position = jnp.where(
        row_index < prompt_rows,
        member * PROMPT_DEV + row_index // NPROMPT,
        prompt_len + row_index - prompt_rows,
    )
    half_dim = HEAD_DIM // 2
    frequency = jnp.exp(
        jnp.arange(half_dim, dtype=jnp.float32) * (-2.0 * math.log(10000.0) / HEAD_DIM)
    )
    angles = position.astype(jnp.float32)[:, None] * frequency[None, :]
    cosine = jnp.cos(angles)[:, None, :]
    sine_part = jnp.sin(angles)[:, None, :]
    queries = rotate(
        projected[:, :query_width].reshape(tok_count, HEADS, HEAD_DIM), cosine, sine_part
    ).astype(jnp.bfloat16)
    key_rows = rotate(
        projected[:, query_width : query_width + key_width].reshape(tok_count, KV_HEADS, HEAD_DIM),
        cosine,
        sine_part,
    ).astype(jnp.bfloat16)
    value_rows = (
        projected[:, query_width + key_width :]
        .astype(jnp.bfloat16)
        .reshape(tok_count, KV_HEADS, HEAD_DIM)
    )
    query_prompt = queries[:prompt_rows].reshape(PROMPT_DEV, NPROMPT, KV_HEADS, repeat, HEAD_DIM)
    query_cont = queries[prompt_rows:].reshape(CLEN, KV_HEADS, repeat, HEAD_DIM)
    key_prompt = key_rows[:prompt_rows].reshape(PROMPT_DEV, NPROMPT, key_width)
    value_prompt = value_rows[:prompt_rows].reshape(PROMPT_DEV, NPROMPT, key_width)
    key_cont = key_rows[prompt_rows:]
    value_cont = value_rows[prompt_rows:]
    group_id = cont_group[0]
    query_pos = member * PROMPT_DEV + jnp.arange(PROMPT_DEV, dtype=jnp.int32)
    cont_pos = jnp.arange(CLEN, dtype=jnp.int32)
    causal = cont_pos[None, :] <= cont_pos[:, None]

    def fold_block(carried, key_piece, value_piece, start_row):
        width = key_piece.shape[0]
        key_heads = key_piece.reshape(width, NPROMPT, KV_HEADS, HEAD_DIM)
        value_heads = value_piece.reshape(width, NPROMPT, KV_HEADS, HEAD_DIM)
        key_pos = start_row + jnp.arange(width, dtype=jnp.int32)
        allowed = (key_pos[None, :] <= query_pos[:, None])[None, None, None]
        prompt_scores = (
            jnp.einsum(
                "ignrd,jgnd->gnrij", query_prompt, key_heads, preferred_element_type=jnp.float32
            )
            * score_scale
        )
        prompt_state = online_step(
            carried[0], prompt_scores, allowed, value_heads, "gnrij,jgnd->gnrid"
        )
        chosen_keys = lax.dynamic_index_in_dim(key_heads, group_id, 1, keepdims=False)
        chosen_values = lax.dynamic_index_in_dim(value_heads, group_id, 1, keepdims=False)
        cont_scores = (
            jnp.einsum(
                "cnrd,jnd->nrcj", query_cont, chosen_keys, preferred_element_type=jnp.float32
            )
            * score_scale
        )
        cont_state = online_step(
            carried[1],
            cont_scores,
            jnp.ones((1, 1, 1, width), jnp.bool_),
            chosen_values,
            "nrcj,jnd->nrcd",
        )
        return (prompt_state, cont_state)

    prompt_init = (
        jnp.full((NPROMPT, KV_HEADS, repeat, PROMPT_DEV), masked_score, jnp.float32),
        jnp.zeros((NPROMPT, KV_HEADS, repeat, PROMPT_DEV), jnp.float32),
        jnp.zeros((NPROMPT, KV_HEADS, repeat, PROMPT_DEV, HEAD_DIM), jnp.float32),
    )
    cont_init = (
        jnp.full((KV_HEADS, repeat, CLEN), masked_score, jnp.float32),
        jnp.zeros((KV_HEADS, repeat, CLEN), jnp.float32),
        jnp.zeros((KV_HEADS, repeat, CLEN, HEAD_DIM), jnp.float32),
    )
    pieces = (
        lax.all_gather(key_prompt, "expert", axis=0, tiled=True),
        lax.all_gather(value_prompt, "expert", axis=0, tiled=True),
    )
    width = pieces[0].shape[0]
    block_rows = math.gcd(width, 512)

    def scan_step(inner_state, block_index):
        first_row = block_index * block_rows
        key_piece = lax.dynamic_slice_in_dim(pieces[0], first_row, block_rows, 0)
        value_piece = lax.dynamic_slice_in_dim(pieces[1], first_row, block_rows, 0)
        return (fold_block(inner_state, key_piece, value_piece, first_row), None)

    result, _ = lax.scan(
        scan_step, (prompt_init, cont_init), jnp.arange(width // block_rows, dtype=jnp.int32)
    )
    self_scores = (
        jnp.einsum("cnrd,jnd->nrcj", query_cont, key_cont, preferred_element_type=jnp.float32)
        * score_scale
    )
    cont_final = online_step(
        result[1], self_scores, causal[None, None], value_cont, "nrcj,jnd->nrcd"
    )
    prompt_final = result[0]
    prompt_heads = prompt_final[2] / prompt_final[1][..., None]
    prompt_lse = prompt_final[0] + jnp.log(prompt_final[1])
    cont_heads = cont_final[2] / cont_final[1][..., None]
    cont_lse = cont_final[0] + jnp.log(cont_final[1])
    mixed_heads = jnp.concatenate(
        [
            prompt_heads.transpose(3, 0, 1, 2, 4).reshape(prompt_rows, query_width),
            cont_heads.transpose(2, 0, 1, 3).reshape(CLEN, query_width),
        ],
        axis=0,
    )
    mixed_low = mixed_heads.astype(jnp.bfloat16)
    hidden = tok_float + jnp.dot(mixed_low, proj_out, preferred_element_type=jnp.float32)
    scale_ffn = lax.rsqrt(jnp.mean(hidden * hidden, axis=-1, keepdims=True) + norm_eps)
    gain_ffn_float = gain_ffn.astype(jnp.float32)
    ffn_in = (hidden * scale_ffn * gain_ffn_float).astype(jnp.bfloat16)
    logits = jnp.dot(ffn_in, proj_router, preferred_element_type=jnp.float32)
    expert_ids = jnp.arange(experts, dtype=jnp.int32)
    one_hot = routes[:, :, None] == expert_ids[None, None, :]
    hot_float = one_hot.astype(jnp.float32)
    chosen = jnp.sum(logits[:, None, :] * hot_float, axis=-1)
    gate_probs = jax.nn.softmax(chosen, axis=-1)
    hot_pairs = one_hot.reshape(pair_count, experts).astype(jnp.int32)
    placed = jnp.sum((jnp.cumsum(hot_pairs, axis=0) - hot_pairs) * hot_pairs, axis=-1)
    flat_routes = routes.reshape(pair_count)
    kept_pairs = placed < capacity
    slots = jnp.where(kept_pairs, flat_routes * capacity + placed, 0)
    target = jnp.where(kept_pairs, slots, experts * capacity)
    slot_table = (
        jnp.full((experts * capacity,), pair_count, jnp.int32)
        .at[target]
        .set(jnp.arange(pair_count, dtype=jnp.int32), mode="drop")
    )
    filled = slot_table < pair_count
    slot_pairs = jnp.where(filled, slot_table, 0)
    zero_low = jnp.zeros((), jnp.bfloat16)
    send_rows = jnp.where(filled[:, None], ffn_in[slot_pairs // TOPK], zero_low)
    arrived = lax.all_to_all(
        send_rows.reshape(members, local_experts * capacity, model_width),
        "expert",
        split_axis=0,
        concat_axis=0,
        tiled=True,
    )
    arrived = arrived.reshape(members, local_experts, capacity, model_width)
    gate_up = jnp.einsum(
        "secd,edf->secf", arrived, proj_gate_up, preferred_element_type=jnp.float32
    )
    gate_lin = gate_up[..., :EXP_FF]
    up_lin = gate_up[..., EXP_FF:]
    activated = (jax.nn.silu(gate_lin) * up_lin).astype(jnp.bfloat16)
    expert_out = jnp.einsum(
        "secf,efd->secd", activated, proj_down, preferred_element_type=jnp.float32
    ).astype(jnp.bfloat16)
    returned = lax.all_to_all(
        expert_out.reshape(members, local_experts * capacity, model_width),
        "expert",
        split_axis=0,
        concat_axis=0,
        tiled=True,
    )
    returned = returned.reshape(experts * capacity, model_width)
    pair_out = jnp.where(kept_pairs[:, None], returned[slots], zero_low).reshape(
        tok_count, TOPK, model_width
    )
    pair_weight = jnp.where(kept_pairs.reshape(tok_count, TOPK), gate_probs, 0.0)
    mixture = jnp.einsum("tk,tkd->td", pair_weight, pair_out, preferred_element_type=jnp.float32)
    output = (hidden + mixture).astype(jnp.bfloat16)
    grad_output = cotangent.astype(jnp.float32)
    grad_gate = jnp.einsum("tkd,td->tk", pair_out, grad_output, preferred_element_type=jnp.float32)
    grad_pair = (
        (pair_weight[:, :, None] * grad_output[:, None, :])
        .astype(jnp.bfloat16)
        .reshape(pair_count, model_width)
    )
    grad_slots = jnp.where(filled[:, None], grad_pair[slot_pairs], zero_low)
    grad_expert_out = lax.all_to_all(
        grad_slots.reshape(members, local_experts * capacity, model_width),
        "expert",
        split_axis=0,
        concat_axis=0,
        tiled=True,
    )
    grad_expert_out = grad_expert_out.reshape(members, local_experts, capacity, model_width)
    grad_activated = jnp.einsum(
        "secd,efd->secf", grad_expert_out, proj_down, preferred_element_type=jnp.float32
    )
    grad_down = jnp.einsum(
        "secf,secd->efd", activated, grad_expert_out, preferred_element_type=jnp.float32
    )
    sigmoid_gate = jax.nn.sigmoid(gate_lin)
    silu_gate = gate_lin * sigmoid_gate
    grad_gate_lin = grad_activated * up_lin * sigmoid_gate * (1.0 + gate_lin * (1.0 - sigmoid_gate))
    grad_up_lin = grad_activated * silu_gate
    grad_gate_up = jnp.concatenate([grad_gate_lin, grad_up_lin], axis=-1).astype(jnp.bfloat16)
    grad_gate_up_weight = jnp.einsum(
        "secd,secf->edf", arrived, grad_gate_up, preferred_element_type=jnp.float32
    )
    grad_arrived = jnp.einsum(
        "secf,edf->secd", grad_gate_up, proj_gate_up, preferred_element_type=jnp.float32
    ).astype(jnp.bfloat16)
    grad_returned = lax.all_to_all(
        grad_arrived.reshape(members, local_experts * capacity, model_width),
        "expert",
        split_axis=0,
        concat_axis=0,
        tiled=True,
    )
    grad_returned = grad_returned.reshape(experts * capacity, model_width)
    grad_pair_rows = jnp.where(kept_pairs[:, None], grad_returned[slots], zero_low).reshape(
        tok_count, TOPK, model_width
    )
    grad_from_experts = jnp.sum(grad_pair_rows, axis=1, dtype=jnp.float32)
    grad_chosen = gate_probs * (grad_gate - jnp.sum(gate_probs * grad_gate, axis=-1, keepdims=True))
    grad_logits = jnp.einsum("tk,tke->te", grad_chosen, hot_float).astype(jnp.bfloat16)
    grad_router = jnp.dot(ffn_in.T, grad_logits, preferred_element_type=jnp.float32)
    grad_ffn = grad_from_experts + jnp.dot(
        grad_logits, proj_router.T, preferred_element_type=jnp.float32
    )
    grad_hidden_norm, grad_gain_ffn = norm_back(hidden, scale_ffn, gain_ffn_float, grad_ffn)
    grad_hidden = grad_output + grad_hidden_norm
    grad_attn = grad_hidden.astype(jnp.bfloat16)
    grad_out_weight = jnp.dot(mixed_low.T, grad_attn, preferred_element_type=jnp.float32)
    grad_mixed = jnp.dot(grad_attn, proj_out.T, preferred_element_type=jnp.float32).astype(
        jnp.bfloat16
    )
    delta_rows = jnp.sum(
        grad_mixed.reshape(tok_count, HEADS, HEAD_DIM).astype(jnp.float32)
        * mixed_heads.reshape(tok_count, HEADS, HEAD_DIM),
        axis=-1,
    )
    delta_prompt = (
        delta_rows[:prompt_rows]
        .reshape(PROMPT_DEV, NPROMPT, KV_HEADS, repeat)
        .transpose(1, 2, 3, 0)
    )
    delta_cont = delta_rows[prompt_rows:].reshape(CLEN, KV_HEADS, repeat).transpose(1, 2, 0)
    grad_prompt_heads = grad_mixed[:prompt_rows].reshape(
        PROMPT_DEV, NPROMPT, KV_HEADS, repeat, HEAD_DIM
    )
    grad_cont_heads = grad_mixed[prompt_rows:].reshape(CLEN, KV_HEADS, repeat, HEAD_DIM)
    back_keys, back_values = (
        lax.all_gather(key_prompt, "expert", axis=0, tiled=True),
        lax.all_gather(value_prompt, "expert", axis=0, tiled=True),
    )
    back_rows = math.gcd(512, prompt_len)
    pick = (jnp.arange(NPROMPT, dtype=jnp.int32) == group_id).astype(jnp.float32)

    def back_block(grads_query, start_row, rows_now):
        key_heads = lax.dynamic_slice_in_dim(back_keys, start_row, rows_now, 0).reshape(
            rows_now, NPROMPT, KV_HEADS, HEAD_DIM
        )
        value_heads = lax.dynamic_slice_in_dim(back_values, start_row, rows_now, 0).reshape(
            rows_now, NPROMPT, KV_HEADS, HEAD_DIM
        )
        key_pos = start_row + jnp.arange(rows_now, dtype=jnp.int32)
        allowed = (key_pos[None, :] <= query_pos[:, None])[None, None, None]
        scores = (
            jnp.einsum(
                "ignrd,jgnd->gnrij", query_prompt, key_heads, preferred_element_type=jnp.float32
            )
            * score_scale
        )
        prob_rows = jnp.where(allowed, jnp.exp(scores - prompt_lse[..., None]), 0.0)
        grad_probs = jnp.einsum(
            "ignrd,jgnd->gnrij", grad_prompt_heads, value_heads, preferred_element_type=jnp.float32
        )
        grad_scores = (prob_rows * (grad_probs - delta_prompt[..., None])).astype(jnp.bfloat16)
        query_prompt_grad = (
            grads_query[0]
            + jnp.einsum(
                "gnrij,jgnd->ignrd", grad_scores, key_heads, preferred_element_type=jnp.float32
            )
            * score_scale
        )
        key_grad_prompt = (
            jnp.einsum(
                "gnrij,ignrd->jgnd", grad_scores, query_prompt, preferred_element_type=jnp.float32
            )
            * score_scale
        )
        value_grad_prompt = jnp.einsum(
            "gnrij,ignrd->jgnd",
            prob_rows.astype(jnp.bfloat16),
            grad_prompt_heads,
            preferred_element_type=jnp.float32,
        )
        chosen_keys = lax.dynamic_index_in_dim(key_heads, group_id, 1, keepdims=False)
        chosen_values = lax.dynamic_index_in_dim(value_heads, group_id, 1, keepdims=False)
        cont_scores = (
            jnp.einsum(
                "cnrd,jnd->nrcj", query_cont, chosen_keys, preferred_element_type=jnp.float32
            )
            * score_scale
        )
        cont_probs = jnp.exp(cont_scores - cont_lse[..., None])
        cont_grad_probs = jnp.einsum(
            "cnrd,jnd->nrcj", grad_cont_heads, chosen_values, preferred_element_type=jnp.float32
        )
        cont_grad_scores = (cont_probs * (cont_grad_probs - delta_cont[..., None])).astype(
            jnp.bfloat16
        )
        query_cont_grad = (
            grads_query[1]
            + jnp.einsum(
                "nrcj,jnd->cnrd", cont_grad_scores, chosen_keys, preferred_element_type=jnp.float32
            )
            * score_scale
        )
        key_grad_cont = (
            jnp.einsum(
                "nrcj,cnrd->jnd", cont_grad_scores, query_cont, preferred_element_type=jnp.float32
            )
            * score_scale
        )
        value_grad_cont = jnp.einsum(
            "nrcj,cnrd->jnd",
            cont_probs.astype(jnp.bfloat16),
            grad_cont_heads,
            preferred_element_type=jnp.float32,
        )
        key_term = key_grad_prompt + pick[None, :, None, None] * key_grad_cont[:, None]
        value_term = value_grad_prompt + pick[None, :, None, None] * value_grad_cont[:, None]
        return (
            (query_prompt_grad, query_cont_grad),
            (
                key_term.reshape(rows_now, NPROMPT, key_width),
                value_term.reshape(rows_now, NPROMPT, key_width),
            ),
        )

    def back_step(grads_query, block_index):
        return back_block(grads_query, block_index * back_rows, back_rows)

    query_grads_init = (
        jnp.zeros((PROMPT_DEV, NPROMPT, KV_HEADS, repeat, HEAD_DIM), jnp.float32),
        jnp.zeros((CLEN, KV_HEADS, repeat, HEAD_DIM), jnp.float32),
    )
    query_grads, key_value_terms = lax.scan(
        back_step, query_grads_init, jnp.arange(prompt_len // back_rows, dtype=jnp.int32)
    )
    key_terms = key_value_terms[0].reshape(prompt_len, NPROMPT, key_width)
    value_terms = key_value_terms[1].reshape(prompt_len, NPROMPT, key_width)
    grad_key_prompt, grad_value_prompt = (
        lax.psum_scatter(
            key_terms.astype(jnp.bfloat16), "expert", scatter_dimension=0, tiled=True
        ).astype(jnp.float32),
        lax.psum_scatter(
            value_terms.astype(jnp.bfloat16), "expert", scatter_dimension=0, tiled=True
        ).astype(jnp.float32),
    )
    self_probs = jnp.where(causal[None, None], jnp.exp(self_scores - cont_lse[..., None]), 0.0)
    self_grad_probs = jnp.einsum(
        "cnrd,jnd->nrcj", grad_cont_heads, value_cont, preferred_element_type=jnp.float32
    )
    self_grad_scores = (self_probs * (self_grad_probs - delta_cont[..., None])).astype(jnp.bfloat16)
    grad_query_cont = (
        query_grads[1]
        + jnp.einsum(
            "nrcj,jnd->cnrd", self_grad_scores, key_cont, preferred_element_type=jnp.float32
        )
        * score_scale
    )
    grad_key_self = (
        jnp.einsum(
            "nrcj,cnrd->jnd", self_grad_scores, query_cont, preferred_element_type=jnp.float32
        )
        * score_scale
    )
    grad_value_self = jnp.einsum(
        "nrcj,cnrd->jnd",
        self_probs.astype(jnp.bfloat16),
        grad_cont_heads,
        preferred_element_type=jnp.float32,
    )
    grad_queries = jnp.concatenate(
        [
            query_grads[0].reshape(prompt_rows, HEADS, HEAD_DIM),
            grad_query_cont.reshape(CLEN, HEADS, HEAD_DIM),
        ],
        axis=0,
    )
    grad_keys = jnp.concatenate(
        [grad_key_prompt.reshape(prompt_rows, KV_HEADS, HEAD_DIM), grad_key_self], axis=0
    )
    grad_values = jnp.concatenate(
        [
            grad_value_prompt.reshape(prompt_rows, key_width),
            grad_value_self.reshape(CLEN, key_width),
        ],
        axis=0,
    )
    grad_projected = jnp.concatenate(
        [
            rotate(grad_queries, cosine, -sine_part).reshape(tok_count, query_width),
            rotate(grad_keys, cosine, -sine_part).reshape(tok_count, key_width),
            grad_values,
        ],
        axis=-1,
    ).astype(jnp.bfloat16)
    grad_qkv_weight = jnp.dot(attn_in.T, grad_projected, preferred_element_type=jnp.float32)
    grad_attn_in = jnp.dot(grad_projected, proj_qkv.T, preferred_element_type=jnp.float32)
    grad_tok_norm, grad_gain_attn = norm_back(tok_float, scale_attn, gain_attn_float, grad_attn_in)
    input_grad = grad_hidden + grad_tok_norm
    dense_total = (
        lax.psum(grad_gain_attn.astype(jnp.bfloat16), "expert").astype(jnp.float32),
        lax.psum(grad_qkv_weight.astype(jnp.bfloat16), "expert").astype(jnp.float32),
        lax.psum(grad_out_weight.astype(jnp.bfloat16), "expert").astype(jnp.float32),
        lax.psum(grad_gain_ffn.astype(jnp.bfloat16), "expert").astype(jnp.float32),
        lax.psum(grad_router.astype(jnp.bfloat16), "expert").astype(jnp.float32),
    )
    shards = (
        lax.psum_scatter(
            dense_total[0].astype(jnp.bfloat16), "dp", scatter_dimension=0, tiled=True
        ).astype(jnp.float32),
        lax.psum_scatter(
            dense_total[1].astype(jnp.bfloat16), "dp", scatter_dimension=0, tiled=True
        ).astype(jnp.float32),
        lax.psum_scatter(
            dense_total[2].astype(jnp.bfloat16), "dp", scatter_dimension=0, tiled=True
        ).astype(jnp.float32),
        lax.psum_scatter(
            dense_total[3].astype(jnp.bfloat16), "dp", scatter_dimension=0, tiled=True
        ).astype(jnp.float32),
        lax.psum_scatter(
            dense_total[4].astype(jnp.bfloat16), "dp", scatter_dimension=0, tiled=True
        ).astype(jnp.float32),
        lax.psum_scatter(
            grad_gate_up_weight.astype(jnp.bfloat16), "dp", scatter_dimension=1, tiled=True
        ).astype(jnp.float32),
        lax.psum_scatter(
            grad_down.astype(jnp.bfloat16), "dp", scatter_dimension=1, tiled=True
        ).astype(jnp.float32),
    )
    grad_scale = (tok_count * groups_dp * members) ** (-0.5)
    weights_now = (
        attn_gain,
        qkv_weight,
        out_weight,
        ffn_gain,
        router_weight,
        gate_up_weight,
        down_weight,
    )
    means_now = (
        mean_attn_gain,
        mean_qkv_weight,
        mean_out_weight,
        mean_ffn_gain,
        mean_router_weight,
        mean_gate_up_weight,
        mean_down_weight,
    )
    squares_now = (
        square_attn_gain,
        square_qkv_weight,
        square_out_weight,
        square_ffn_gain,
        square_router_weight,
        square_gate_up_weight,
        square_down_weight,
    )
    decays = (0.0, decay_rate, decay_rate, 0.0, decay_rate, decay_rate, decay_rate)
    updated = [
        adamw(weight_one, mean_one, square_one, shard_one, grad_scale, decay_one)
        for weight_one, mean_one, square_one, shard_one, decay_one in zip(
            weights_now, means_now, squares_now, shards, decays
        )
    ]
    new_steps = (
        lax.all_gather(updated[0][0].astype(jnp.bfloat16), "dp", axis=0, tiled=True).astype(
            jnp.float32
        ),
        lax.all_gather(updated[1][0].astype(jnp.bfloat16), "dp", axis=0, tiled=True).astype(
            jnp.float32
        ),
        lax.all_gather(updated[2][0].astype(jnp.bfloat16), "dp", axis=0, tiled=True).astype(
            jnp.float32
        ),
        lax.all_gather(updated[3][0].astype(jnp.bfloat16), "dp", axis=0, tiled=True).astype(
            jnp.float32
        ),
        lax.all_gather(updated[4][0].astype(jnp.bfloat16), "dp", axis=0, tiled=True).astype(
            jnp.float32
        ),
        lax.all_gather(updated[5][0].astype(jnp.bfloat16), "dp", axis=1, tiled=True).astype(
            jnp.float32
        ),
        lax.all_gather(updated[6][0].astype(jnp.bfloat16), "dp", axis=1, tiled=True).astype(
            jnp.float32
        ),
    )
    return (
        output,
        input_grad,
        new_steps[0],
        new_steps[1],
        new_steps[2],
        new_steps[3],
        new_steps[4],
        new_steps[5],
        new_steps[6],
        updated[0][1],
        updated[1][1],
        updated[2][1],
        updated[3][1],
        updated[4][1],
        updated[5][1],
        updated[6][1],
        updated[0][2],
        updated[1][2],
        updated[2][2],
        updated[3][2],
        updated[4][2],
        updated[5][2],
        updated[6][2],
    )


def solution(mesh):
    return jax.shard_map(
        per_device,
        mesh=mesh,
        in_specs=(
            P(("dp", "expert"), None),
            P(("dp", "expert"), None),
            P(("dp", "expert"), None),
            P(("dp", "expert")),
            P("dp"),
            P("dp", None),
            P("dp", None),
            P("dp"),
            P("dp", None),
            P("expert", "dp", None),
            P("expert", "dp", None),
            P("dp"),
            P("dp", None),
            P("dp", None),
            P("dp"),
            P("dp", None),
            P("expert", "dp", None),
            P("expert", "dp", None),
            P("dp"),
            P("dp", None),
            P("dp", None),
            P("dp"),
            P("dp", None),
            P("expert", "dp", None),
            P("expert", "dp", None),
        ),
        out_specs=(
            P(("dp", "expert"), None),
            P(("dp", "expert"), None),
            P(),
            P(),
            P(),
            P(),
            P(),
            P("expert", None, None),
            P("expert", None, None),
            P("dp"),
            P("dp", None),
            P("dp", None),
            P("dp"),
            P("dp", None),
            P("expert", "dp", None),
            P("expert", "dp", None),
            P("dp"),
            P("dp", None),
            P("dp", None),
            P("dp"),
            P("dp", None),
            P("expert", "dp", None),
            P("expert", "dp", None),
        ),
        check_vma=False,
    )
```

profile of v0, /device:TPU:0, one launch (start us, length us, event | category | flops | bytes accessed | tf_op | source)
XLA Modules:
  0.0 1906.5 jit_solution(11326839973411782534)
XLA Ops:
  11.3 5.3 all-gather
  17.7 53.1 %all-gather.15.cloned.1.call-done = bf16[1024,2048]{1,0:T(8,128)(2,1)} async-done(((bf16[512,2048]{1,0:T(8,128)(2,1)}), bf16[1024,2048]{1,0:T(8,128)(2,1)}) %all-gather.15.cloned.1.call-update) | async-done | bytes 4194320 | tf_op jit(solution)/shard_map/all_gather | solution.py:113
  70.8 5.2 fusion.222
  86.2 4.6 reduce-window.6
  92.6 11.8 scatter_custom_fusion
  105.1 4.3 all-gather.1
  117.7 15.5 all-gather.17.cloned.1.call-done
  133.3 11.1 copy.222
  144.4 43.3 %all-gather.19.cloned.1.call-done = bf16[2048,2,512]{0,2,1:T(8,128)(2,1)} async-done(((bf16[128,2,512]{0,2,1:T(8,128)(2,1)}), bf16[2048,2,512]{0,2,1:T(8,128)(2,1)}) %all-gather.19.cloned.1.call-update) | async-done | bytes 4194320 | tf_op jit(solution)/shard_map/all_gather | solution.py:207
  187.8 79.0 %while.42 = (s32[]{:T(128)}, f32[2,8,2,128]{3,2,1,0:T(2,128)S(1)}, f32[2,8,2,128]{3,2,1,0:T(2,128)S(1)}, f32[2,8,2,128,64]{3,4,2,1,0:T(8,128)}, f32[8,2,128]{2,1...) while((s32[]{:T(128)}, f32[2,8,2,128]{3,2,1,0:T(2,128)S(1)}, ...), condition=%wide.region_6.7_spmd.clone, body=%wide.region_1.6_spmd.clone.sunk | while | flops 842234496 | bytes 74847568 | solution.py:218
  277.1 12.6 gather_fusion
  289.7 7.0 broadcast_select_fusion.3
  296.7 5.3 all-to-all-start
  305.4 33.2 %all-gather.23.cloned.1.call-done = bf16[1,1024,1024]{2,1,0:T(8,128)(2,1)} async-done(((bf16[1,512,1024]{2,1,0:T(8,128)(2,1)}), bf16[1,1024,1024]{2,1,0:T(8,128)(2,1)}) %all-gather.23.cloned.1.call-update) | async-done | bytes 2097168 | tf_op jit(solution)/shard_map/all_gather | solution.py:117
  338.6 104.5 %all-to-all-done = bf16[16,240,1024]{2,1,0:T(8,128)(2,1)} async-done(((bf16[16,240,1024]{2,1,0:T(8,128)(2,1)}), bf16[16,240,1024]{2,1,0:T(8,128)(2,1)}, u32[]{:S(2)}, u32[]{:S(2)}) %all-to-all-start) | async-done | bytes 7864352 | tf_op jit(solution)/shard_map/all_to_all | solution.py:266
  443.1 11.5 convolution_bitcast_fusion.1
  454.6 5.4 copy-done.13
  464.1 9.9 convolution_convert_fusion.1
  474.0 34.6 %all-to-all-start.1 = ((bf16[16,240,1024]{2,1,0:T(8,128)(2,1)}), bf16[16,240,1024]{2,1,0:T(8,128)(2,1)}, u32[]{:S(2)}, u32[]{:S(2)}) async-start(bf16[16,240,1024]{2,1,0:T(8,128)(2,1)} %convolution_convert_fusion.1), calls=%async_computation.1 | async-start | bytes 15728640 | tf_op jit(solution)/shard_map/all_to_all | solution.py:283
  509.0 4.6 all_gather.56
  514.0 136.2 %all-to-all-done.1 = bf16[16,240,1024]{2,1,0:T(8,128)(2,1)} async-done(((bf16[16,240,1024]{2,1,0:T(8,128)(2,1)}), bf16[16,240,1024]{2,1,0:T(8,128)(2,1)}, u32[]{:S(2)}, u32[]{:S(2)}) %all-to-all-start.1) | async-done | bytes 7864352 | tf_op jit(solution)/shard_map/all_to_all | solution.py:283
  650.2 20.1 %gather_fusion.1 = bf16[3072,1024]{1,0:T(8,128)(2,1)} fusion(bf16[3840,1024]{1,0:T(8,128)(2,1)} %bitcast.31, s32[3072]{0:T(1024)S(1)} %broadcast_clamp_fusion), kind=kCustom, calls=%fused_computation.1 | custom fusion | bytes 12595200 | tf_op jit(solution)/shard_map/gather | solution.py:291
  670.2 6.6 fusion.89
  680.6 21.0 %gather_fusion.2 = bf16[3840,1024]{1,0:T(8,128)(2,1)} fusion(bf16[3072,1024]{1,0:T(8,128)(2,1)} %fusion.83, s32[4096]{0:T(1024)S(1)} %copy-done.64), kind=kCustom, calls=%fused_computation.2 | custom fusion | bytes 15744000 | tf_op jit(solution)/shard_map/gather | solution.py:304
  701.6 5.2 broadcast_select_fusion.2
  706.8 205.7 %all_to_all.20 = bf16[16,240,1024]{2,1,0:T(8,128)(2,1)} all-to-all(bf16[16,240,1024]{2,1,0:T(8,128)(2,1)S(1)} %broadcast_select_fusion.2), channel_id=1, replica_groups=mesh['dp'=2,'expert'=16] {'expert'}, dimensions={0} | all-to-all | bytes 15728640 | tf_op jit(solution)/shard_map/all_to_all | solution.py:305
  912.6 12.6 fusion.97
  925.1 14.2 convolution_convert_fusion
  939.3 5.8 all-to-all-start.3
  949.2 4.8 fusion.90
  953.9 132.8 %all-to-all-done.3 = bf16[16,240,1024]{2,1,0:T(8,128)(2,1)} async-done(((bf16[16,240,1024]{2,1,0:T(8,128)(2,1)}), bf16[16,240,1024]{2,1,0:T(8,128)(2,1)}, u32[]{:S(2)}, u32[]{:S(2)}) %all-to-all-start.3) | async-done | bytes 7864352 | tf_op jit(solution)/shard_map/all_to_all | solution.py:330
  1086.7 20.1 %gather_fusion.3 = bf16[3072,1024]{1,0:T(8,128)(2,1)} fusion(bf16[3840,1024]{1,0:T(8,128)(2,1)} %bitcast.44, s32[3072]{0:T(1024)S(1)} %broadcast_clamp_fusion), kind=kCustom, calls=%fused_computation.3 | custom fusion | bytes 12595200 | tf_op jit(solution)/shard_map/gather | solution.py:338
  1106.8 6.1 convert_reduce_fusion
  1126.3 167.6 %while.43 = (s32[]{:T(128)}, f32[128,2,8,2,64]{0,4,3,2,1:T(8,128)}, f32[128,8,2,64]{0,3,2,1:T(8,128)}, bf16[4,512,2,512]{3,1,0,2:T(8,128)(2,1)}, bf16[4,512,2,51...) while((s32[]{:T(128)}, f32[128,2,8,2,64]{0,4,3,2,1:T(8,128)}, ...), condition=%wide.region_22.23_spmd.clone, body=%wide.region_21.22_spmd.clone.sunk | while | flops 2047804032 | bytes 154941360 | solution.py:467
  1133.7 4.4 fusion.352
  1150.7 6.2 bitcast_add_fusion.5
  1174.5 4.4 fusion.352
  1191.6 6.2 bitcast_add_fusion.5
  1216.7 4.4 fusion.352
  1233.7 6.2 bitcast_add_fusion.5
  1258.9 4.4 fusion.352
  1275.9 6.2 bitcast_add_fusion.5
  1309.4 86.7 %reduce-scatter.8.cloned.1.call-done = bf16[128,2,512]{2,0,1:T(8,128)(2,1)} async-done(((bf16[2048,2,512]{2,0,1:T(8,128)(2,1)}), bf16[128,2,512]{2,0,1:T(8,128)(2,1)}) %reduce-scatter.8.cloned.1.call-update) | async-done | bytes 262160 | tf_op jit(solution)/shard_map/reduce_scatter | solution.py:473
  1398.3 74.3 %reduce-scatter.10.cloned.1.call-done = bf16[128,2,512]{2,0,1:T(8,128)(2,1)} async-done(((bf16[2048,2,512]{2,0,1:T(8,128)(2,1)}), bf16[128,2,512]{2,0,1:T(8,128)(2,1)}) %reduce-scatter.10.cloned.1.call-update) | async-done | bytes 262160 | tf_op jit(solution)/shard_map/reduce_scatter | solution.py:476
  1474.3 5.7 convolution_convert_fusion.2
  1480.1 10.0 fusion.123
  1490.2 14.2 fusion.112
  1506.3 57.1 %reduce-scatter.16.cloned.1.call-done = bf16[512,2048]{1,0:T(8,128)(2,1)} async-done(((bf16[1024,2048]{1,0:T(8,128)(2,1)}), bf16[512,2048]{1,0:T(8,128)(2,1)}) %reduce-scatter.16.cloned.1.call-update) | async-done | bytes 2097168 | tf_op jit(solution)/shard_map/reduce_scatter | solution.py:544
  1563.5 23.1 %reduce-scatter.14.cloned.1.call-done = bf16[1,256,1024]{2,1,0:T(8,128)(2,1)} async-done(((bf16[1,512,1024]{2,1,0:T(8,128)(2,1)}), bf16[1,256,1024]{2,1,0:T(8,128)(2,1)}) %reduce-scatter.14.cloned.1.call-update) | async-done | bytes 524304 | tf_op jit(solution)/shard_map/reduce_scatter | solution.py:559
  1590.8 30.5 %reduce-scatter.12.cloned.1.call-done = bf16[1,512,1024]{2,1,0:T(8,128)(2,1)} async-done(((bf16[1,1024,1024]{2,1,0:T(8,128)(2,1)}), bf16[1,512,1024]{2,1,0:T(8,128)(2,1)}) %reduce-scatter.12.cloned.1.call-update) | async-done | bytes 1048592 | tf_op jit(solution)/shard_map/reduce_scatter | solution.py:556
  1621.3 6.1 add_convert_fusion.1
  1628.5 100.4 %all-reduce.7.cloned.1.call-done = (bf16[512,2048]{1,0:T(8,128)(2,1)}, bf16[512,1024]{1,0:T(8,128)(2,1)}) async-done(((bf16[512,2048]{1,0:T(8,128)(2,1)}, bf16[512,1024]{1,0:T(8,128)(2,1)}), (bf16[512,2048]{1,0:T(8,128)(2,1)}, bf16[512,1024]{1,0:T(8,128)(2,1)})) %all-reduce.7.cloned.1.call-update) | async-done | bytes 3145744 | tf_op jit(solution)/shard_map/psum | solution.py:535
  1728.9 6.9 add_convert_fusion.2
  1735.9 9.2 add_convert_fusion
  1746.4 4.8 all-gather.33.cloned.1.call-done
  1753.9 32.3 %all-gather.31.cloned.1.call-done = bf16[1,1024,1024]{2,1,0:T(8,128)(2,1)} async-done(((bf16[1,512,1024]{2,1,0:T(8,128)(2,1)}), bf16[1,1024,1024]{2,1,0:T(8,128)(2,1)}) %all-gather.31.cloned.1.call-update) | async-done | bytes 2097168 | tf_op jit(solution)/shard_map/all_gather | solution.py:614
  1790.5 5.0 fusion.118
  1795.5 5.1 all-reduce.4
  1800.7 60.0 %all-reduce.2 = (bf16[512]{0:T(512)(128)(2,1)S(1)}, bf16[512]{0:T(512)(128)(2,1)S(1)}, bf16[512,16]{0,1:T(8,128)(2,1)S(1)}) all-reduce(bf16[512]{0:T(512)(128)(2,1)S(1)} %dynamic-slice.1, bf16[512]{0:T(512)(128)(2,1)S(1)} %dynamic-slice.3, ...), channel_id=1, replica_groups=mesh['dp'=2,'expert'=16] {'expert'}, use_global_device_ids=true, to_apply=%region_27.28 | all-reduce | flops 9216 | bytes 36864 | tf_op jit(solution)/shard_map/psum | solution.py:534
  1862.2 4.7 all_gather.63
  1868.9 4.3 all-gather.2
  1875.1 4.3 all-gather.3
  1887.8 4.7 all-gather.27.cloned.1.call-done
  1892.5 6.7 convert_element_type.302
  (546 shorter events, 310.5 us)
Async XLA Ops:
  7.2 9.4 copy-start.26
  7.2 63.6 %all-gather.15.cloned.1.call-start = ((), (), s32[]{:S(2)}) async-start(), calls=%async_computation.11 | async-start | bytes 6291456 | tf_op jit(solution)/shard_map/all_gather | solution.py:113
  11.2 122.1 %all-gather.17.cloned.1.call-start = ((), (), s32[]{:S(2)}) async-start(), calls=%async_computation.12 | async-start | bytes 4456448 | tf_op jit(solution)/shard_map/all_gather | solution.py:206
  16.5 59.5 %copy-start.70 = (f32[2,1,512]{2,1,0:T(1,128)}, f32[2,1,512]{2,1,0:T(1,128)S(1)}, u32[]{:S(2)}) copy-start(f32[2,1,512]{2,1,0:T(1,128)S(1)} %convert_element_type.326) | copy-start | bytes 12292
  16.8 59.2 %copy-start.72 = (f32[384]{0:T(512)}, f32[384]{0:T(512)S(1)}, u32[]{:S(2)}) copy-start(f32[384]{0:T(512)S(1)} %add_rsqrt_fusion.1) | copy-start | bytes 4612
  17.7 94.4 %copy-start.41 = (f32[384,32]{0,1:T(8,128)}, f32[384,32]{0,1:T(8,128)S(1)}, u32[]{:S(2)}) copy-start(f32[384,32]{0,1:T(8,128)S(1)} %get-tuple-element.820) | copy-start | bytes 147460
  82.4 105.4 %all-gather.19.cloned.1.call-start = ((), (), s32[]{:S(2)}) async-start(), calls=%async_computation.13 | async-start | bytes 4456448 | tf_op jit(solution)/shard_map/all_gather | solution.py:207
  83.5 21.5 %copy-start.77 = (f32[512]{0:T(512)S(1)}, f32[512]{0:T(512)}, u32[]{:S(2)}) copy-start(f32[512]{0:T(512)} %param.36) | copy-start | bytes 6148
  84.5 188.5 %all-gather.21.cloned.1.call-start = ((), (), s32[]{:S(2)}) async-start(), calls=%async_computation.14 | async-start | bytes 3145728 | tf_op jit(solution)/shard_map/all_gather | solution.py:114
  85.8 181.8 %copy-start.55 = (pred[128,128]{0,1:T(8,128)(4,1)}, pred[128,128]{0,1:T(8,128)(4,1)S(1)}, u32[]{:S(2)}) copy-start(pred[128,128]{0,1:T(8,128)(4,1)S(1)} %iota_compare_fusion.3) | copy-start | bytes 49156
  91.9 20.5 %copy-start.60 = (s32[3072]{0:T(1024)}, s32[3072]{0:T(1024)S(1)}, u32[]{:S(2)}) copy-start(s32[3072]{0:T(1024)S(1)} %fusion.164) | copy-start | bytes 36868
  109.4 166.4 %copy-start.65 = (f32[2,1,512]{2,1,0:T(1,128)}, f32[2,1,512]{2,1,0:T(1,128)S(1)}, u32[]{:S(2)}) copy-start(f32[2,1,512]{2,1,0:T(1,128)S(1)} %convert_element_type.327) | copy-start | bytes 12292
  117.7 149.9 %copy-start.11 = (f32[8,2,128,128]{2,3,1,0:T(8,128)}, f32[8,2,128,128]{2,3,1,0:T(8,128)S(1)}, u32[]{:S(2)}) copy-start(f32[8,2,128,128]{2,3,1,0:T(8,128)S(1)} %get-tuple-element.824) | copy-start | bytes 3145732
  275.8 13.9 copy-start.68
  277.1 236.4 %copy-start = (bf16[384,1024]{1,0:T(8,128)(2,1)}, bf16[384,1024]{1,0:T(8,128)(2,1)S(1)}, u32[]{:S(2)}) copy-start(bf16[384,1024]{1,0:T(8,128)(2,1)S(1)} %multiply_convert_fusion.1) | copy-start | bytes 2359300
  296.7 146.4 %all-to-all-start = ((bf16[16,240,1024]{2,1,0:T(8,128)(2,1)}), bf16[16,240,1024]{2,1,0:T(8,128)(2,1)}, u32[]{:S(2)}, u32[]{:S(2)}) async-start(bf16[16,240,1024]{2,1,0:T(8,128)(2,1)} %broadcast_select_fusion.3), calls=%async_computation | async-start | bytes 15728640 | tf_op jit(solution)/shard_map/all_to_all | solution.py:266
  302.0 36.6 %all-gather.23.cloned.1.call-start = ((), (), s32[]{:S(2)}) async-start(), calls=%async_computation.15 | async-start | bytes 3145728 | tf_op jit(solution)/shard_map/all_gather | solution.py:117
  303.2 160.9 %all-gather.25.cloned.1.call-start = ((), (), s32[]{:S(2)}) async-start(), calls=%async_computation.16 | async-start | bytes 1572864 | tf_op jit(solution)/shard_map/all_gather | solution.py:118
  474.0 34.6 %copy-start.61 = (s32[3072]{0:T(1024)S(1)}, s32[3072]{0:T(1024)}, u32[]{:S(2)}) copy-start(s32[3072]{0:T(1024)} %copy-done.60) | copy-start | bytes 36868
  474.0 34.8 %copy-start.63 = (f32[512,16]{0,1:T(8,128)S(1)}, f32[512,16]{0,1:T(8,128)}, u32[]{:S(2)}) copy-start(f32[512,16]{0,1:T(8,128)} %param.37) | copy-start | bytes 98308
  474.0 34.8 %copy-start.23 = (bf16[384,1024]{1,0:T(8,128)(2,1)S(1)}, bf16[384,1024]{1,0:T(8,128)(2,1)}, u32[]{:S(2)}) copy-start(bf16[384,1024]{1,0:T(8,128)(2,1)} %param.30) | copy-start | bytes 2359300
  474.0 39.6 %copy-start.67 = (s32[3072,1]{0,1:T(1,128)S(1)}, s32[3072,1]{0,1:T(1,128)}, u32[]{:S(2)}) copy-start(s32[3072,1]{0,1:T(1,128)} %get-tuple-element.814) | copy-start | bytes 36868
  474.0 39.9 %copy-start.59 = (s32[384,8]{0,1:T(8,128)S(1)}, s32[384,8]{0,1:T(8,128)}, u32[]{:S(2)}) copy-start(s32[384,8]{0,1:T(8,128)} %param.31) | copy-start | bytes 36868
  474.0 176.1 %all-to-all-start.1 = ((bf16[16,240,1024]{2,1,0:T(8,128)(2,1)}), bf16[16,240,1024]{2,1,0:T(8,128)(2,1)}, u32[]{:S(2)}, u32[]{:S(2)}) async-start(bf16[16,240,1024]{2,1,0:T(8,128)(2,1)} %convolution_convert_fusion.1), calls=%async_computation.1 | async-start | bytes 15728640 | tf_op jit(solution)/shard_map/all_to_all | solution.py:283
  701.6 210.9 %slice-start = ((s8[15728640]{0:T(1024)(128)(4,1)}), s8[4194304]{0:T(1024)(128)(4,1)S(1)}, s32[]{:S(2)}) async-start(s8[15728640]{0:T(1024)(128)(4,1)} %bitcast.519), calls=%async_computation.29 | async-start | bytes 8388608
  701.6 210.9 %slice-start.1 = ((s8[15728640]{0:T(1024)(128)(4,1)}), s8[4194304]{0:T(1024)(128)(4,1)S(1)}, s32[]{:S(2)}) async-start(s8[15728640]{0:T(1024)(128)(4,1)} %bitcast.519), calls=%async_computation.30 | async-start | bytes 8388608
  701.6 210.9 %slice-start.2 = ((s8[15728640]{0:T(1024)(128)(4,1)}), s8[4194304]{0:T(1024)(128)(4,1)S(1)}, s32[]{:S(2)}) async-start(s8[15728640]{0:T(1024)(128)(4,1)} %bitcast.519), calls=%async_computation.31 | async-start | bytes 8388608
  706.8 205.7 %slice-start.3 = ((s8[15728640]{0:T(1024)(128)(4,1)}), s8[3145728]{0:T(1024)(128)(4,1)S(1)}, s32[]{:S(2)}) async-start(s8[15728640]{0:T(1024)(128)(4,1)} %bitcast.519), calls=%async_computation.32 | async-start | bytes 6291456
  706.8 205.7 %copy-start.80 = (bf16[1,512,1024]{2,1,0:T(8,128)(2,1)S(1)}, bf16[1,512,1024]{2,1,0:T(8,128)(2,1)}, u32[]{:S(2)}) copy-start(bf16[1,512,1024]{2,1,0:T(8,128)(2,1)} %all-gather.25.cloned.1.call-done) | copy-start | bytes 3145732
  939.3 6.4 copy-start.22
  939.3 147.4 %all-to-all-start.3 = ((bf16[16,240,1024]{2,1,0:T(8,128)(2,1)}), bf16[16,240,1024]{2,1,0:T(8,128)(2,1)}, u32[]{:S(2)}, u32[]{:S(2)}) async-start(bf16[16,240,1024]{2,1,0:T(8,128)(2,1)} %convolution_convert_fusion), calls=%async_computation.3 | async-start | bytes 15728640 | tf_op jit(solution)/shard_map/all_to_all | solution.py:330
  945.1 451.0 %reduce-scatter.8.cloned.1.call-start = ((), (), s32[]{:S(2)}) async-start(), calls=%async_computation.17 | async-start | bytes 4456448 | tf_op jit(solution)/shard_map/reduce_scatter | solution.py:473
  949.1 163.7 %copy-start.49 = (bf16[384,16]{1,0:T(8,128)(2,1)}, bf16[384,16]{1,0:T(8,128)(2,1)S(1)}, u32[]{:S(2)}) copy-start(bf16[384,16]{1,0:T(8,128)(2,1)S(1)} %copy.283) | copy-start | bytes 36868
  1106.8 6.1 copy-start.69
  1131.4 6.6 copy-start.5
  1172.2 6.7 copy-start.5
  1214.4 6.6 copy-start.5
  1256.6 6.6 copy-start.5
  1293.9 178.7 %reduce-scatter.10.cloned.1.call-start = ((), (), s32[]{:S(2)}) async-start(), calls=%async_computation.18 | async-start | bytes 4456448 | tf_op jit(solution)/shard_map/reduce_scatter | solution.py:476
  1294.7 211.6 %reduce-scatter.18.cloned.1.call-start = ((), (), s32[]{:S(2)}) async-start(), calls=%async_computation.26 | async-start | bytes 3145728 | tf_op jit(solution)/shard_map/reduce_scatter | solution.py:547
  1299.0 264.5 %reduce-scatter.16.cloned.1.call-start = ((), (), s32[]{:S(2)}) async-start(), calls=%async_computation.25 | async-start | bytes 6291456 | tf_op jit(solution)/shard_map/reduce_scatter | solution.py:544
  1299.1 6.4 copy-start.32
  1309.0 165.1 %copy-start.48 = (f32[128,8,64]{0,2,1:T(8,128)S(1)}, f32[128,8,64]{0,2,1:T(8,128)}, u32[]{:S(2)}) copy-start(f32[128,8,64]{0,2,1:T(8,128)} %fusion.132) | copy-start | bytes 786436
  1309.4 170.7 %copy-start.62 = (bf16[8,64,128]{2,1,0:T(8,128)(2,1)}, bf16[8,64,128]{2,1,0:T(8,128)(2,1)S(1)}, u32[]{:S(2)}) copy-start(bf16[8,64,128]{2,1,0:T(8,128)(2,1)S(1)} %fusion.133) | copy-start | bytes 393220
  1309.4 164.9 %copy-start.28 = (bf16[384,1024]{1,0:T(8,128)(2,1)S(1)}, bf16[384,1024]{1,0:T(8,128)(2,1)}, u32[]{:S(2)}) copy-start(bf16[384,1024]{1,0:T(8,128)(2,1)} %param.29) | copy-start | bytes 2359300
  1309.4 164.9 %copy-start.71 = (f32[2,1,512]{2,1,0:T(1,128)S(1)}, f32[2,1,512]{2,1,0:T(1,128)}, u32[]{:S(2)}) copy-start(f32[2,1,512]{2,1,0:T(1,128)} %copy-done.70) | copy-start | bytes 12292
  1309.4 164.9 %copy-start.73 = (f32[384]{0:T(512)S(1)}, f32[384]{0:T(512)}, u32[]{:S(2)}) copy-start(f32[384]{0:T(512)} %copy-done.72) | copy-start | bytes 4612
  1480.1 106.6 %reduce-scatter.14.cloned.1.call-start = ((), (), s32[]{:S(2)}) async-start(), calls=%async_computation.23 | async-start | bytes 1572864 | tf_op jit(solution)/shard_map/reduce_scatter | solution.py:559
  1490.1 131.1 %reduce-scatter.12.cloned.1.call-start = ((), (), s32[]{:S(2)}) async-start(), calls=%async_computation.21 | async-start | bytes 3145728 | tf_op jit(solution)/shard_map/reduce_scatter | solution.py:556
  1504.4 224.5 %all-reduce.7.cloned.1.call-start = ((), (), s32[]{:S(2)}) async-start(), calls=%async_computation.28 | async-start | bytes 6291456 | tf_op jit(solution)/shard_map/psum | solution.py:535
  1563.5 57.8 %copy-start.20 = (f32[1,512,1024]{2,1,0:T(8,128)S(1)}, f32[1,512,1024]{2,1,0:T(8,128)}, u32[]{:S(2)}) copy-start(f32[1,512,1024]{2,1,0:T(8,128)} %param.38) | copy-start | bytes 6291460
  1563.5 187.7 %all-gather.33.cloned.1.call-start = ((), (), s32[]{:S(2)}) async-start(), calls=%async_computation.24 | async-start | bytes 1572864 | tf_op jit(solution)/shard_map/all_gather | solution.py:617
  1590.7 36.8 %copy-start.1 = (bf16[384,1024]{1,0:T(8,128)(2,1)S(1)}, bf16[384,1024]{1,0:T(8,128)(2,1)}, u32[]{:S(2)}) copy-start(bf16[384,1024]{1,0:T(8,128)(2,1)} %copy-done) | copy-start | bytes 2359300
  1590.8 36.8 %copy-start.50 = (bf16[384,16]{1,0:T(8,128)(2,1)S(1)}, bf16[384,16]{1,0:T(8,128)(2,1)}, u32[]{:S(2)}) copy-start(bf16[384,16]{1,0:T(8,128)(2,1)} %copy-done.49) | copy-start | bytes 36868
  1590.8 195.5 %all-gather.31.cloned.1.call-start = ((), (), s32[]{:S(2)}) async-start(), calls=%async_computation.22 | async-start | bytes 3145728 | tf_op jit(solution)/shard_map/all_gather | solution.py:614
  1627.4 173.3 %reduce-scatter.20.cloned.1.call-start = ((), (), s32[]{:S(2)}) async-start(), calls=%async_computation.27 | async-start | bytes 49152 | tf_op jit(solution)/shard_map/reduce_scatter | solution.py:553
  1628.4 255.3 %all-gather.29.cloned.1.call-start = ((), (), s32[]{:S(2)}) async-start(), calls=%async_computation.20 | async-start | bytes 3145728 | tf_op jit(solution)/shard_map/all_gather | solution.py:605
  1728.9 7.0 copy-start.35
  1735.8 156.6 %all-gather.27.cloned.1.call-start = ((), (), s32[]{:S(2)}) async-start(), calls=%async_computation.19 | async-start | bytes 6291456 | tf_op jit(solution)/shard_map/all_gather | solution.py:602
  1735.9 9.2 copy-start.81
  1746.4 44.1 %copy-start.29 = (bf16[384,1024]{1,0:T(8,128)(2,1)S(1)}, bf16[384,1024]{1,0:T(8,128)(2,1)}, u32[]{:S(2)}) copy-start(bf16[384,1024]{1,0:T(8,128)(2,1)} %param.29) | copy-start | bytes 2359300
  1746.4 44.1 %copy-start.53 = (bf16[384,16,64]{0,2,1:T(8,128)(2,1)S(1)}, bf16[384,16,64]{0,2,1:T(8,128)(2,1)}, u32[]{:S(2)}) copy-start(bf16[384,16,64]{0,2,1:T(8,128)(2,1)} %pad_maximum_fusion.9) | copy-start | bytes 2359300
  1790.5 77.1 %copy-start.76 = (f32[512]{0:T(512)S(1)}, f32[512]{0:T(512)}, u32[]{:S(2)}) copy-start(f32[512]{0:T(512)} %param.33) | copy-start | bytes 6148
  1790.5 90.2 %copy-start.16 = (f32[384,1024]{1,0:T(8,128)S(1)}, f32[384,1024]{1,0:T(8,128)}, u32[]{:S(2)}) copy-start(f32[384,1024]{1,0:T(8,128)} %copy-done.14) | copy-start | bytes 4718596
  (65 other events, 215.3 us)
Sparse Core Ops, SparseCore 0:
  11.3 59.4 all-gather.14
  82.5 50.7 all-gather.16
  136.0 51.7 all-gather.18
  189.7 31.2 all-gather.20
  304.6 33.9 all-gather.22
  340.5 21.2 all-gather.24
  1294.0 102.0 reduce-scatter.7
  1401.1 71.5 reduce-scatter.9
  1475.5 30.8 reduce-scatter.17
  1509.1 54.2 reduce-scatter.15
  1566.3 20.3 reduce-scatter.13
  1589.4 31.8 reduce-scatter.11
  1625.0 103.8 all-reduce.6
  1730.9 20.2 all-gather.32
  1753.1 33.1 all-gather.30
  1788.9 9.8 reduce-scatter.19
  1800.1 33.1 all-gather.28
  1835.2 57.1 all-gather.26
where the time goes:
time: 1920 us; the launch traced here: 1910 us
  waiting for transfers between devices  936 us (49%)
  blocking collectives  298 us (16%)
  matrix products  270 us (14%)
  local copies, waits for them, and re-layouts  205 us (11%)
  other arithmetic  127 us (7%)
  starting transfers between devices  46.8 us (2%)
    all_to_all x1, blocking collectives, per_device(): lax.all_to_all(grad_slots.reshape(members, local_experts * capacity, mode...  206 us
    all_to_all x1, waiting for transfers between devices, per_device(): lax.all_to_all(expert_out.reshape(members, local_experts * capacity, mode...  136 us
    all_to_all x1, waiting for transfers between devices, per_device(): lax.all_to_all(grad_arrived.reshape(members, local_experts * capacity, mo...  133 us
    all_to_all x1, waiting for transfers between devices, per_device(): lax.all_to_all(send_rows.reshape(members, local_experts * capacity, model...  104 us
    psum x1, waiting for transfers between devices, per_device(): lax.psum(grad_qkv_weight.astype(jnp.bfloat16), 'expert').astype(jnp.float32)  100 us
    reduce_scatter x1, waiting for transfers between devices, per_device(): lax.psum_scatter(key_terms.astype(jnp.bfloat16), 'expert', scatter_dimens...  86.7 us
    reduce_scatter x1, waiting for transfers between devices, per_device(): lax.psum_scatter(value_terms.astype(jnp.bfloat16), 'expert', scatter_dime...  74.3 us
    psum x1, blocking collectives, per_device(): lax.psum(grad_gain_attn.astype(jnp.bfloat16), 'expert').astype(jnp.float32)  60 us
  transfers between devices with their start and end apart: 21, of which 17 were waited for; matrix products, arithmetic and copies ran while one was open for 13% of the time, Pallas kernels for 0%

commit v1 on v0

v1 whole, which is shorter than its diff:
```python
import functools
import math

import jax
import jax.numpy as jnp
from jax import lax
from jax.experimental import pallas as pl
from jax.experimental.pallas import tpu as pltpu
from jax.sharding import Mesh
from jax.sharding import PartitionSpec as P

HEADS = 16
KV_HEADS = 8
HEAD_DIM = 64
EXP_FF = 512
TOPK = 8
NPROMPT = 2
PROMPT_DEV = 128
CLEN = 128
REPEAT = HEADS // KV_HEADS
PROMPT_ROWS = NPROMPT * PROMPT_DEV

norm_eps = 1e-05
masked_score = -1e30
decay_rate = 0.1
adam_eps = 1e-08
bias_first = 0.999973438601112
bias_second = 0.99407947078
score_scale = HEAD_DIM ** (-0.5)

bf16 = jnp.bfloat16
f32 = jnp.float32


def dot(left, right):
    return jnp.dot(left, right, preferred_element_type=f32)


def dot_tn(left, right):
    return lax.dot_general(left, right, (((0,), (0,)), ((), ())), preferred_element_type=f32)


def dot_nt(left, right):
    return lax.dot_general(left, right, (((1,), (1,)), ((), ())), preferred_element_type=f32)


def norm_back(values, scale_rows, gain_row, grad_rows):
    normed = values * scale_rows
    grad_normed = grad_rows * gain_row
    grad_values = scale_rows * (
        grad_normed - normed * jnp.mean(grad_normed * normed, axis=-1, keepdims=True)
    )
    return (grad_values, jnp.sum(grad_rows * normed, axis=0))


def adamw(weight, mean_in, square_in, gradient, grad_scale, decay_factor):
    scaled = gradient * grad_scale
    mean_out = 0.9 * mean_in + 0.1 * scaled
    square_out = 0.95 * square_in + 0.05 * scaled * scaled
    spread = square_out * (1.0 / bias_second)
    spread = spread * lax.rsqrt(spread) + adam_eps
    update = mean_out * (1.0 / bias_first) / spread
    return (update + decay_factor * weight, mean_out, square_out)


def split_rows(values):
    head = values[:PROMPT_ROWS].reshape(PROMPT_DEV, NPROMPT, -1).transpose(1, 0, 2)
    return jnp.concatenate([head.reshape(PROMPT_ROWS, -1), values[PROMPT_ROWS:]], axis=0)


def merge_rows(values):
    head = values[:PROMPT_ROWS].reshape(NPROMPT, PROMPT_DEV, -1).transpose(1, 0, 2)
    return jnp.concatenate([head.reshape(PROMPT_ROWS, -1), values[PROMPT_ROWS:]], axis=0)


def swap(values):
    return lax.ppermute(values, "core", [(0, 1), (1, 0)])


class Ring:
    def __init__(self, chips):
        rows = 4 if chips % 4 == 0 else chips
        cols = chips // rows
        cycle = [(0, x) for x in range(cols)]
        for z in range(1, rows):
            line = [(z, x) for x in range(1, cols)]
            cycle += line[::-1] if z % 2 == 1 else line
        if cols > 1:
            cycle += [(z, 0) for z in range(rows - 1, 0, -1)]
        else:
            cycle = [(z, 0) for z in range(rows)]
        self.chips = chips
        self.order = [z * cols + x for z, x in cycle]
        self.forward = [
            (self.order[k], self.order[(k + 1) % chips]) for k in range(chips)
        ]
        self.backward = [(b, a) for a, b in self.forward]
        self.half = chips // 2
        self.by_distance = [r for group in self.groups() for r in group]

    def chips_from(self, me):
        table = [[0] * self.chips for _ in range(self.chips)]
        for k in range(self.chips):
            for column, offset in enumerate(self.by_distance):
                table[self.order[k]][column] = self.order[(k + offset) % self.chips]
        return lax.dynamic_index_in_dim(jnp.asarray(table, jnp.int32), me, 0, False)

    def gather_steps(self, block):
        gather = RingGather(self, block)
        yield {0: block}
        for _ in range(self.half):
            yield gather.step()

    @staticmethod
    def cut(block):
        return block.shape[0] // 32 * 16

    def groups(self):
        return [[0]] + [[-s, s] for s in range(1, self.half)] + [[self.half]]


class RingGather:
    def __init__(self, ring, block):
        self.ring = ring
        self.place = 0
        self.ahead = self.behind = block
        self.blocks = {0: block}

    def ends(self):
        return (self.ahead, self.behind)

    def step(self, *others):
        ring = self.ring
        self.place += 1
        if others:
            self.ahead, self.behind = after(self.ends(), others)
        self.before = self.ends()
        if self.place < ring.half:
            self.ahead = lax.ppermute(self.ahead, "chip", ring.forward)
            self.behind = lax.ppermute(self.behind, "chip", ring.backward)
            arrived = {-self.place: self.ahead, self.place: self.behind}
        else:
            cut = ring.cut(self.ahead)
            first = lax.ppermute(self.ahead[:cut], "chip", ring.forward)
            second = lax.ppermute(self.behind[cut:], "chip", ring.backward)
            arrived = {ring.half: jnp.concatenate([first, second], axis=0)}
        self.blocks.update(arrived)
        return arrived


class RingSum:
    def __init__(self, ring, part):
        cut = ring.cut(part)
        self.ring = ring
        self.place = ring.half
        self.cut = cut
        self.sent = (part[:cut], part[cut:])
        self.send()

    def send(self):
        self.ahead = lax.ppermute(self.sent[0], "chip", self.ring.forward)
        self.behind = lax.ppermute(self.sent[1], "chip", self.ring.backward)

    def arrived(self):
        return (self.ahead, self.behind)

    def add(self, parts, *others):
        ring, cut = self.ring, self.cut
        self.place -= 1
        up, down = parts[self.place], parts[-self.place]
        if others:
            up, down = after((up, down), others)
        self.ahead, self.behind = lax.optimization_barrier((self.ahead, self.behind))
        if self.place == ring.half - 1:
            ahead = jnp.concatenate([self.ahead + up[:cut], up[cut:]], axis=0)
            behind = jnp.concatenate([down[:cut], self.behind + down[cut:]], axis=0)
        else:
            ahead, behind = self.ahead + up, self.behind + down
        self.sent = (ahead, behind)
        self.send()

    def finish(self, part):
        return part.astype(f32) + self.ahead.astype(f32) + self.behind.astype(f32)


def after(values, *others):
    return lax.optimization_barrier((values, others))[0]


def total_stages(values, axes):
    for axis in axes:
        size = lax.axis_size(axis)
        reach = 1
        while reach < size:
            values = values + lax.ppermute(values, axis, [(k, k ^ reach) for k in range(size)])
            reach *= 2
            yield values


def dp_shards(values):
    size = lax.axis_size("dp")
    pieces = [values]
    for shift in range(1, size):
        perm = [(k, (k - shift) % size) for k in range(size)]
        pieces.append(lax.ppermute(values, "dp", perm))
    return pieces


def join_dp(pieces, axis):
    size = len(pieces)
    dp = lax.axis_index("dp")
    if size == 2:
        return jnp.concatenate(
            [
                jnp.where(dp == 0, pieces[0], pieces[1]),
                jnp.where(dp == 0, pieces[1], pieces[0]),
            ],
            axis=axis,
        )
    twice = jnp.concatenate(pieces + pieces, axis=axis)
    shard = pieces[0].shape[axis]
    return lax.dynamic_slice_in_dim(twice, (size - dp) % size * shard, size * shard, axis)


def gather_dp(values, axis):
    return join_dp(dp_shards(values), axis)


def pick_core(first, second):
    return jnp.where(lax.axis_index("core") == 0, first, second)


LOG2E = 1.4426950408889634


def stack_heads(wide):
    wide = wide.astype(f32)
    first, second = wide[:, :128], wide[:, 128:]
    lane = lax.broadcasted_iota(jnp.int32, first.shape, 1)
    low_lanes = lane < HEAD_DIM
    zero = jnp.zeros_like(first)
    return jnp.concatenate(
        [
            jnp.where(low_lanes, first, zero),
            jnp.where(low_lanes, pltpu.roll(first, HEAD_DIM, 1), zero),
            jnp.where(low_lanes, zero, pltpu.roll(second, HEAD_DIM, 1)),
            jnp.where(low_lanes, zero, second),
        ],
        axis=0,
    )


def unstack_heads(tall):
    rows = tall.shape[0] // 4
    parts = [tall[k * rows : (k + 1) * rows] for k in range(4)]
    lane = lax.broadcasted_iota(jnp.int32, parts[0].shape, 1)
    low_lanes = lane < HEAD_DIM
    return jnp.concatenate(
        [
            jnp.where(low_lanes, parts[0], pltpu.roll(parts[1], HEAD_DIM, 1)),
            jnp.where(low_lanes, pltpu.roll(parts[2], HEAD_DIM, 1), parts[3]),
        ],
        axis=1,
    )


def row_of(column_sum_of):
    return jnp.sum(jnp.transpose(column_sum_of), axis=0, keepdims=True)


def tile_masks(meta_ref, half, is_cont):
    shape = (PROMPT_ROWS, 4 * PROMPT_DEV)
    key = lax.broadcasted_iota(jnp.int32, shape, 0)
    query = lax.broadcasted_iota(jnp.int32, shape, 1) % PROMPT_DEV
    key_member = jnp.where(key < PROMPT_DEV, meta_ref[2], meta_ref[3])
    key_pos = key_member * PROMPT_DEV + key % PROMPT_DEV
    query_pos = meta_ref[2 + half] * PROMPT_DEV + query
    own = (key_pos <= query_pos) | is_cont
    shape = (CLEN, 4 * CLEN)
    key = lax.broadcasted_iota(jnp.int32, shape, 0)
    query = lax.broadcasted_iota(jnp.int32, shape, 1) % CLEN
    self_seen = (key <= query) & is_cont
    return own, self_seen


META = 8


def block_bias(meta_ref, is_cont, first_block, blocks):
    chips = [meta_ref[META + first_block + k] for k in range(blocks)]
    return [jnp.where(is_cont | (c <= meta_ref[6]), 0.0, masked_score) for c in chips]


def attend_kernel(first_block, blocks, first, last, meta_ref, q_ref, *refs):
    kv_refs, refs = refs[:blocks], refs[blocks:]
    if first:
        self_ref, refs = refs[0], refs[1:]
    else:
        acc_in, stat_in = refs[:2]
        refs = refs[2:]
    if last:
        out_ref, low_ref, lse_ref, scores = refs
    else:
        acc_out, stat_out, scores = refs
    tile = pl.program_id(0)
    half = tile // 3
    part = tile % 3
    is_cont = part == NPROMPT
    prompt = jnp.where(is_cont, meta_ref[half], part)
    rows = pl.ds(pl.multiple_of(prompt * PROMPT_ROWS, PROMPT_ROWS), PROMPT_ROWS)
    if first:
        own, self_seen = tile_masks(meta_ref, half, is_cont)
    bias = block_bias(meta_ref, is_cont, first_block, blocks)
    scale = score_scale * LOG2E
    k_width = KV_HEADS // 2 * HEAD_DIM
    for pair in range(2):
        lanes = pl.ds(pair * 128, 128)
        v_lanes = pl.ds(k_width + pair * 128, 128)
        q = stack_heads(q_ref[:, pair * 256 : (pair + 1) * 256]).astype(bf16)
        if first:
            s_self = jnp.where(self_seen, dot_nt(self_ref[0, :, lanes], q), masked_score)
            top = jnp.max(s_self, axis=0, keepdims=True)
        else:
            old = stat_in[0, pair, :1, :]
            top = old
        for k in range(blocks):
            s = dot_nt(kv_refs[k][rows, lanes], q)
            if first:
                s = jnp.where(own, s, masked_score)
            scores[pl.ds(k * PROMPT_ROWS, PROMPT_ROWS), :] = s
            top = jnp.maximum(top, jnp.max(s, axis=0, keepdims=True) + bias[k])
        top2 = top * scale
        if first:
            p = jnp.exp2(s_self * scale - top2)
            total = jnp.sum(p, axis=0, keepdims=True)
            acc = dot(jnp.transpose(self_ref[0, :, v_lanes]), p.astype(bf16))
        else:
            factor = jnp.exp2(old * scale - top2)
            total = stat_in[0, pair, 1:2, :] * factor
            acc = acc_in[0, pair] * factor
        for k in range(blocks):
            s = scores[pl.ds(k * PROMPT_ROWS, PROMPT_ROWS), :]
            p = jnp.exp2(s * scale - (top2 - bias[k]))
            total = total + jnp.sum(p, axis=0, keepdims=True)
            acc = acc + dot(jnp.transpose(kv_refs[k][rows, v_lanes]), p.astype(bf16))
        if last:
            out = unstack_heads(jnp.transpose(acc / total))
            out_ref[:, pair * 256 : (pair + 1) * 256] = out
            low_ref[:, pair * 256 : (pair + 1) * 256] = out.astype(bf16)
            lse = top2 + jnp.log2(total)
            for head in range(4):
                lse_ref[pl.ds(pair * 4 + head, 1), :] = lse[
                    :, head * PROMPT_DEV : (head + 1) * PROMPT_DEV
                ]
        else:
            acc_out[0, pair] = acc
            stat_out[0, pair, :1, :] = top
            stat_out[0, pair, 1:2, :] = total


def attend_back_kernel(first_block, blocks, first, last, meta_ref, q_ref, do_ref, out_ref, lse_ref, *refs):
    kv_refs, refs = refs[:blocks], refs[blocks:]
    if last:
        self_ref, cos_ref, sin_ref = refs[:3]
        refs = refs[3:]
    if not first:
        dq_in, refs = refs[0], refs[1:]
    dkv_refs, refs = refs[:blocks], refs[blocks:]
    if last:
        dq_ref, dself_ref, acc = refs
    else:
        dq_out, acc = refs
    tile = pl.program_id(0)
    half = tile // 3
    part = tile % 3
    is_cont = part == NPROMPT
    prompt = jnp.where(is_cont, meta_ref[half], part)
    start = pl.multiple_of(prompt * PROMPT_ROWS, PROMPT_ROWS)
    rows = pl.ds(start, PROMPT_ROWS)
    if last:
        own, self_seen = tile_masks(meta_ref, half, is_cont)
    bias = block_bias(meta_ref, is_cont, first_block, blocks)
    scale = score_scale * LOG2E
    k_width = KV_HEADS // 2 * HEAD_DIM

    @pl.when(tile == 0)
    def _():
        acc[...] = jnp.zeros_like(acc)

    for pair in range(2):
        lanes = pl.ds(pair * 128, 128)
        v_lanes = pl.ds(k_width + pair * 128, 128)
        cut = slice(pair * 256, (pair + 1) * 256)
        q = stack_heads(q_ref[:, cut]).astype(bf16)
        do_wide = stack_heads(do_ref[:, cut])
        delta = row_of(do_wide * stack_heads(out_ref[:, cut]))
        do = do_wide.astype(bf16)
        lse = jnp.concatenate(
            [lse_ref[pl.ds(pair * 4 + head, 1), :] for head in range(4)], axis=1
        )
        dq = jnp.zeros((128, 4 * PROMPT_DEV), f32) if first else dq_in[0, pair]
        for k in range(blocks):
            key, value = kv_refs[k][rows, lanes], kv_refs[k][rows, v_lanes]
            s = dot_nt(key, q)
            if last:
                s = jnp.where(own, s, masked_score)
            p = jnp.exp2(s * scale - (lse - bias[k]))
            ds = (p * (dot_nt(value, do) - delta)).astype(bf16)
            dq = dq + dot(jnp.transpose(key), ds)
            acc[k, rows, lanes] += dot(ds, q)
            acc[k, rows, v_lanes] += dot(p.astype(bf16), do)
        if last:
            key, value = self_ref[0, :, lanes], self_ref[0, :, v_lanes]
            s = jnp.where(self_seen, dot_nt(key, q), masked_score)
            p = jnp.exp2(s * scale - lse)
            ds = (p * (dot_nt(value, do) - delta)).astype(bf16)
            dq = dq + dot(jnp.transpose(key), ds)
            dself_ref[0, :, lanes] = dot(ds, q) * score_scale
            dself_ref[0, :, v_lanes] = dot(p.astype(bf16), do)
            wide = unstack_heads(jnp.transpose(dq)) * score_scale
            for group in range(2):
                turned = turn(wide[:, group * 128 : (group + 1) * 128], cos_ref[...], -sin_ref[...])
                lo = pair * 256 + group * 128
                dq_ref[:, lo : lo + 128] = turned.astype(bf16)
        else:
            dq_out[0, pair] = dq

    @pl.when(tile == pl.num_programs(0) - 1)
    def _():
        for k in range(blocks):
            dkv_refs[k][:, :k_width] = (acc[k, :, :k_width] * score_scale).astype(bf16)
            dkv_refs[k][:, k_width:] = acc[k, :, k_width:].astype(bf16)


def turn(values, cosine, sine_signed):
    lane = lax.broadcasted_iota(jnp.int32, values.shape, 1) % HEAD_DIM
    swapped = jnp.where(
        lane < HEAD_DIM // 2,
        pltpu.roll(values, 128 - HEAD_DIM // 2, 1),
        pltpu.roll(values, HEAD_DIM // 2, 1),
    )
    return values * cosine + swapped * sine_signed


VMEM_LIMIT = 40 * 1024 * 1024
SMALL_LIMIT = 24 * 1024 * 1024
WHOLE_LIMIT = 60 * 1024 * 1024


def whole_spec(array):
    return pl.BlockSpec(
        array.shape, lambda *_: (0,) * array.ndim, pipeline_mode=pl.Buffered(1)
    )


def attend(meta, queries, first_block, kv_blocks, state, cont_kv=None, last=False):
    blocks = len(kv_blocks)
    first = state is None
    rows, q_width = queries.shape
    tiles = rows // PROMPT_DEV
    columns = 4 * PROMPT_DEV
    row_spec = pl.BlockSpec((PROMPT_DEV, q_width), lambda t, meta: (t, 0))
    lse_spec = pl.BlockSpec((HEADS // 2, PROMPT_DEV), lambda t, meta: (0, t))
    acc_spec = pl.BlockSpec((1, 2, 128, columns), lambda t, meta: (t, 0, 0, 0))
    stat_spec = pl.BlockSpec((1, 2, 8, columns), lambda t, meta: (t, 0, 0, 0))
    pairs = rows * HEADS // 2 * blocks * PROMPT_ROWS
    in_specs = [row_spec] + [whole_spec(b) for b in kv_blocks]
    operands = [meta, queries, *kv_blocks]
    if first:
        in_specs.append(pl.BlockSpec((1,) + cont_kv.shape[1:], lambda t, meta: (t // 3, 0, 0)))
        operands.append(cont_kv)
    else:
        in_specs += [acc_spec, stat_spec]
        operands += list(state)
    if last:
        out_specs = [row_spec, row_spec, lse_spec]
        out_shape = [
            jax.ShapeDtypeStruct((rows, q_width), f32),
            jax.ShapeDtypeStruct((rows, q_width), bf16),
            jax.ShapeDtypeStruct((HEADS // 2, rows), f32),
        ]
    else:
        out_specs = [acc_spec, stat_spec]
        out_shape = [
            jax.ShapeDtypeStruct((tiles, 2, 128, columns), f32),
            jax.ShapeDtypeStruct((tiles, 2, 8, columns), f32),
        ]
    return pl.pallas_call(
        functools.partial(attend_kernel, first_block, blocks, first, last),
        grid_spec=pltpu.PrefetchScalarGridSpec(
            num_scalar_prefetch=1,
            grid=(tiles,),
            in_specs=in_specs,
            out_specs=out_specs,
            scratch_shapes=[pltpu.VMEM((blocks * PROMPT_ROWS, columns), f32)],
        ),
        out_shape=out_shape,
        compiler_params=pltpu.CompilerParams(vmem_limit_bytes=VMEM_LIMIT),
        cost_estimate=pl.CostEstimate(
            flops=48 * 64 * pairs, bytes_accessed=12 << 20, transcendentals=pairs
        ),
        name="attend",
    )(*operands)


def attend_back(meta, queries, grads, mixed, lse, first_block, kv_blocks, dq, own=None):
    blocks = len(kv_blocks)
    first, last = dq is None, own is not None
    rows, q_width = queries.shape
    tiles = rows // PROMPT_DEV
    columns = 4 * PROMPT_DEV
    row_spec = pl.BlockSpec((PROMPT_DEV, q_width), lambda t, meta: (t, 0))
    lse_spec = pl.BlockSpec((HEADS // 2, PROMPT_DEV), lambda t, meta: (0, t))
    dq_spec = pl.BlockSpec((1, 2, 128, columns), lambda t, meta: (t, 0, 0, 0))
    block = kv_blocks[0]
    pairs = rows * HEADS // 2 * blocks * PROMPT_ROWS
    in_specs = [row_spec, row_spec, row_spec, lse_spec] + [whole_spec(b) for b in kv_blocks]
    operands = [meta, queries, grads, mixed, lse, *kv_blocks]
    out_specs = [whole_spec(b) for b in kv_blocks]
    out_shape = [jax.ShapeDtypeStruct(b.shape, bf16) for b in kv_blocks]
    if last:
        cont_kv, cosine, sine = own
        self_spec = pl.BlockSpec((1,) + cont_kv.shape[1:], lambda t, meta: (t // 3, 0, 0))
        turn_spec = pl.BlockSpec((PROMPT_DEV, 128), lambda t, meta: (t, 0))
        in_specs += [self_spec, turn_spec, turn_spec]
        operands += [cont_kv, cosine, sine]
        out_specs += [row_spec, self_spec]
        out_shape += [
            jax.ShapeDtypeStruct((rows, q_width), bf16),
            jax.ShapeDtypeStruct(cont_kv.shape, f32),
        ]
    else:
        out_specs.append(dq_spec)
        out_shape.append(jax.ShapeDtypeStruct((tiles, 2, 128, columns), f32))
    if not first:
        in_specs.append(dq_spec)
        operands.append(dq)
    return pl.pallas_call(
        functools.partial(attend_back_kernel, first_block, blocks, first, last),
        grid_spec=pltpu.PrefetchScalarGridSpec(
            num_scalar_prefetch=1,
            grid=(tiles,),
            in_specs=in_specs,
            out_specs=out_specs,
            scratch_shapes=[pltpu.VMEM((blocks,) + block.shape, f32)],
        ),
        out_shape=out_shape,
        compiler_params=pltpu.CompilerParams(vmem_limit_bytes=VMEM_LIMIT),
        cost_estimate=pl.CostEstimate(
            flops=110 * 64 * pairs, bytes_accessed=16 << 20, transcendentals=pairs
        ),
        name="attend_back",
    )(*operands)


def core_pieces(columns, core, dp_size):
    width = columns.shape[-1] // (2 * dp_size)
    pieces = []
    for s in range(dp_size):
        lo = 2 * s * width
        pieces.append(
            jnp.where(core == 0, columns[:, lo : lo + width], columns[:, lo + width : lo + 2 * width])
        )
    return pieces


def core_heads(columns, core, dp_size):
    q, k = HEADS * HEAD_DIM, KV_HEADS * HEAD_DIM
    cuts = [columns[:, :q], columns[:, q : q + k], columns[:, q + k :]]
    return jnp.concatenate([p for cut in cuts for p in core_pieces(cut, core, dp_size)], axis=1)


def all_heads(mine, other, core, dp_size):
    first, second = jnp.where(core == 0, mine, other), jnp.where(core == 0, other, mine)
    q, k = HEADS // 2 * HEAD_DIM, KV_HEADS // 2 * HEAD_DIM
    pieces = []
    for lo, size in ((0, q), (q, k), (q + k, k)):
        width = size // dp_size
        for s in range(dp_size):
            cut = slice(lo + s * width, lo + (s + 1) * width)
            pieces += [first[:, cut], second[:, cut]]
    return jnp.concatenate(pieces, axis=1)


def cast_kernel(dp_size, meta_ref, weight_ref, out_ref):
    out_ref[...] = core_heads(weight_ref[...], meta_ref[0], dp_size).astype(bf16)


def cast_core_columns(core, weight, dp_size):
    rows, columns = weight.shape
    tile = rows // 4
    return pl.pallas_call(
        functools.partial(cast_kernel, dp_size),
        grid_spec=pltpu.PrefetchScalarGridSpec(
            num_scalar_prefetch=1,
            grid=(4,),
            in_specs=[pl.BlockSpec((tile, columns), lambda t, meta: (t, 0))],
            out_specs=pl.BlockSpec((tile, columns // 2), lambda t, meta: (t, 0)),
        ),
        out_shape=jax.ShapeDtypeStruct((rows, columns // 2), bf16),
        compiler_params=pltpu.CompilerParams(vmem_limit_bytes=SMALL_LIMIT),
        cost_estimate=pl.CostEstimate(
            flops=rows * columns, bytes_accessed=5 * rows * columns, transcendentals=0
        ),
        name="cast_core_columns",
    )(core[None], weight)


def project_kernel(shards, meta_ref, own_ref, other_ref, *refs):
    weights = refs[:shards]
    cos_ref, sin_ref, q_ref, prompt_ref, cont_ref = refs[shards:]
    half = pl.program_id(0)
    depth = weights[0].shape[0]
    q_width = q_ref.shape[-1]
    k_width = cont_ref.shape[-1] // 2
    cosine, sine = cos_ref[...], sin_ref[...]

    def run(x_ref):
        xs = []
        for k in range(shards):
            start = pl.multiple_of((meta_ref[5] + k) % shards * depth, depth)
            xs.append(x_ref[:, pl.ds(start, depth)])
        for lo in range(0, q_width + 2 * k_width, 128):
            if lo % 256 == 0:
                out = sum(dot(x, w[:, lo : lo + 256]) for x, w in zip(xs, weights))
            piece = out[:, lo % 256 : lo % 256 + 128]
            if lo < q_width + k_width:
                piece = turn(piece, cosine, sine)
            piece = piece.astype(bf16)
            if lo < q_width:
                q_ref[:, lo : lo + 128] = piece
            else:
                at = lo - q_width
                for g in range(NPROMPT):
                    rows = piece[g * PROMPT_DEV : (g + 1) * PROMPT_DEV]
                    prompt_ref[g, 0, :, at : at + 128] = rows
                cont_ref[0, :, at : at + 128] = piece[PROMPT_ROWS:]

    pl.when(half == 0)(lambda: run(own_ref))
    pl.when(half == 1)(lambda: run(other_ref))


def project(meta, own, other, weights, cosine, sine):
    rows, width = own.shape
    columns = weights[0].shape[1]
    kv_width = columns // 2
    turn_spec = pl.BlockSpec((rows, 128), lambda h, meta: (h, 0))
    return pl.pallas_call(
        functools.partial(project_kernel, len(weights)),
        grid_spec=pltpu.PrefetchScalarGridSpec(
            num_scalar_prefetch=1,
            grid=(2,),
            in_specs=[whole_spec(a) for a in (own, other, *weights)] + [turn_spec] * 2,
            out_specs=[
                pl.BlockSpec((rows, columns - kv_width), lambda h, meta: (h, 0)),
                pl.BlockSpec((NPROMPT, 1, PROMPT_DEV, kv_width), lambda h, meta: (0, h, 0, 0)),
                pl.BlockSpec((1, CLEN, kv_width), lambda h, meta: (h, 0, 0)),
            ],
        ),
        out_shape=[
            jax.ShapeDtypeStruct((2 * rows, columns - kv_width), bf16),
            jax.ShapeDtypeStruct((NPROMPT, 2, PROMPT_DEV, kv_width), bf16),
            jax.ShapeDtypeStruct((2, CLEN, kv_width), bf16),
        ],
        compiler_params=pltpu.CompilerParams(vmem_limit_bytes=SMALL_LIMIT),
        cost_estimate=pl.CostEstimate(
            flops=4 * rows * width * columns, bytes_accessed=8 << 20, transcendentals=0
        ),
        name="project",
    )(meta, own, other, *weights, cosine, sine)


def projected_grad_kernel(dq_ref, *refs):
    dkv_refs = refs[:3]
    dself_ref, cos_ref, sin_ref, out_ref = refs[3:]
    q_width = dq_ref.shape[-1]
    k_width = dself_ref.shape[-1] // 2
    out_ref[:, :q_width] = dq_ref[...]
    parts = [sum(ref[g, 0].astype(f32) for ref in dkv_refs) for g in range(NPROMPT)]
    dkv = jnp.concatenate(parts + [dself_ref[0]], axis=0)
    cosine, sine = cos_ref[...], -sin_ref[...]
    for lo in range(0, 2 * k_width, 128):
        piece = dkv[:, lo : lo + 128]
        if lo < k_width:
            piece = turn(piece, cosine, sine)
        out_ref[:, q_width + lo : q_width + lo + 128] = piece.astype(bf16)


def projected_grad(dq, dkv_parts, dself, cosine, sine):
    rows2, q_width = dq.shape
    rows = rows2 // 2
    kv_width = dself.shape[-1]
    dkv_parts = [p.reshape(NPROMPT, 2, PROMPT_DEV, kv_width) for p in dkv_parts]
    turn_spec = pl.BlockSpec((rows, 128), lambda h: (h, 0))
    return pl.pallas_call(
        projected_grad_kernel,
        grid=(2,),
        in_specs=[pl.BlockSpec((rows, q_width), lambda h: (h, 0))]
        + [pl.BlockSpec((NPROMPT, 1, PROMPT_DEV, kv_width), lambda h: (0, h, 0, 0))] * 3
        + [pl.BlockSpec((1, CLEN, kv_width), lambda h: (h, 0, 0)), turn_spec, turn_spec],
        out_specs=pl.BlockSpec((rows, q_width + kv_width), lambda h: (h, 0)),
        out_shape=jax.ShapeDtypeStruct((rows2, q_width + kv_width), bf16),
        compiler_params=pltpu.CompilerParams(vmem_limit_bytes=SMALL_LIMIT),
        cost_estimate=pl.CostEstimate(
            flops=20 * rows2 * kv_width, bytes_accessed=6 << 20, transcendentals=0
        ),
        name="projected_grad",
    )(dq, *dkv_parts, dself, cosine, sine)


def order_kernel(meta_ref, qkv_ref, out_ref, parts_ref):
    top = qkv_ref.shape[1]
    shards = qkv_ref.shape[0]
    rows = top + out_ref.shape[1]
    for s in range(shards):
        parts_ref[0, s * rows : s * rows + top, :] = qkv_ref[s]
        parts_ref[0, s * rows + top : (s + 1) * rows, :] = out_ref[s]


def order_parts(meta, qkv, out, chips, dp_size):
    width = qkv.shape[1]
    qkv = qkv.reshape(dp_size, -1, width)
    out = out.reshape(dp_size, -1, width)
    rows = [a.shape[1] // chips for a in (qkv, out)]
    return pl.pallas_call(
        order_kernel,
        grid_spec=pltpu.PrefetchScalarGridSpec(
            num_scalar_prefetch=1,
            grid=(chips,),
            in_specs=[
                pl.BlockSpec((dp_size, r, width), lambda k, meta: (0, meta[META + k], 0))
                for r in rows
            ],
            out_specs=pl.BlockSpec((1, dp_size * sum(rows), width), lambda k, meta: (k, 0, 0)),
        ),
        out_shape=jax.ShapeDtypeStruct((chips, dp_size * sum(rows), width), bf16),
        compiler_params=pltpu.CompilerParams(vmem_limit_bytes=SMALL_LIMIT),
        cost_estimate=pl.CostEstimate(
            flops=qkv.size, bytes_accessed=6 * qkv.size, transcendentals=0
        ),
        name="order_parts",
    )(meta, qkv, out)


def step_kernel(dp_size, grad_scale, meta_ref, grad_ref, *refs):
    qkv, out, step_ref = refs[:3], refs[3:6], refs[6]
    top = qkv[0].shape[0]
    grad = grad_ref[...].astype(f32)
    args = [core_heads(ref[...], meta_ref[4], dp_size) for ref in qkv]
    step_ref[:top, :] = adamw(*args, grad[:top], grad_scale, decay_rate)[0].astype(bf16)
    args = [ref[...] for ref in out]
    step_ref[top:, :] = adamw(*args, grad[top:], grad_scale, decay_rate)[0].astype(bf16)


def shard_step(meta, grad, qkv, out, chips, dp_size, grad_scale):
    qkv_rows, out_rows = qkv[0].shape[0] // chips, out[0].shape[0] // (2 * chips)
    width = grad.shape[1]
    return pl.pallas_call(
        functools.partial(step_kernel, dp_size, grad_scale),
        grid_spec=pltpu.PrefetchScalarGridSpec(
            num_scalar_prefetch=1,
            grid=(1,),
            in_specs=[whole_spec(grad)]
            + [pl.BlockSpec((qkv_rows, 2 * width), lambda t, meta: (meta[6], 0))] * 3
            + [pl.BlockSpec((out_rows, width), lambda t, meta: (meta[4] * chips + meta[6], 0))] * 3,
            out_specs=whole_spec(grad),
        ),
        out_shape=jax.ShapeDtypeStruct(grad.shape, bf16),
        compiler_params=pltpu.CompilerParams(vmem_limit_bytes=WHOLE_LIMIT),
        cost_estimate=pl.CostEstimate(
            flops=20 * grad.size, bytes_accessed=16 * grad.size, transcendentals=grad.size
        ),
        name="shard_step",
    )(meta, grad, *qkv, *out)


def optimizer_kernel(blocks, dp_size, grad_scale, spill, meta_ref, *refs):
    mine, refs = refs[:blocks], refs[blocks:]
    other, refs = refs[:blocks], refs[blocks:]
    qkv, out = refs[:3], refs[3:6]
    refs = refs[6 + spill :]
    step_qkv, mean_qkv, square_qkv, step_out, mean_out, square_out = refs
    core = meta_ref[4]
    top = qkv[0].shape[0]

    def run(mine_ref, other_ref):
        for shift in range(dp_size):
            a, b = mine_ref[shift], other_ref[shift]
            whole = all_heads(a[:top], b[:top], core, dp_size).astype(f32)
            low = jnp.concatenate(
                [
                    jnp.where(core == 0, a[top:], b[top:])[None],
                    jnp.where(core == 0, b[top:], a[top:])[None],
                ],
                axis=0,
            ).astype(f32)
            if shift == 0:
                whole, mean, square = adamw(*[r[...] for r in qkv], whole, grad_scale, decay_rate)
                whole = whole.astype(bf16).astype(f32)
                mean_qkv[...] = mean
                square_qkv[...] = square
                low, mean, square = adamw(*[r[...] for r in out], low, grad_scale, decay_rate)
                low = low.astype(bf16).astype(f32)
                mean_out[...] = mean
                square_out[...] = square
            at = (meta_ref[5] + shift) % dp_size
            step_qkv[pl.ds(at, 1)] = whole[None]
            step_out[pl.ds(at, 1)] = low[None]

    for k in range(blocks):
        if blocks == 1:
            run(mine[k], other[k])
        else:
            pl.when(pl.program_id(0) == k)(functools.partial(run, mine[k], other[k]))


def optimize(meta, first_block, mine, other, qkv, out, buffers, chips, dp_size, grad_scale):
    blocks = len(mine)
    spill = 0 if buffers is None else 6
    qkv_rows = qkv[0].shape[0] // chips
    out_rows = out[0].shape[0] // (2 * chips)
    width = out[0].shape[1]
    out = [a.reshape(2, a.shape[0] // 2, width) for a in out]

    def at_chip(block, meta):
        return meta[META + first_block + block]

    own_qkv = pl.BlockSpec((qkv_rows, 2 * width), lambda b, meta: (at_chip(b, meta), 0))
    own_out = pl.BlockSpec((2, out_rows, width), lambda b, meta: (0, at_chip(b, meta), 0))
    step_qkv = pl.BlockSpec(
        (dp_size, qkv_rows, 2 * width), lambda b, meta: (0, at_chip(b, meta), 0)
    )
    step_out = pl.BlockSpec(
        (dp_size, 2, out_rows, width), lambda b, meta: (0, 0, at_chip(b, meta), 0)
    )
    shapes = [
        (dp_size,) + qkv[0].shape,
        qkv[0].shape,
        qkv[0].shape,
        (dp_size,) + out[0].shape,
        out[0].shape,
        out[0].shape,
    ]
    specs = [step_qkv, own_qkv, own_qkv, step_out, own_out, own_out]
    first = 1 + 2 * blocks + 6
    return pl.pallas_call(
        functools.partial(optimizer_kernel, blocks, dp_size, grad_scale, spill),
        grid_spec=pltpu.PrefetchScalarGridSpec(
            num_scalar_prefetch=1,
            grid=(blocks,),
            in_specs=[whole_spec(a) for a in (*mine, *other)]
            + [own_qkv] * 3
            + [own_out] * 3
            + [pl.BlockSpec(memory_space=pl.ANY)] * spill,
            out_specs=specs,
        ),
        out_shape=[jax.ShapeDtypeStruct(shape, f32) for shape in shapes],
        input_output_aliases={first + k: k for k in range(spill)},
        compiler_params=pltpu.CompilerParams(vmem_limit_bytes=WHOLE_LIMIT),
        cost_estimate=pl.CostEstimate(
            flops=blocks * qkv_rows * width * 60,
            bytes_accessed=blocks * qkv_rows * width * 90,
            transcendentals=blocks * qkv_rows * width * 3,
        ),
        name="optimize",
    )(meta, *mine, *other, *qkv, *out, *(buffers or ()))


def expert_kernel(count, tok, spill, meta_ref, *refs):
    x_refs, refs = refs[:count], refs[count:]
    cot_refs, refs = refs[:count], refs[count:]
    gate_ups, downs = refs[:2], refs[2:4]
    refs = refs[4 + spill :]
    mix_refs, refs = refs[:count], refs[count:]
    grad_refs, refs = refs[:count], refs[count:]
    x_all, cot_all, act_all, dgu_all = refs
    width = x_all.shape[-1]

    def run(x_ref, cot_ref, mix_ref, grad_ref):
        x = x_ref[:tok, :]
        cot = cot_ref[...]
        x_all[...] = x
        cot_all[...] = cot
        extra = x_ref[tok:, :].astype(f32)
        extra = extra[:, :tok] + extra[:, tok : 2 * tok]
        row = lax.broadcasted_iota(jnp.int32, extra.shape, 0)
        gates = jnp.zeros_like(extra)
        for e in range(2):
            mine = row == meta_ref[2 + e]
            weight = jnp.sum(jnp.where(mine, extra, 0.0), axis=0, keepdims=True)
            weight = jnp.transpose(jnp.broadcast_to(weight, (128, tok)))
            weight = jnp.concatenate([weight, weight], axis=1)
            gate_grad = jnp.zeros((tok, 1), f32)
            for lo in range(0, EXP_FF, 256):
                hi = lo + 256
                gate = dot(x, gate_ups[e][:, lo:hi])
                up = dot(x, gate_ups[e][:, EXP_FF + lo : EXP_FF + hi])
                dact = dot_nt(cot, downs[e][lo:hi, :])
                sig = 0.5 * jnp.tanh(0.5 * gate) + 0.5
                silu = gate * sig
                act = silu * up
                gate_grad = gate_grad + jnp.sum(act * dact, axis=-1, keepdims=True)
                act_all[:, e * EXP_FF + lo : e * EXP_FF + hi] = (act * weight).astype(bf16)
                dact = dact * weight
                dgate = dact * up * (sig + silu * (1.0 - sig))
                at = 2 * e * EXP_FF
                dgu_all[:, at + lo : at + hi] = dgate.astype(bf16)
                dgu_all[:, at + EXP_FF + lo : at + EXP_FF + hi] = (dact * silu).astype(bf16)
            gate_row = jnp.transpose(jnp.broadcast_to(gate_grad, (tok, 128)))[:1, :]
            gates = jnp.where(mine, gate_row, gates)
        acts = [act_all[:, e * EXP_FF : (e + 1) * EXP_FF] for e in range(2)]
        dgus = [dgu_all[:, 2 * e * EXP_FF : 2 * (e + 1) * EXP_FF] for e in range(2)]
        for lo in range(0, width, 256):
            mix = sum(dot(acts[e], downs[e][:, lo : lo + 256]) for e in range(2))
            mix_ref[:, lo : lo + 256] = mix.astype(bf16)
        for lo in range(0, width, 256):
            grad = sum(dot_nt(dgus[e], gate_ups[e][lo : lo + 256, :]) for e in range(2))
            grad_ref[:tok, lo : lo + 256] = grad.astype(bf16)
        high = gates.astype(bf16)
        grad_ref[tok:, :tok] = high
        grad_ref[tok:, tok : 2 * tok] = (gates - high.astype(f32)).astype(bf16)
        grad_ref[tok:, 2 * tok :] = jnp.zeros((extra.shape[0], width - 2 * tok), bf16)

    for b in range(count):
        body = functools.partial(run, x_refs[b], cot_refs[b], mix_refs[b], grad_refs[b])
        if count == 1:
            body()
        else:
            pl.when(pl.program_id(0) == b)(body)


def run_experts(meta, x_blocks, cot_blocks, weights, buffers, place, total):
    count = len(x_blocks)
    packed, width = x_blocks[0].shape
    tok = cot_blocks[0].shape[0]
    rows = count * tok
    spill = 0 if buffers is None else 4
    any_spec = pl.BlockSpec(memory_space=pl.ANY)
    stream_width = [width, width, 2 * EXP_FF, 4 * EXP_FF]
    stream = [pl.BlockSpec((tok, w), lambda g, ids: (place + g, 0)) for w in stream_width]
    out = pl.pallas_call(
        functools.partial(expert_kernel, count, tok, spill),
        grid_spec=pltpu.PrefetchScalarGridSpec(
            num_scalar_prefetch=1,
            grid=(count,),
            in_specs=[
                whole_spec(a) for a in (*x_blocks, *cot_blocks, *weights)
            ]
            + [any_spec] * spill,
            out_specs=[whole_spec(c) for c in cot_blocks]
            + [whole_spec(x) for x in x_blocks]
            + stream,
        ),
        out_shape=[jax.ShapeDtypeStruct(c.shape, bf16) for c in cot_blocks]
        + [jax.ShapeDtypeStruct(x.shape, bf16) for x in x_blocks]
        + [jax.ShapeDtypeStruct((total, w), bf16) for w in stream_width],
        input_output_aliases={1 + 2 * count + 4 + k: 2 * count + k for k in range(spill)},
        compiler_params=pltpu.CompilerParams(vmem_limit_bytes=VMEM_LIMIT),
        cost_estimate=pl.CostEstimate(
            flops=2 * 2 * rows * width * EXP_FF * 6,
            bytes_accessed=rows * width * 20 + 6 * width * width,
            transcendentals=2 * rows * EXP_FF,
        ),
        name="experts",
    )(meta, *x_blocks, *cot_blocks, *weights, *(buffers or ()))
    return out[:count], out[count : 2 * count], out[2 * count :]


def per_device(
    ring,
    tokens,
    cotangent,
    routes,
    cont_group,
    attn_gain,
    qkv_weight,
    out_weight,
    ffn_gain,
    router_weight,
    gate_up_weight,
    down_weight,
    mean_attn_gain,
    mean_qkv_weight,
    mean_out_weight,
    mean_ffn_gain,
    mean_router_weight,
    mean_gate_up_weight,
    mean_down_weight,
    square_attn_gain,
    square_qkv_weight,
    square_out_weight,
    square_ffn_gain,
    square_router_weight,
    square_gate_up_weight,
    square_down_weight,
):
    chips = ring.chips
    dp_size = lax.axis_size("dp")
    dp = lax.axis_index("dp")
    chip = lax.axis_index("chip")
    core = lax.axis_index("core")
    members = 2 * chips
    tok_count, width = tokens.shape
    experts = router_weight.shape[1]
    capacity = 5 * tok_count * TOPK // (4 * experts)
    prompt_len = PROMPT_DEV * members
    core_heads = HEADS // 2
    core_kv = KV_HEADS // 2
    q_width = core_heads * HEAD_DIM
    k_width = core_kv * HEAD_DIM

    member_pair = jnp.stack([2 * chip + core, 2 * chip + 1 - core])
    groups = jnp.concatenate([cont_group, swap(cont_group)])
    own_place = jnp.stack([core, dp, chip, 0])
    meta = jnp.concatenate([groups, member_pair, own_place, ring.chips_from(chip)])

    tokens = split_rows(tokens)
    cotangent = split_rows(cotangent)
    routes = split_rows(routes)
    tok_float = tokens.astype(f32)

    qkv_core = cast_core_columns(core, qkv_weight, dp_size)
    small = jnp.concatenate([attn_gain[None], ffn_gain[None], router_weight.T], axis=0).astype(bf16)
    small = gather_dp(small, 1)
    qkv_shards = dp_shards(qkv_core)
    gain_attn = small[0].astype(f32)
    gain_ffn = small[1].astype(f32)
    proj_router_t = small[2:]

    scale_attn = lax.rsqrt(jnp.mean(tok_float * tok_float, axis=-1, keepdims=True) + norm_eps)
    attn_in = (tok_float * scale_attn * gain_attn).astype(bf16)
    within = jnp.arange(PROMPT_DEV, dtype=jnp.int32)
    prompt_pos = member_pair[:, None] * PROMPT_DEV + within
    cont_pos = jnp.broadcast_to(prompt_len + within, (2, CLEN))
    position = jnp.stack([prompt_pos, prompt_pos, cont_pos], axis=1).reshape(-1)
    half_dim = HEAD_DIM // 2
    frequency = jnp.exp(
        jnp.arange(half_dim, dtype=f32) * (-2.0 * math.log(10000.0) / HEAD_DIM)
    )
    angles = position.astype(f32)[:, None] * frequency[None, :]
    cosine_part, sine_part = jnp.cos(angles), jnp.sin(angles)
    cosine = jnp.concatenate([cosine_part] * 4, axis=1)
    sine_signed = jnp.concatenate([-sine_part, sine_part] * 2, axis=1)
    cot_ring = RingGather(ring, cotangent)
    cot_ring.step()
    attn_in = after(attn_in, cot_ring.ends())
    half_rows = out_weight.shape[0] // 2
    late_gate_up, late_down, late_out = after(
        (gate_up_weight[0], down_weight[0], out_weight), cot_ring.ends()
    )
    out_core = pick_core(late_out[:half_rows], late_out[half_rows:]).astype(bf16)
    own_gate_up = lax.all_gather(late_gate_up.astype(bf16), "dp", axis=0, tiled=True)
    own_down = lax.all_gather(late_down.astype(bf16), "dp", axis=0, tiled=True)
    expert_weights = [own_gate_up, swap(own_gate_up), own_down, swap(own_down)]
    cot_ring.step(cosine, sine_signed)
    attn_other = swap(attn_in)
    attn_in2 = jnp.concatenate([attn_in, attn_other], axis=0)
    qkv_shards = after(qkv_shards, cot_ring.ends())
    while cot_ring.place < ring.half - 1:
        cot_ring.step()
    rows2 = 2 * tok_count
    queries, prompt_kv, cont_kv = project(
        meta, attn_in, attn_other, qkv_shards, cosine, sine_signed
    )
    prompt_kv = prompt_kv.reshape(2 * PROMPT_ROWS, 2 * k_width)
    prompt_kv = after(prompt_kv, cot_ring.ends())
    proj_out = gather_dp(after(out_core, qkv_shards), 0)
    kv_blocks, state = {}, None
    for arrived in ring.gather_steps(prompt_kv):
        kv_blocks.update(arrived)
        if 2 in arrived:
            proj_qkv = join_dp(after(qkv_shards, state), 0)
        if ring.half in arrived:
            state, proj_qkv = after((state, proj_qkv))
        state = attend(
            meta,
            queries,
            ring.by_distance.index(min(arrived)),
            list(arrived.values()),
            state,
            cont_kv if 0 in arrived else None,
            ring.half in arrived,
        )
    mixed, mixed_low, lse = state
    cot_blocks = cot_ring.blocks

    part = dot(mixed_low, proj_out)
    other = swap(part[tok_count:].astype(bf16))
    hidden = tok_float + part[:tok_count] + other.astype(f32)
    scale_ffn = lax.rsqrt(jnp.mean(hidden * hidden, axis=-1, keepdims=True) + norm_eps)
    ffn_in = (hidden * scale_ffn * gain_ffn).astype(bf16)
    logits = dot_nt(proj_router_t, ffn_in)
    expert_ids = jnp.arange(experts, dtype=jnp.int32)
    hot = jnp.any(routes.T[None] == expert_ids[:, None, None], axis=1)
    hot_float = hot.astype(f32)
    shown = jnp.where(hot, logits, masked_score)
    raised = jnp.where(hot, jnp.exp(shown - jnp.max(shown, axis=0, keepdims=True)), 0.0)
    gate_probs = raised / jnp.sum(raised, axis=0, keepdims=True)
    spot = jnp.arange(tok_count, dtype=jnp.int32)
    spot = jnp.where(
        spot < PROMPT_ROWS, (spot % PROMPT_DEV) * NPROMPT + spot // PROMPT_DEV, spot
    )
    earlier = (spot[:, None] < spot[None, :]).astype(bf16)
    placed = dot(hot.astype(bf16), earlier)
    kept = hot & (placed < capacity)
    pair_weight = jnp.where(kept, gate_probs, 0.0)
    weight_high = lax.reduce_precision(pair_weight, 8, 7)
    weight_rows = jnp.concatenate([weight_high, pair_weight - weight_high], axis=1).astype(bf16)
    weight_rows = jnp.pad(weight_rows, ((0, 0), (0, width - 2 * tok_count)))
    packed = jnp.concatenate([ffn_in, weight_rows], axis=0)

    total_rows = chips * tok_count
    mix_parts, grad_parts = {}, {}
    buffers = None
    packed = after(packed, cot_ring.ends())
    ffn_ring = RingGather(ring, packed)
    arrived, place = {0: packed}, 0
    while arrived:
        later = {}
        if ffn_ring.place < ring.half:
            later = ffn_ring.step(*(buffers or ()))
        if ring.half in later:
            cot_ring.step(ffn_ring.before)
        mixes, grads, buffers = run_experts(
            meta,
            list(arrived.values()),
            [cot_blocks[r] for r in arrived],
            expert_weights,
            buffers,
            place,
            total_rows,
        )
        mix_parts.update(zip(arrived, mixes))
        grad_parts.update(zip(arrived, grads))
        place += len(arrived)
        arrived = later

    grad_sum = RingSum(ring, grad_parts[ring.half])
    grad_sum.add(grad_parts)
    x_all, cot_all, act_all, dgu_all = after(buffers, grad_sum.sent)
    other_gate_up = dot_tn(x_all, dgu_all[:, 2 * EXP_FF :]).astype(bf16)
    other_down = dot_tn(act_all[:, EXP_FF:], cot_all).astype(bf16)
    grad_sum.add(grad_parts, other_gate_up, other_down)
    other_gate_up, other_down = after((other_gate_up, other_down), grad_sum.sent)
    other_gate_up, other_down = swap(other_gate_up), swap(other_down)
    while grad_sum.place > 1:
        grad_sum.add(grad_parts, other_gate_up, other_down)
    x_all, cot_all, act_all, dgu_all = after(buffers, grad_sum.sent)
    grad_gate_up = dot_tn(x_all, dgu_all[:, : 2 * EXP_FF]) + other_gate_up.astype(f32)
    grad_gate_up = grad_gate_up.astype(bf16)
    grad_down = dot_tn(act_all[:, :EXP_FF], cot_all) + other_down.astype(f32)
    grad_down = grad_down.astype(bf16)
    grad_packed, grad_gate_up, grad_down = lax.optimization_barrier(
        (grad_sum.finish(grad_parts[0]), grad_gate_up, grad_down)
    )
    mix_sum = RingSum(ring, after(mix_parts[ring.half], grad_sum.arrived()))

    def shards_dp(whole):
        pieces = whole.reshape((dp_size, whole.shape[0] // dp_size) + whole.shape[1:])
        out = [lax.dynamic_index_in_dim(pieces, dp, 0, False)]
        for shift in range(1, dp_size):
            perm = [(k, (k + shift) % dp_size) for k in range(dp_size)]
            part = lax.dynamic_index_in_dim(pieces, (dp + shift) % dp_size, 0, False)
            out.append(lax.ppermute(part, "dp", perm))
        return out

    def sum_of(pieces, *others):
        return sum(piece.astype(f32) for piece in after(pieces, others))


    grad_gate = grad_packed[tok_count:, :tok_count] + grad_packed[tok_count:, tok_count : 2 * tok_count]
    grad_gate = jnp.where(kept, grad_gate, 0.0)
    grad_chosen = gate_probs * (grad_gate - jnp.sum(gate_probs * grad_gate, axis=0, keepdims=True))
    grad_logits = (hot_float * grad_chosen).astype(bf16)
    grad_router_t = dot(grad_logits, ffn_in)
    grad_ffn = grad_packed[:tok_count] + dot_tn(grad_logits, proj_router_t)
    grad_output = cotangent.astype(f32)
    grad_hidden_norm, grad_gain_ffn = norm_back(hidden, scale_ffn, gain_ffn, grad_ffn)
    grad_hidden = grad_output + grad_hidden_norm
    grad_attn = after(grad_hidden.astype(bf16), mix_sum.arrived())
    grad_attn2 = jnp.concatenate([grad_attn, swap(grad_attn)], axis=0)
    grad_mixed = dot_nt(grad_attn2, proj_out).astype(bf16)
    mix_sum.add(mix_parts, grad_mixed)

    grad_scale = (tok_count * dp_size * members) ** (-0.5)

    dq, dkv, dkv_sum = None, (), None
    for turn_no, places in enumerate(ring.groups()[::-1]):
        if turn_no >= 2:
            grad_mixed = after(grad_mixed, dkv_before)
        if 0 in places or (turn_no % 2 == 0 and mix_sum.place > 3):
            grad_mixed = after(grad_mixed, mix_sum.arrived())
            if 0 not in places:
                mix_sum.add(mix_parts, dkv)
        dkv = attend_back(
            meta,
            queries,
            grad_mixed,
            mixed,
            lse,
            ring.by_distance.index(min(places)),
            [kv_blocks[r] for r in places],
            dq,
            (cont_kv, cosine, sine_signed) if 0 in places else None,
        )
        parts = dict(zip(places, dkv))
        if ring.half in places:
            dkv_sum = RingSum(ring, parts[ring.half])
        elif 0 not in places:
            grad_out_weight = dot_tn(after(mixed_low, dkv), grad_attn2)
            if turn_no == 1:
                late_gate_up, late_down = after((grad_gate_up, grad_down), dkv)
                gate_up_shards, down_shards = shards_dp(late_gate_up), shards_dp(late_down)
            dkv_before = dkv_sum.arrived()
            dkv_sum.add(parts)
        if 0 not in places:
            dq = dkv[len(places)]
    grad_projected = projected_grad(
        dkv[1], (parts[0], *dkv_sum.arrived()), dkv[2], cosine, sine_signed
    )
    grad_qkv_weight = dot_tn(attn_in2, grad_projected)
    part = dot_nt(grad_projected, proj_qkv)
    other_part = swap(part[tok_count:].astype(bf16))

    qkv_rows = width // dp_size // chips
    out_rows = HEADS * HEAD_DIM // dp_size // 2 // chips
    dense_parts = order_parts(
        meta, grad_qkv_weight.astype(bf16), grad_out_weight.astype(bf16), chips, dp_size
    )
    parts = {r: dense_parts[k] for k, r in enumerate(ring.by_distance)}
    dense_sum = RingSum(ring, parts[ring.half])
    dense_sum.add(parts)
    gate_up_new = adamw(
        gate_up_weight,
        mean_gate_up_weight,
        square_gate_up_weight,
        sum_of(gate_up_shards, dense_sum.sent)[None],
        grad_scale,
        decay_rate,
    )
    dense_sum.add(parts, gate_up_new, other_part)
    grad_attn_in = part[:tok_count] + after(other_part, dense_sum.sent).astype(f32)
    grad_tok_norm, grad_gain_attn = norm_back(tok_float, scale_attn, gain_attn, grad_attn_in)
    input_grad = grad_hidden + grad_tok_norm
    small_grad = jnp.concatenate(
        [grad_gain_attn[None], grad_gain_ffn[None], grad_router_t], axis=0
    )
    down_new = adamw(
        down_weight,
        mean_down_weight,
        square_down_weight,
        sum_of(down_shards, dense_sum.sent)[None],
        grad_scale,
        decay_rate,
    )
    dense_sum.add(parts, down_new, small_grad)
    while dense_sum.place > 1:
        dense_sum.add(parts)
    for small_grad in total_stages(small_grad, ("core", "dp")):
        pass
    dense = after(dense_sum.finish(parts[0]), small_grad)
    dense = dense.reshape(dp_size, qkv_rows + out_rows, width)
    mix_sum.add(mix_parts, dense)
    shard = lax.dynamic_index_in_dim(dense, dp, 0, False)
    for shift in range(1, dp_size):
        perm = [(k, (k + shift) % dp_size) for k in range(dp_size)]
        sent = lax.dynamic_index_in_dim(dense, (dp + shift) % dp_size, 0, False)
        shard = shard + lax.ppermute(sent.astype(bf16), "dp", perm).astype(f32)
    shard_low = shard.astype(bf16)

    qkv_state = (qkv_weight, mean_qkv_weight, square_qkv_weight)
    out_state = (out_weight, mean_out_weight, square_out_weight)
    step_shard = shard_step(
        meta, shard_low, qkv_state, out_state, chips, dp_size, grad_scale
    )
    carried = jnp.stack([shard_low, *dp_shards(step_shard)[1:]])
    carried = after(carried, mix_sum.arrived())
    while mix_sum.place > 1:
        mix_sum.add(mix_parts, step_shard)
    output = hidden + mix_sum.finish(mix_parts[0])
    carried = carried.reshape(dp_size * (qkv_rows + out_rows), width)
    dense_new = None
    shape = (dp_size, qkv_rows + out_rows, width)
    dense_ring = RingGather(ring, carried)
    arrived, first_place, earlier = dict(dense_ring.blocks), 0, ()
    while arrived:
        later = {}
        if dense_ring.place < ring.half:
            later = dense_ring.step(*earlier)
        earlier = tuple(dense_new or ())
        dense_new = optimize(
            meta,
            first_place,
            [m.reshape(shape) for m in arrived.values()],
            [swap(m).reshape(shape) for m in arrived.values()],
            qkv_state,
            out_state,
            dense_new,
            chips,
            dp_size,
            grad_scale,
        )
        first_place += len(arrived)
        arrived = later
    dense_new = [a.reshape(-1, a.shape[-1]) for a in dense_new]

    small_grad = after(small_grad, dense_ring.blocks[ring.half - 1])
    for small_grad in total_stages(small_grad, ("chip",)):
        pass
    shard_cols = width // dp_size
    small_shard = lax.dynamic_slice_in_dim(small_grad, dp * shard_cols, shard_cols, 1)
    attn_new = adamw(
        attn_gain, mean_attn_gain, square_attn_gain, small_shard[0], grad_scale, 0.0
    )
    ffn_new = adamw(ffn_gain, mean_ffn_gain, square_ffn_gain, small_shard[1], grad_scale, 0.0)
    router_new = adamw(
        router_weight,
        mean_router_weight,
        square_router_weight,
        small_shard[2:].T,
        grad_scale,
        decay_rate,
    )
    small_step = jnp.concatenate(
        [attn_new[0][None], ffn_new[0][None], router_new[0].T], axis=0
    ).astype(bf16)
    small_step = gather_dp(small_step, 1).astype(f32)

    step_gate_up = lax.all_gather(gate_up_new[0].astype(bf16), "dp", axis=1, tiled=True)
    step_down = lax.all_gather(down_new[0].astype(bf16), "dp", axis=1, tiled=True)
    return (
        merge_rows(output.astype(bf16)),
        merge_rows(input_grad),
        small_step[0],
        dense_new[0],
        dense_new[3],
        small_step[1],
        small_step[2:].T,
        step_gate_up.astype(f32),
        step_down.astype(f32),
        attn_new[1],
        dense_new[1],
        dense_new[4],
        ffn_new[1],
        router_new[1],
        gate_up_new[1],
        down_new[1],
        attn_new[2],
        dense_new[2],
        dense_new[5],
        ffn_new[2],
        router_new[2],
        gate_up_new[2],
        down_new[2],
    )


def solution(mesh):
    dp_size, members = mesh.shape["dp"], mesh.shape["expert"]
    chips = members // 2
    fine = Mesh(mesh.devices.reshape(dp_size, chips, 2), ("dp", "chip", "core"))
    ring = Ring(chips)
    member = ("chip", "core")
    token = P(("dp",) + member, None)
    matrices = (P("dp"), P("dp", None), P("dp", None), P("dp"), P("dp", None))
    expert = (P(member, "dp", None), P(member, "dp", None))

    def body(*arrays):
        return per_device(ring, *arrays)

    return jax.shard_map(
        body,
        mesh=fine,
        in_specs=(token, token, token, P(("dp",) + member)) + (matrices + expert) * 3,
        out_specs=(token, token)
        + (P(),) * 5
        + (P(member, None, None),) * 2
        + (matrices + expert) * 2,
        check_vma=False,
    )
```

time: 1920 us -> 598 us (0.31)
  waiting for transfers between devices: 936 us -> 146 us
  blocking collectives: 298 us -> 0 us
  matrix products: 270 us -> 43.6 us
  Pallas kernels: 0 us -> 193 us
  local copies, waits for them, and re-layouts: 205 us -> 38.1 us
  other arithmetic: 127 us -> 66.9 us
  starting transfers between devices: 46.8 us -> 83.5 us
    all_to_all x3 -> x0, waiting for transfers between devices: 373 us -> none  [the longest x1 136 us: per_device(): lax.all_to_all(expert_out.reshape(members, local_experts * capacity, mode...]
    reduce_scatter x7 -> x0, waiting for transfers between devices: 274 us -> none  [the longest x1 86.7 us: per_device(): lax.psum_scatter(key_terms.astype(jnp.bfloat16), 'expert', scatter_dimens...]
    dot_general x79 -> x13, matrix products: 270 us -> 43.6 us  [the longest x7 37.7 us: dot_tn(): lax.dot_general(left, right, (((0,), (0,)), ((), ())), preferred_element_...]
    all_to_all x1 -> x0, blocking collectives: 206 us -> none  [per_device(): lax.all_to_all(grad_slots.reshape(members, local_experts * capacity, mode...]
    pallas_call x0 -> x25, Pallas kernels: none -> 193 us  [the longest x5 60.7 us: attend_back(): pl.pallas_call(functools.partial(attend_back_kernel, first_block, blocks,...]
    all_gather x10 -> x4, waiting for transfers between devices: 187 us -> 0.03 us  [the longest x1 0.02 us: per_device(): lax.all_gather(late_gate_up.astype(bf16), 'dp', axis=0, tiled=True)]
    ppermute x0 -> x94, waiting for transfers between devices: none -> 146 us  [the longest x12 45.4 us: step(): self.ahead = lax.ppermute(self.ahead, 'chip', ring.forward)]
    psum x1 -> x0, waiting for transfers between devices: 100 us -> none  [per_device(): lax.psum(grad_qkv_weight.astype(jnp.bfloat16), 'expert').astype(jnp.float32)]
  transfers between devices with their start and end apart: 21 -> 98, of which waited for: 17 -> 38; matrix products, arithmetic and copies ran while one was open for 13% -> 21% of each run, Pallas kernels for 0% -> 30%
where the time goes in v1:
time: 598 us; the launch traced here: 588 us
  Pallas kernels  193 us (32%)
  waiting for transfers between devices  146 us (24%)
  starting transfers between devices  83.5 us (14%)
  other arithmetic  66.9 us (11%)
  matrix products  43.6 us (7%)
  local copies, waits for them, and re-layouts  38.1 us (6%)
  between operations  16.8 us (3%)
    pallas_call x5, Pallas kernels, attend_back(): pl.pallas_call(functools.partial(attend_back_kernel, first_block, blocks,...  60.7 us
    pallas_call x5, Pallas kernels, run_experts(): pl.pallas_call(functools.partial(expert_kernel, count, tok, spill), grid_...  52.5 us
    ppermute x12, waiting for transfers between devices, step(): self.ahead = lax.ppermute(self.ahead, 'chip', ring.forward)  45.4 us
    pallas_call x5, Pallas kernels, attend(): pl.pallas_call(functools.partial(attend_kernel, first_block, blocks, firs...  40.7 us
    dot_general x7, matrix products, dot_tn(): lax.dot_general(left, right, (((0,), (0,)), ((), ())), preferred_element_...  37.7 us
    ppermute x16, waiting for transfers between devices, send(): self.behind = lax.ppermute(self.sent[1], 'chip', self.ring.backward)  31.5 us
    pallas_call x5, Pallas kernels, optimize(): pl.pallas_call(functools.partial(optimizer_kernel, blocks, dp_size, grad_...  28.3 us
    ppermute x16, starting transfers between devices, send(): self.ahead = lax.ppermute(self.sent[0], 'chip', self.ring.forward)  25.3 us
  transfers between devices with their start and end apart: 98, of which 38 were waited for; matrix products, arithmetic and copies ran while one was open for 21% of the time, Pallas kernels for 30%

profile of v1, /device:TPU:0, one launch (start us, length us, event | category | flops | bytes accessed | tf_op | source)
XLA Modules:
  0.0 587.7 jit_solution(2047239035564586556)
XLA Ops:
  10.4 2.9 collective-permute-start.2
  13.5 2.2 copy-done
  15.9 2.0 collective-permute-start.5
  22.1 2.0 reshape.352
  24.1 1.9 copy.107
  26.2 4.8 collective-permute-done.2.refs_2_
  32.4 3.0 convert_element_type.163
  42.0 2.2 fusion.18.own_ref
  44.2 14.0 %collective-permute-done.6.refs_2_ = bf16[384,1024]{1,0:T(8,128)(2,1)} collective-permute-done((bf16[384,1024]{1,0:T(8,128)(2,1)S(1)}, bf16[384,1024]{1,0:T(8,128)(2,1)}, u32[]{:S(2)}, u32[]{:S(2)}) %collective-permute-start.6) | collective-permute-done | bytes 786464 | tf_op jit(solution)/shard_map/ppermute | solution.py:139
  60.2 2.4 select_convert_fusion
  66.2 2.1 convert_element_type.164
  69.4 4.7 project.1
  81.4 7.2 %attend.5 = (f32[6,2,128,512]{3,2,1,0:T(8,128)S(1)}, f32[6,2,8,512]{3,2,1,0:T(8,128)S(1)}) custom-call(s32[16]{0:T(128)S(1)} %concatenate.102.meta_ref, bf16[768,512]{1,0:T(8,128)(2,1)S(1)} %get-tuple-element.218.q_ref, bf16[512,512]{1,0:T(8,128)(2,1)S(1)} %bitcast.159, bf16[2,128,512]{2,1,0:T(8,128)(2,1)S(1)} %get-tuple-element.221.refs_1_), custom_call_target="tpu_custom_call" | custom-call | flops 4831838208 | bytes 12582912 | tf_op jit(solution)/shard_map/attend/pallas_call | solution.py:488
  90.7 8.8 %attend.6 = (f32[6,2,128,512]{3,2,1,0:T(8,128)S(1)}, f32[6,2,8,512]{3,2,1,0:T(8,128)S(1)}) custom-call(s32[16]{0:T(128)S(1)} %concatenate.102.meta_ref, bf16[768,512]{1,0:T(8,128)(2,1)S(1)} %get-tuple-element.218.q_ref, bf16[512,512]{1,0:T(8,128)(2,1)S(1)} %collective-permute-done.10.refs_0_, bf16[512,512]{1,0:T(8,128)(2,1)S(1)} %collective-permute-done.14.refs_1_, ...), custom_call_target="tpu_custom_call" | custom-call | flops 9663676416 | bytes 12582912 | tf_op jit(solution)/shard_map/attend/pallas_call | solution.py:488
  104.4 8.7 %attend.7 = (f32[6,2,128,512]{3,2,1,0:T(8,128)S(1)}, f32[6,2,8,512]{3,2,1,0:T(8,128)S(1)}) custom-call(s32[16]{0:T(128)S(1)} %concatenate.102.meta_ref, bf16[768,512]{1,0:T(8,128)(2,1)S(1)} %get-tuple-element.218.q_ref, bf16[512,512]{1,0:T(8,128)(2,1)S(1)} %collective-permute-done.11.refs_0_, bf16[512,512]{1,0:T(8,128)(2,1)S(1)} %collective-permute-done.15.refs_1_, ...), custom_call_target="tpu_custom_call" | custom-call | flops 9663676416 | bytes 12582912 | tf_op jit(solution)/shard_map/attend/pallas_call | solution.py:488
  116.9 8.8 %attend.8 = (f32[6,2,128,512]{3,2,1,0:T(8,128)S(1)}, f32[6,2,8,512]{3,2,1,0:T(8,128)S(1)}) custom-call(s32[16]{0:T(128)S(1)} %concatenate.102.meta_ref, bf16[768,512]{1,0:T(8,128)(2,1)S(1)} %get-tuple-element.218.q_ref, bf16[512,512]{1,0:T(8,128)(2,1)S(1)} %collective-permute-done.12.refs_0_, bf16[512,512]{1,0:T(8,128)(2,1)S(1)} %collective-permute-done.16.refs_1_, ...), custom_call_target="tpu_custom_call" | custom-call | flops 9663676416 | bytes 12582912 | tf_op jit(solution)/shard_map/attend/pallas_call | solution.py:488
  125.8 7.3 %attend.9 = (f32[768,512]{1,0:T(8,128)S(1)}, bf16[768,512]{1,0:T(8,128)(2,1)S(1)}, f32[8,768]{1,0:T(8,128)S(1)}) custom-call(s32[16]{0:T(128)S(1)} %concatenate.102.meta_ref, bf16[768,512]{1,0:T(8,128)(2,1)S(1)} %get-tuple-element.218.q_ref, bf16[512,512]{1,0:T(8,128)(2,1)S(1)} %constant_dynamic-update-slice_fusion.refs_0_, ...), custom_call_target="tpu_custom_call" | custom-call | flops 4831838208 | bytes 12582912 | tf_op jit(solution)/shard_map/attend/pallas_call | solution.py:488
  139.1 2.2 multiply_reduce_fusion.2
  144.5 6.0 %experts.5 = (bf16[384,1024]{1,0:T(8,128)(2,1)S(1)}, bf16[400,1024]{1,0:T(8,128)(2,1)S(1)}, bf16[3072,1024]{1,0:T(8,128)(2,1)}, bf16[3072,1024]{1,0:T(8,128)(2,1...) custom-call(s32[16]{0:T(128)S(1)} %concatenate.102.meta_ref, bf16[400,1024]{1,0:T(8,128)(2,1)S(1)} %pad_maximum_fusion.3.refs_0_, ...), custom_call_target="tpu_custom_call" | custom-call | flops 4831838208 | bytes 14155776 | tf_op jit(solution)/shard_map/experts/pallas_call | solution.py:941
  150.4 12.3 %collective-permute-done.22.refs_0_ = bf16[400,1024]{1,0:T(8,128)(2,1)S(1)} collective-permute-done((bf16[400,1024]{1,0:T(8,128)(2,1)S(1)}, bf16[400,1024]{1,0:T(8,128)(2,1)S(1)}, u32[]{:S(2)}, u32[]{:S(2)}) %collective-permute-start.22) | collective-permute-done | bytes 819232 | tf_op jit(solution)/shard_map/ppermute | solution.py:139
  166.3 13.1 %experts.6 = (bf16[384,1024]{1,0:T(8,128)(2,1)S(1)}, bf16[384,1024]{1,0:T(8,128)(2,1)S(1)}, bf16[400,1024]{1,0:T(8,128)(2,1)S(1)}, bf16[400,1024]{1,0:T(8,128)(2...) custom-call(s32[16]{0:T(128)S(1)} %concatenate.102.meta_ref, ...), custom_call_target="tpu_custom_call", output_to_operand_aliasing={{4}: (9, {}), {5}: (10, {}), {6}: (11, {}), {7}: (12, {})} | custom-call | flops 9663676416 | bytes 22020096 | tf_op jit(solution)/shard_map/experts/pallas_call | solution.py:941
  186.8 14.3 %experts.7 = (bf16[384,1024]{1,0:T(8,128)(2,1)S(1)}, bf16[384,1024]{1,0:T(8,128)(2,1)S(1)}, bf16[400,1024]{1,0:T(8,128)(2,1)S(1)}, bf16[400,1024]{1,0:T(8,128)(2...) custom-call(s32[16]{0:T(128)S(1)} %concatenate.102.meta_ref, ...), custom_call_target="tpu_custom_call", output_to_operand_aliasing={{4}: (9, {}), {5}: (10, {}), {6}: (11, {}), {7}: (12, {})} | custom-call | flops 9663676416 | bytes 22020096 | tf_op jit(solution)/shard_map/experts/pallas_call | solution.py:941
  208.4 13.4 %experts.8 = (bf16[384,1024]{1,0:T(8,128)(2,1)S(1)}, bf16[384,1024]{1,0:T(8,128)(2,1)S(1)}, bf16[400,1024]{1,0:T(8,128)(2,1)S(1)}, bf16[400,1024]{1,0:T(8,128)(2...) custom-call(s32[16]{0:T(128)S(1)} %concatenate.102.meta_ref, ...), custom_call_target="tpu_custom_call", output_to_operand_aliasing={{4}: (9, {}), {5}: (10, {}), {6}: (11, {}), {7}: (12, {})} | custom-call | flops 9663676416 | bytes 22020096 | tf_op jit(solution)/shard_map/experts/pallas_call | solution.py:941
  222.2 5.8 experts.9
  230.3 8.9 %collective-permute-done.32 = bf16[192,1024]{1,0:T(8,128)(2,1)S(1)} collective-permute-done((bf16[192,1024]{1,0:T(8,128)(2,1)S(1)}, bf16[192,1024]{1,0:T(8,128)(2,1)S(1)}, u32[]{:S(2)}, u32[]{:S(2)}) %collective-permute-start.32) | collective-permute-done | bytes 393248 | tf_op jit(solution)/shard_map/ppermute | solution.py:161
  241.6 9.0 %fusion.15 = bf16[1024,1024]{1,0:T(8,128)(2,1)S(1)} fusion(bf16[3072,1024]{1,0:T(8,128)(2,1)S(1)} %copy-done.53, bf16[3072,2048]{1,0:T(8,128)(2,1)} %get-tuple-element.299), kind=kOutput, calls=%fused_computation.25 | convolution fusion | flops 6443499520 | bytes 14680064 | tf_op jit(solution)/shard_map/dot_general | solution.py:40
  250.6 7.3 %fusion.29 = bf16[512,1024]{1,0:T(8,128)(2,1)S(1)} fusion(bf16[3072,1024]{1,0:T(8,128)(2,1)} %get-tuple-element.301, bf16[3072,1024]{1,0:T(8,128)(2,1)} %get-tuple-element.300), kind=kOutput, calls=%fused_computation.52 | convolution fusion | flops 3221749760 | bytes 10485760 | tf_op jit(solution)/shard_map/dot_general | solution.py:40
  261.1 18.2 %collective-permute-done.37 = bf16[400,1024]{1,0:T(8,128)(2,1)S(1)} collective-permute-done((bf16[400,1024]{1,0:T(8,128)(2,1)S(1)}, bf16[400,1024]{1,0:T(8,128)(2,1)S(1)}, u32[]{:S(2)}, u32[]{:S(2)}) %collective-permute-start.37) | collective-permute-done | bytes 819232 | tf_op jit(solution)/shard_map/ppermute | solution.py:162
  280.4 2.0 collective-permute-start.40
  282.4 9.7 %add_convert_fusion = bf16[1024,1024]{1,0:T(8,128)(2,1)} fusion(bf16[1024,1024]{1,0:T(8,128)(2,1)S(1)} %collective-permute-done.38, bf16[3072,1024]{1,0:T(8,128)(2,1)} %get-tuple-element.298, bf16[3072,2048]{1,0:T(8,128)(2,1)S(1)} %bitcast.162), kind=kOutput, calls=%fused_computation.4 | convolution fusion | flops 6445596672 | bytes 16777216 | tf_op jit(solution)/shard_map/dot_general | solution.py:40
  292.1 6.3 %add_convert_fusion.1 = bf16[512,1024]{1,0:T(8,128)(2,1)} fusion(bf16[512,1024]{1,0:T(8,128)(2,1)S(1)} %collective-permute-done.39, bf16[3072,1024]{1,0:T(8,128)(2,1)S(1)} %bitcast.165, bf16[3072,1024]{1,0:T(8,128)(2,1)} %get-tuple-element.300), kind=kOutput, calls=%fused_computation.24 | convolution fusion | flops 3222798336 | bytes 11534336 | tf_op jit(solution)/shard_map/dot_general | solution.py:40
  305.3 5.4 collective-permute-done.42
  312.8 2.4 collective-permute-done.44
  318.8 7.7 %attend_back.5 = (bf16[512,512]{1,0:T(8,128)(2,1)S(1)}, f32[6,2,128,512]{3,2,1,0:T(8,128)S(1)}) custom-call(s32[16]{0:T(128)S(1)} %concatenate.102.meta_ref, bf16[768,512]{1,0:T(8,128)(2,1)S(1)} %copy-done.48, bf16[768,512]{1,0:T(8,128)(2,1)S(1)} %convolution_convert_fusion.2.do_ref, f32[768,512]{1,0:T(8,128)S(1)} %copy-done.52, ...), custom_call_target="tpu_custom_call" | custom-call | flops 11072962560 | bytes 16777216 | tf_op jit(solution)/shard_map/attend_back/pallas_call | solution.py:538
  331.3 13.2 %attend_back.6 = (bf16[512,512]{1,0:T(8,128)(2,1)S(1)}, bf16[512,512]{1,0:T(8,128)(2,1)S(1)}, f32[6,2,128,512]{3,2,1,0:T(8,128)S(1)}) custom-call(s32[16]{0:T(128)S(1)} %concatenate.102.meta_ref, bf16[768,512]{1,0:T(8,128)(2,1)S(1)} %copy-done.48, bf16[768,512]{1,0:T(8,128)(2,1)S(1)} %convolution_convert_fusion.2.do_ref, f32[768,512]{1,0:T(8,128)S(1)} %copy-done.52, ...), custom_call_target="tpu_custom_call" | custom-call | flops 22145925120 | bytes 16777216 | tf_op jit(solution)/shard_map/attend_back/pallas_call | solution.py:538
  349.6 13.2 %attend_back.7 = (bf16[512,512]{1,0:T(8,128)(2,1)S(1)}, bf16[512,512]{1,0:T(8,128)(2,1)S(1)}, f32[6,2,128,512]{3,2,1,0:T(8,128)S(1)}) custom-call(s32[16]{0:T(128)S(1)} %concatenate.102.meta_ref, bf16[768,512]{1,0:T(8,128)(2,1)S(1)} %copy-done.48, bf16[768,512]{1,0:T(8,128)(2,1)S(1)} %convolution_convert_fusion.2.do_ref, f32[768,512]{1,0:T(8,128)S(1)} %copy-done.52, ...), custom_call_target="tpu_custom_call" | custom-call | flops 22145925120 | bytes 16777216 | tf_op jit(solution)/shard_map/attend_back/pallas_call | solution.py:538
  366.9 13.2 %attend_back.8 = (bf16[512,512]{1,0:T(8,128)(2,1)S(1)}, bf16[512,512]{1,0:T(8,128)(2,1)S(1)}, f32[6,2,128,512]{3,2,1,0:T(8,128)S(1)}) custom-call(s32[16]{0:T(128)S(1)} %concatenate.102.meta_ref, bf16[768,512]{1,0:T(8,128)(2,1)S(1)} %copy-done.48, bf16[768,512]{1,0:T(8,128)(2,1)S(1)} %convolution_convert_fusion.2.do_ref, f32[768,512]{1,0:T(8,128)S(1)} %copy-done.52, ...), custom_call_target="tpu_custom_call" | custom-call | flops 22145925120 | bytes 16777216 | tf_op jit(solution)/shard_map/attend_back/pallas_call | solution.py:538
  382.4 2.2 collective-permute-start.53
  384.6 13.5 %attend_back.9 = (bf16[512,512]{1,0:T(8,128)(2,1)S(1)}, bf16[768,512]{1,0:T(8,128)(2,1)S(1)}, f32[2,128,512]{2,1,0:T(8,128)S(1)}) custom-call(s32[16]{0:T(128)S(1)} %concatenate.102.meta_ref, bf16[768,512]{1,0:T(8,128)(2,1)S(1)} %copy-done.48, bf16[768,512]{1,0:T(8,128)(2,1)S(1)} %convolution_convert_fusion.2.do_ref, f32[768,512]{1,0:T(8,128)S(1)} %copy-done.52, ...), custom_call_target="tpu_custom_call" | custom-call | flops 11072962560 | bytes 16777216 | tf_op jit(solution)/shard_map/attend_back/pallas_call | solution.py:538
  403.3 3.2 convolution_convert_fusion
  410.9 4.2 collective-permute-done.55
  418.3 4.6 fusion.14
  422.9 3.7 collective-permute-done.58
  428.0 2.1 add.376
  430.2 1.9 add.375
  432.1 3.7 fusion.35
  439.5 2.4 fusion.20
  441.9 5.0 collective-permute-done.62
  453.9 4.7 collective-permute-done.67
  466.6 9.3 %collective-permute-done.70 = bf16[96,1024]{1,0:T(8,128)(2,1)S(1)} collective-permute-done((bf16[96,1024]{1,0:T(8,128)(2,1)S(1)}, bf16[96,1024]{1,0:T(8,128)(2,1)S(1)}, u32[]{:S(2)}, u32[]{:S(2)}) %collective-permute-start.70) | collective-permute-done | bytes 196640 | tf_op jit(solution)/shard_map/ppermute | solution.py:1268
  476.7 3.3 shard_step.1
  480.2 9.8 %collective-permute-done.73 = bf16[96,1024]{1,0:T(8,128)(2,1)S(1)} collective-permute-done((bf16[96,1024]{1,0:T(8,128)(2,1)}, bf16[96,1024]{1,0:T(8,128)(2,1)S(1)}, u32[]{:S(2)}, u32[]{:S(2)}) %collective-permute-start.73) | collective-permute-done | bytes 196640 | tf_op jit(solution)/shard_map/ppermute | solution.py:205
  492.2 8.3 %collective-permute-done.74 = bf16[192,1024]{1,0:T(8,128)(2,1)S(1)} collective-permute-done((bf16[192,1024]{1,0:T(8,128)(2,1)S(1)}, bf16[192,1024]{1,0:T(8,128)(2,1)S(1)}, u32[]{:S(2)}, u32[]{:S(2)}) %collective-permute-start.74) | collective-permute-done | bytes 393248 | tf_op jit(solution)/shard_map/ppermute | solution.py:139
  507.9 4.9 optimize.5
  514.9 2.1 fusion.23
  520.8 2.8 convert_element_type.201
  523.6 4.1 convert_element_type.199
  527.7 6.3 %optimize.6 = (f32[2,512,2048]{2,1,0:T(8,128)}, f32[512,2048]{1,0:T(8,128)}, f32[512,2048]{1,0:T(8,128)}, f32[2,2,256,1024]{3,2,1,0:T(8,128)}, f32[2,256,1024]{2,1,0:T(8,128)}, /*index=5*/f32[2,256,1024]{2,1,0:T(8,128)}) custom-call(s32[16]{0:T(128)} %copy-done.36, ...), custom_call_target="tpu_custom_call", output_to_operand_aliasing={{0}: (11, {}), {1}: (12, {}), {2}: (13, {}), {3}: (14, {}),... | custom-call | flops 7864320 | bytes 11796480 | tf_op jit(solution)/shard_map/optimize/pallas_call | solution.py:846
  546.8 6.3 %optimize.7 = (f32[2,512,2048]{2,1,0:T(8,128)}, f32[512,2048]{1,0:T(8,128)}, f32[512,2048]{1,0:T(8,128)}, f32[2,2,256,1024]{3,2,1,0:T(8,128)}, f32[2,256,1024]{2,1,0:T(8,128)}, /*index=5*/f32[2,256,1024]{2,1,0:T(8,128)}) custom-call(s32[16]{0:T(128)} %copy-done.36, ...), custom_call_target="tpu_custom_call", output_to_operand_aliasing={{0}: (11, {}), {1}: (12, {}), {2}: (13, {}), {3}: (14, {}),... | custom-call | flops 7864320 | bytes 11796480 | tf_op jit(solution)/shard_map/optimize/pallas_call | solution.py:846
  553.1 2.4 collective-permute-start.82
  555.5 5.7 collective-permute-done.82
  563.4 3.7 collective-permute-done.83
  569.3 6.1 %optimize.8 = (f32[2,512,2048]{2,1,0:T(8,128)}, f32[512,2048]{1,0:T(8,128)}, f32[512,2048]{1,0:T(8,128)}, f32[2,2,256,1024]{3,2,1,0:T(8,128)}, f32[2,256,1024]{2,1,0:T(8,128)}, /*index=5*/f32[2,256,1024]{2,1,0:T(8,128)}) custom-call(s32[16]{0:T(128)} %copy-done.36, ...), custom_call_target="tpu_custom_call", output_to_operand_aliasing={{0}: (11, {}), {1}: (12, {}), {2}: (13, {}), {3}: (14, {}),... | custom-call | flops 7864320 | bytes 11796480 | tf_op jit(solution)/shard_map/optimize/pallas_call | solution.py:846
  576.2 4.7 optimize.9
  (601 shorter events, 171.5 us)
Async XLA Ops:
  7.2 129.6 %all-gather.5.cloned.1.call-start = ((), (), s32[]{:S(2)}) async-start(), calls=%async_computation | async-start | bytes 3145728 | tf_op jit(solution)/shard_map/all_gather | solution.py:1052
  10.4 20.6 %collective-permute-start.2 = (bf16[384,1024]{1,0:T(8,128)(2,1)S(1)}, bf16[384,1024]{1,0:T(8,128)(2,1)S(1)}, u32[]{:S(2)}, u32[]{:S(2)}) collective-permute-start(bf16[384,1024]{1,0:T(8,128)(2,1)S(1)} %pad_maximum_fusion.8.refs_1_), channel_id=1, source_target_pairs={{0,2},{2,6},{6,10},{10,14},{14,12},{12,8},{8,4},{4,0},{1,3},{3,7},... | collective-permute-start | bytes 2359304 | tf_op jit(solution)/shard_map/ppermute | solution.py:139
  13.4 19.0 %collective-permute-start.3 = (bf16[384,1024]{1,0:T(8,128)(2,1)S(1)}, bf16[384,1024]{1,0:T(8,128)(2,1)S(1)}, u32[]{:S(2)}, u32[]{:S(2)}) collective-permute-start(bf16[384,1024]{1,0:T(8,128)(2,1)S(1)} %pad_maximum_fusion.8.refs_1_), channel_id=1, source_target_pairs={{2,0},{6,2},{10,6},{14,10},{12,14},{8,12},{4,8},{0,4},{3,1},{7,3},... | collective-permute-start | bytes 2359304 | tf_op jit(solution)/shard_map/ppermute | solution.py:140
  15.9 46.7 %collective-permute-start.5 = (bf16[512,1024]{1,0:T(8,128)(2,1)S(1)}, bf16[512,1024]{1,0:T(8,128)(2,1)}, u32[]{:S(2)}, u32[]{:S(2)}) collective-permute-start(bf16[512,1024]{1,0:T(8,128)(2,1)S(1)} %cast_core_columns.1.refs_0_), channel_id=1, source_target_pairs={{0,16},{16,0},{1,17},{17,1},{2,18},{18,2},{3,19},{19,3},{4,20},{20... | collective-permute-start | bytes 3145736 | tf_op jit(solution)/shard_map/ppermute | solution.py:205
  18.1 23.8 %collective-permute-start.1 = (bf16[18,512]{1,0:T(8,128)(2,1)S(1)}, bf16[18,512]{1,0:T(8,128)(2,1)S(1)}, u32[]{:S(2)}, u32[]{:S(2)}) collective-permute-start(bf16[18,512]{1,0:T(8,128)(2,1)S(1)} %pad_maximum_fusion.25), channel_id=1, source_target_pairs={{0,16},{16,0},{1,17},{17,1},{2,18},{18,2},{3,19},{19,3},{4,20},{20... | collective-permute-start | bytes 55304 | tf_op jit(solution)/shard_map/ppermute | solution.py:205
  35.4 101.9 %all-gather.7.cloned.1.call-start = ((), (), s32[]{:S(2)}) async-start(), calls=%async_computation.1 | async-start | bytes 1572864 | tf_op jit(solution)/shard_map/all_gather | solution.py:1053
  39.8 18.3 %collective-permute-start.6 = (bf16[384,1024]{1,0:T(8,128)(2,1)S(1)}, bf16[384,1024]{1,0:T(8,128)(2,1)}, u32[]{:S(2)}, u32[]{:S(2)}) collective-permute-start(bf16[384,1024]{1,0:T(8,128)(2,1)S(1)} %collective-permute-done.2.refs_2_), channel_id=1, source_target_pairs={{0,2},{2,6},{6,10},{10,14},{14,12},{12,8},{8,4},{4,0},{1,3},{3,7},... | collective-permute-start | bytes 2359304 | tf_op jit(solution)/shard_map/ppermute | solution.py:139
  41.4 18.3 %collective-permute-start.7 = (bf16[384,1024]{1,0:T(8,128)(2,1)S(1)}, bf16[384,1024]{1,0:T(8,128)(2,1)}, u32[]{:S(2)}, u32[]{:S(2)}) collective-permute-start(bf16[384,1024]{1,0:T(8,128)(2,1)S(1)} %copy-done.28), channel_id=1, source_target_pairs={{2,0},{6,2},{10,6},{14,10},{12,14},{8,12},{4,8},{0,4},{3,1},{7,3},... | collective-permute-start | bytes 2359304 | tf_op jit(solution)/shard_map/ppermute | solution.py:140
  44.2 24.2 %collective-permute-start.4 = (bf16[384,1024]{1,0:T(8,128)(2,1)}, bf16[384,1024]{1,0:T(8,128)(2,1)}, u32[]{:S(2)}, u32[]{:S(2)}) collective-permute-start(bf16[384,1024]{1,0:T(8,128)(2,1)} %fusion.18.own_ref), channel_id=1, source_target_pairs={{0,1},{1,0},{2,3},{3,2},{4,5},{5,4},{6,7},{7,6},{8,9},{9,8},{10,11... | collective-permute-start | bytes 2359304 | tf_op jit(solution)/shard_map/ppermute | solution.py:77
  58.1 17.5 %collective-permute-start.8 = (bf16[384,1024]{1,0:T(8,128)(2,1)}, bf16[384,1024]{1,0:T(8,128)(2,1)S(1)}, u32[]{:S(2)}, u32[]{:S(2)}) collective-permute-start(bf16[384,1024]{1,0:T(8,128)(2,1)} %collective-permute-done.6.refs_2_), channel_id=1, source_target_pairs={{0,2},{2,6},{6,10},{10,14},{14,12},{12,8},{8,4},{4,0},{1,3},{3,7},... | collective-permute-start | bytes 2359304 | tf_op jit(solution)/shard_map/ppermute | solution.py:139
  59.7 17.2 %collective-permute-start.9 = (bf16[384,1024]{1,0:T(8,128)(2,1)}, bf16[384,1024]{1,0:T(8,128)(2,1)S(1)}, u32[]{:S(2)}, u32[]{:S(2)}) collective-permute-start(bf16[384,1024]{1,0:T(8,128)(2,1)} %collective-permute-done.7.refs_3_), channel_id=1, source_target_pairs={{2,0},{6,2},{10,6},{14,10},{12,14},{8,12},{4,8},{0,4},{3,1},{7,3},... | collective-permute-start | bytes 2359304 | tf_op jit(solution)/shard_map/ppermute | solution.py:140
  62.6 17.5 %collective-permute-start.18 = (bf16[256,1024]{1,0:T(8,128)(2,1)}, bf16[256,1024]{1,0:T(8,128)(2,1)}, u32[]{:S(2)}, u32[]{:S(2)}) collective-permute-start(bf16[256,1024]{1,0:T(8,128)(2,1)} %select_convert_fusion), channel_id=1, source_target_pairs={{0,16},{16,0},{1,17},{17,1},{2,18},{18,2},{3,19},{19,3},{4,20},{20... | collective-permute-start | bytes 1572872 | tf_op jit(solution)/shard_map/ppermute | solution.py:205
  68.3 452.5 %all-gather.11.cloned.1.call-start = ((), (), s32[]{:S(2)}) async-start(), calls=%async_computation.3 | async-start | bytes 1572864 | tf_op jit(solution)/shard_map/all_gather | solution.py:1330
  88.6 13.7 %collective-permute-start.11 = (bf16[512,512]{1,0:T(8,128)(2,1)S(1)}, bf16[512,512]{1,0:T(8,128)(2,1)S(1)}, u32[]{:S(2)}, u32[]{:S(2)}) collective-permute-start(bf16[512,512]{1,0:T(8,128)(2,1)S(1)} %collective-permute-done.10.refs_0_), channel_id=1, source_target_pairs={{0,2},{2,6},{6,10},{10,14},{14,12},{12,8},{8,4},{4,0},{1,3},{3,7},... | collective-permute-start | bytes 1572872 | tf_op jit(solution)/shard_map/ppermute | solution.py:139
  90.2 13.7 %collective-permute-start.15 = (bf16[512,512]{1,0:T(8,128)(2,1)S(1)}, bf16[512,512]{1,0:T(8,128)(2,1)S(1)}, u32[]{:S(2)}, u32[]{:S(2)}) collective-permute-start(bf16[512,512]{1,0:T(8,128)(2,1)S(1)} %collective-permute-done.14.refs_1_), channel_id=1, source_target_pairs={{2,0},{6,2},{10,6},{14,10},{12,14},{8,12},{4,8},{0,4},{3,1},{7,3},... | collective-permute-start | bytes 1572872 | tf_op jit(solution)/shard_map/ppermute | solution.py:140
  102.4 12.2 %collective-permute-start.12 = (bf16[512,512]{1,0:T(8,128)(2,1)S(1)}, bf16[512,512]{1,0:T(8,128)(2,1)S(1)}, u32[]{:S(2)}, u32[]{:S(2)}) collective-permute-start(bf16[512,512]{1,0:T(8,128)(2,1)S(1)} %collective-permute-done.11.refs_0_), channel_id=1, source_target_pairs={{0,2},{2,6},{6,10},{10,14},{14,12},{12,8},{8,4},{4,0},{1,3},{3,7},... | collective-permute-start | bytes 1572872 | tf_op jit(solution)/shard_map/ppermute | solution.py:139
  103.9 12.2 %collective-permute-start.16 = (bf16[512,512]{1,0:T(8,128)(2,1)S(1)}, bf16[512,512]{1,0:T(8,128)(2,1)S(1)}, u32[]{:S(2)}, u32[]{:S(2)}) collective-permute-start(bf16[512,512]{1,0:T(8,128)(2,1)S(1)} %collective-permute-done.15.refs_1_), channel_id=1, source_target_pairs={{2,0},{6,2},{10,6},{14,10},{12,14},{8,12},{4,8},{0,4},{3,1},{7,3},... | collective-permute-start | bytes 1572872 | tf_op jit(solution)/shard_map/ppermute | solution.py:140
  142.4 20.3 %collective-permute-start.22 = (bf16[400,1024]{1,0:T(8,128)(2,1)S(1)}, bf16[400,1024]{1,0:T(8,128)(2,1)S(1)}, u32[]{:S(2)}, u32[]{:S(2)}) collective-permute-start(bf16[400,1024]{1,0:T(8,128)(2,1)S(1)} %pad_maximum_fusion.3.refs_0_), channel_id=1, source_target_pairs={{0,2},{2,6},{6,10},{10,14},{14,12},{12,8},{8,4},{4,0},{1,3},{3,7},... | collective-permute-start | bytes 2457608 | tf_op jit(solution)/shard_map/ppermute | solution.py:139
  143.9 20.0 %collective-permute-start.23 = (bf16[400,1024]{1,0:T(8,128)(2,1)S(1)}, bf16[400,1024]{1,0:T(8,128)(2,1)S(1)}, u32[]{:S(2)}, u32[]{:S(2)}) collective-permute-start(bf16[400,1024]{1,0:T(8,128)(2,1)S(1)} %pad_maximum_fusion.3.refs_0_), channel_id=1, source_target_pairs={{2,0},{6,2},{10,6},{14,10},{12,14},{8,12},{4,8},{0,4},{3,1},{7,3},... | collective-permute-start | bytes 2457608 | tf_op jit(solution)/shard_map/ppermute | solution.py:140
  163.9 19.1 %collective-permute-start.24 = (bf16[400,1024]{1,0:T(8,128)(2,1)S(1)}, bf16[400,1024]{1,0:T(8,128)(2,1)S(1)}, u32[]{:S(2)}, u32[]{:S(2)}) collective-permute-start(bf16[400,1024]{1,0:T(8,128)(2,1)S(1)} %collective-permute-done.22.refs_0_), channel_id=1, source_target_pairs={{0,2},{2,6},{6,10},{10,14},{14,12},{12,8},{8,4},{4,0},{1,3},{3,7},... | collective-permute-start | bytes 2457608 | tf_op jit(solution)/shard_map/ppermute | solution.py:139
  165.4 19.2 %collective-permute-start.25 = (bf16[400,1024]{1,0:T(8,128)(2,1)S(1)}, bf16[400,1024]{1,0:T(8,128)(2,1)S(1)}, u32[]{:S(2)}, u32[]{:S(2)}) collective-permute-start(bf16[400,1024]{1,0:T(8,128)(2,1)S(1)} %collective-permute-done.23.refs_1_), channel_id=1, source_target_pairs={{2,0},{6,2},{10,6},{14,10},{12,14},{8,12},{4,8},{0,4},{3,1},{7,3},... | collective-permute-start | bytes 2457608 | tf_op jit(solution)/shard_map/ppermute | solution.py:140
  184.6 17.9 %collective-permute-start.26 = (bf16[400,1024]{1,0:T(8,128)(2,1)S(1)}, bf16[400,1024]{1,0:T(8,128)(2,1)S(1)}, u32[]{:S(2)}, u32[]{:S(2)}) collective-permute-start(bf16[400,1024]{1,0:T(8,128)(2,1)S(1)} %collective-permute-done.24.refs_0_), channel_id=1, source_target_pairs={{0,2},{2,6},{6,10},{10,14},{14,12},{12,8},{8,4},{4,0},{1,3},{3,7},... | collective-permute-start | bytes 2457608 | tf_op jit(solution)/shard_map/ppermute | solution.py:139
  186.1 17.8 %collective-permute-start.27 = (bf16[400,1024]{1,0:T(8,128)(2,1)S(1)}, bf16[400,1024]{1,0:T(8,128)(2,1)S(1)}, u32[]{:S(2)}, u32[]{:S(2)}) collective-permute-start(bf16[400,1024]{1,0:T(8,128)(2,1)S(1)} %collective-permute-done.25.refs_1_), channel_id=1, source_target_pairs={{2,0},{6,2},{10,6},{14,10},{12,14},{8,12},{4,8},{0,4},{3,1},{7,3},... | collective-permute-start | bytes 2457608 | tf_op jit(solution)/shard_map/ppermute | solution.py:140
  204.0 17.8 %collective-permute-start.30 = (bf16[192,1024]{1,0:T(8,128)(2,1)S(1)}, bf16[192,1024]{1,0:T(8,128)(2,1)S(1)}, u32[]{:S(2)}, u32[]{:S(2)}) collective-permute-start(bf16[192,1024]{1,0:T(8,128)(2,1)S(1)} %slice.253), channel_id=1, source_target_pairs={{0,2},{2,6},{6,10},{10,14},{14,12},{12,8},{8,4},{4,0},{1,3},{3,7},... | collective-permute-start | bytes 1179656 | tf_op jit(solution)/shard_map/ppermute | solution.py:144
  205.8 16.0 %collective-permute-start.31 = (bf16[192,1024]{1,0:T(8,128)(2,1)S(1)}, bf16[192,1024]{1,0:T(8,128)(2,1)S(1)}, u32[]{:S(2)}, u32[]{:S(2)}) collective-permute-start(bf16[192,1024]{1,0:T(8,128)(2,1)S(1)} %slice.254), channel_id=1, source_target_pairs={{2,0},{6,2},{10,6},{14,10},{12,14},{8,12},{4,8},{0,4},{3,1},{7,3},... | collective-permute-start | bytes 1179656 | tf_op jit(solution)/shard_map/ppermute | solution.py:145
  206.2 16.0 %collective-permute-start.29 = (bf16[208,1024]{1,0:T(8,128)(2,1)S(1)}, bf16[208,1024]{1,0:T(8,128)(2,1)S(1)}, u32[]{:S(2)}, u32[]{:S(2)}) collective-permute-start(bf16[208,1024]{1,0:T(8,128)(2,1)S(1)} %slice.252), channel_id=1, source_target_pairs={{2,0},{6,2},{10,6},{14,10},{12,14},{8,12},{4,8},{0,4},{3,1},{7,3},... | collective-permute-start | bytes 1277960 | tf_op jit(solution)/shard_map/ppermute | solution.py:145
  206.7 15.2 %collective-permute-start.28 = (bf16[192,1024]{1,0:T(8,128)(2,1)S(1)}, bf16[192,1024]{1,0:T(8,128)(2,1)S(1)}, u32[]{:S(2)}, u32[]{:S(2)}) collective-permute-start(bf16[192,1024]{1,0:T(8,128)(2,1)S(1)} %slice.251), channel_id=1, source_target_pairs={{0,2},{2,6},{6,10},{10,14},{14,12},{12,8},{8,4},{4,0},{1,3},{3,7},... | collective-permute-start | bytes 1179656 | tf_op jit(solution)/shard_map/ppermute | solution.py:144
  239.4 18.5 %collective-permute-start.35 = (bf16[400,1024]{1,0:T(8,128)(2,1)S(1)}, bf16[400,1024]{1,0:T(8,128)(2,1)S(1)}, u32[]{:S(2)}, u32[]{:S(2)}) collective-permute-start(bf16[400,1024]{1,0:T(8,128)(2,1)S(1)} %pad_maximum_fusion.6), channel_id=1, source_target_pairs={{2,0},{6,2},{10,6},{14,10},{12,14},{8,12},{4,8},{0,4},{3,1},{7,3},... | collective-permute-start | bytes 2457608 | tf_op jit(solution)/shard_map/ppermute | solution.py:162
  239.8 18.1 %collective-permute-start.34 = (bf16[400,1024]{1,0:T(8,128)(2,1)S(1)}, bf16[400,1024]{1,0:T(8,128)(2,1)S(1)}, u32[]{:S(2)}, u32[]{:S(2)}) collective-permute-start(bf16[400,1024]{1,0:T(8,128)(2,1)S(1)} %pad_maximum_fusion.5), channel_id=1, source_target_pairs={{0,2},{2,6},{6,10},{10,14},{14,12},{12,8},{8,4},{4,0},{1,3},{3,7},... | collective-permute-start | bytes 2457608 | tf_op jit(solution)/shard_map/ppermute | solution.py:161
  258.5 20.9 %collective-permute-start.38 = (bf16[1024,1024]{1,0:T(8,128)(2,1)S(1)}, bf16[1024,1024]{1,0:T(8,128)(2,1)S(1)}, u32[]{:S(2)}, u32[]{:S(2)}) collective-permute-start(bf16[1024,1024]{1,0:T(8,128)(2,1)S(1)} %fusion.15), channel_id=1, source_target_pairs={{0,1},{1,0},{2,3},{3,2},{4,5},{5,4},{6,7},{7,6},{8,9},{9,8},{10,11... | collective-permute-start | bytes 6291464 | tf_op jit(solution)/shard_map/ppermute | solution.py:77
  258.6 20.8 %collective-permute-start.39 = (bf16[512,1024]{1,0:T(8,128)(2,1)S(1)}, bf16[512,1024]{1,0:T(8,128)(2,1)S(1)}, u32[]{:S(2)}, u32[]{:S(2)}) collective-permute-start(bf16[512,1024]{1,0:T(8,128)(2,1)S(1)} %fusion.29), channel_id=1, source_target_pairs={{0,1},{1,0},{2,3},{3,2},{4,5},{5,4},{6,7},{7,6},{8,9},{9,8},{10,11... | collective-permute-start | bytes 3145736 | tf_op jit(solution)/shard_map/ppermute | solution.py:77
  259.1 20.2 %collective-permute-start.37 = (bf16[400,1024]{1,0:T(8,128)(2,1)S(1)}, bf16[400,1024]{1,0:T(8,128)(2,1)S(1)}, u32[]{:S(2)}, u32[]{:S(2)}) collective-permute-start(bf16[400,1024]{1,0:T(8,128)(2,1)S(1)} %add.345), channel_id=1, source_target_pairs={{2,0},{6,2},{10,6},{14,10},{12,14},{8,12},{4,8},{0,4},{3,1},{7,3},... | collective-permute-start | bytes 2457608 | tf_op jit(solution)/shard_map/ppermute | solution.py:162
  259.4 19.9 %collective-permute-start.36 = (bf16[400,1024]{1,0:T(8,128)(2,1)S(1)}, bf16[400,1024]{1,0:T(8,128)(2,1)S(1)}, u32[]{:S(2)}, u32[]{:S(2)}) collective-permute-start(bf16[400,1024]{1,0:T(8,128)(2,1)S(1)} %add.344), channel_id=1, source_target_pairs={{0,2},{2,6},{6,10},{10,14},{14,12},{12,8},{8,4},{4,0},{1,3},{3,7},... | collective-permute-start | bytes 2457608 | tf_op jit(solution)/shard_map/ppermute | solution.py:161
  279.7 19.4 %collective-permute-start.41 = (bf16[400,1024]{1,0:T(8,128)(2,1)S(1)}, bf16[400,1024]{1,0:T(8,128)(2,1)S(1)}, u32[]{:S(2)}, u32[]{:S(2)}) collective-permute-start(bf16[400,1024]{1,0:T(8,128)(2,1)S(1)} %add.347), channel_id=1, source_target_pairs={{2,0},{6,2},{10,6},{14,10},{12,14},{8,12},{4,8},{0,4},{3,1},{7,3},... | collective-permute-start | bytes 2457608 | tf_op jit(solution)/shard_map/ppermute | solution.py:162
  280.4 19.3 %collective-permute-start.40 = (bf16[400,1024]{1,0:T(8,128)(2,1)S(1)}, bf16[400,1024]{1,0:T(8,128)(2,1)S(1)}, u32[]{:S(2)}, u32[]{:S(2)}) collective-permute-start(bf16[400,1024]{1,0:T(8,128)(2,1)S(1)} %add.346), channel_id=1, source_target_pairs={{0,2},{2,6},{6,10},{10,14},{14,12},{12,8},{8,4},{4,0},{1,3},{3,7},... | collective-permute-start | bytes 2457608 | tf_op jit(solution)/shard_map/ppermute | solution.py:161
  326.5 20.7 %collective-permute-start.47 = (bf16[256,512]{1,0:T(8,128)(2,1)S(1)}, bf16[256,512]{1,0:T(8,128)(2,1)S(1)}, u32[]{:S(2)}, u32[]{:S(2)}) collective-permute-start(bf16[256,512]{1,0:T(8,128)(2,1)S(1)} %get-tuple-element.455), channel_id=1, source_target_pairs={{0,2},{2,6},{6,10},{10,14},{14,12},{12,8},{8,4},{4,0},{1,3},{3,7},... | collective-permute-start | bytes 786440 | tf_op jit(solution)/shard_map/ppermute | solution.py:161
  328.3 19.0 %collective-permute-start.48 = (bf16[256,512]{1,0:T(8,128)(2,1)S(1)}, bf16[256,512]{1,0:T(8,128)(2,1)S(1)}, u32[]{:S(2)}, u32[]{:S(2)}) collective-permute-start(bf16[256,512]{1,0:T(8,128)(2,1)S(1)} %get-tuple-element.454), channel_id=1, source_target_pairs={{2,0},{6,2},{10,6},{14,10},{12,14},{8,12},{4,8},{0,4},{3,1},{7,3},... | collective-permute-start | bytes 786440 | tf_op jit(solution)/shard_map/ppermute | solution.py:162
  328.8 53.6 %collective-permute-start.46 = (bf16[384,1024]{1,0:T(8,128)(2,1)S(1)}, bf16[384,1024]{1,0:T(8,128)(2,1)S(1)}, u32[]{:S(2)}, u32[]{:S(2)}) collective-permute-start(bf16[384,1024]{1,0:T(8,128)(2,1)S(1)} %pad_maximum_fusion.11), channel_id=1, source_target_pairs={{2,0},{6,2},{10,6},{14,10},{12,14},{8,12},{4,8},{0,4},{3,1},{7,3},... | collective-permute-start | bytes 2359304 | tf_op jit(solution)/shard_map/ppermute | solution.py:162
  329.6 55.0 %collective-permute-start.45 = (bf16[384,1024]{1,0:T(8,128)(2,1)S(1)}, bf16[384,1024]{1,0:T(8,128)(2,1)S(1)}, u32[]{:S(2)}, u32[]{:S(2)}) collective-permute-start(bf16[384,1024]{1,0:T(8,128)(2,1)S(1)} %pad_maximum_fusion.10), channel_id=1, source_target_pairs={{0,2},{2,6},{6,10},{10,14},{14,12},{12,8},{8,4},{4,0},{1,3},{3,7},... | collective-permute-start | bytes 2359304 | tf_op jit(solution)/shard_map/ppermute | solution.py:161
  345.6 72.7 %collective-permute-start.59 = (bf16[512,1024]{1,0:T(8,128)(2,1)}, bf16[512,1024]{1,0:T(8,128)(2,1)}, u32[]{:S(2)}, u32[]{:S(2)}) collective-permute-start(bf16[512,1024]{1,0:T(8,128)(2,1)} %get-tuple-element.436), channel_id=1, source_target_pairs={{0,16},{16,0},{1,17},{17,1},{2,18},{18,2},{3,19},{19,3},{4,20},{20... | collective-permute-start | bytes 3145736 | tf_op jit(solution)/shard_map/ppermute | solution.py:1164
  347.3 17.1 %collective-permute-start.50 = (bf16[512,512]{1,0:T(8,128)(2,1)S(1)}, bf16[512,512]{1,0:T(8,128)(2,1)S(1)}, u32[]{:S(2)}, u32[]{:S(2)}) collective-permute-start(bf16[512,512]{1,0:T(8,128)(2,1)S(1)} %pad_maximum_fusion.16), channel_id=1, source_target_pairs={{2,0},{6,2},{10,6},{14,10},{12,14},{8,12},{4,8},{0,4},{3,1},{7,3},... | collective-permute-start | bytes 1572872 | tf_op jit(solution)/shard_map/ppermute | solution.py:162
  347.9 16.5 %collective-permute-start.49 = (bf16[512,512]{1,0:T(8,128)(2,1)S(1)}, bf16[512,512]{1,0:T(8,128)(2,1)S(1)}, u32[]{:S(2)}, u32[]{:S(2)}) collective-permute-start(bf16[512,512]{1,0:T(8,128)(2,1)S(1)} %pad_maximum_fusion.15), channel_id=1, source_target_pairs={{0,2},{2,6},{6,10},{10,14},{14,12},{12,8},{8,4},{4,0},{1,3},{3,7},... | collective-permute-start | bytes 1572872 | tf_op jit(solution)/shard_map/ppermute | solution.py:161
  364.6 16.5 %collective-permute-start.52 = (bf16[512,512]{1,0:T(8,128)(2,1)S(1)}, bf16[512,512]{1,0:T(8,128)(2,1)S(1)}, u32[]{:S(2)}, u32[]{:S(2)}) collective-permute-start(bf16[512,512]{1,0:T(8,128)(2,1)S(1)} %add.360), channel_id=1, source_target_pairs={{2,0},{6,2},{10,6},{14,10},{12,14},{8,12},{4,8},{0,4},{3,1},{7,3},... | collective-permute-start | bytes 1572872 | tf_op jit(solution)/shard_map/ppermute | solution.py:162
  365.1 16.6 %collective-permute-start.51 = (bf16[512,512]{1,0:T(8,128)(2,1)S(1)}, bf16[512,512]{1,0:T(8,128)(2,1)S(1)}, u32[]{:S(2)}, u32[]{:S(2)}) collective-permute-start(bf16[512,512]{1,0:T(8,128)(2,1)S(1)} %add.359), channel_id=1, source_target_pairs={{0,2},{2,6},{6,10},{10,14},{14,12},{12,8},{8,4},{4,0},{1,3},{3,7},... | collective-permute-start | bytes 1572872 | tf_op jit(solution)/shard_map/ppermute | solution.py:161
  381.1 50.9 %collective-permute-start.63 = (bf16[256,1024]{1,0:T(8,128)(2,1)}, bf16[256,1024]{1,0:T(8,128)(2,1)}, u32[]{:S(2)}, u32[]{:S(2)}) collective-permute-start(bf16[256,1024]{1,0:T(8,128)(2,1)} %get-tuple-element.440), channel_id=1, source_target_pairs={{0,16},{16,0},{1,17},{17,1},{2,18},{18,2},{3,19},{19,3},{4,20},{20... | collective-permute-start | bytes 1572872 | tf_op jit(solution)/shard_map/ppermute | solution.py:1164
  381.9 16.2 %collective-permute-start.54 = (bf16[512,512]{1,0:T(8,128)(2,1)S(1)}, bf16[512,512]{1,0:T(8,128)(2,1)S(1)}, u32[]{:S(2)}, u32[]{:S(2)}) collective-permute-start(bf16[512,512]{1,0:T(8,128)(2,1)S(1)} %add.362), channel_id=1, source_target_pairs={{2,0},{6,2},{10,6},{14,10},{12,14},{8,12},{4,8},{0,4},{3,1},{7,3},... | collective-permute-start | bytes 1572872 | tf_op jit(solution)/shard_map/ppermute | solution.py:162
  382.4 15.7 %collective-permute-start.53 = (bf16[512,512]{1,0:T(8,128)(2,1)S(1)}, bf16[512,512]{1,0:T(8,128)(2,1)S(1)}, u32[]{:S(2)}, u32[]{:S(2)}) collective-permute-start(bf16[512,512]{1,0:T(8,128)(2,1)S(1)} %add.361), channel_id=1, source_target_pairs={{0,2},{2,6},{6,10},{10,14},{14,12},{12,8},{8,4},{4,0},{1,3},{3,7},... | collective-permute-start | bytes 1572872 | tf_op jit(solution)/shard_map/ppermute | solution.py:161
  403.3 24.0 %collective-permute-start.60 = (bf16[384,1024]{1,0:T(8,128)(2,1)S(1)}, bf16[384,1024]{1,0:T(8,128)(2,1)}, u32[]{:S(2)}, u32[]{:S(2)}) collective-permute-start(bf16[384,1024]{1,0:T(8,128)(2,1)S(1)} %slice.399), channel_id=1, source_target_pairs={{0,1},{1,0},{2,3},{3,2},{4,5},{5,4},{6,7},{7,6},{8,9},{9,8},{10,11... | collective-permute-start | bytes 2359304 | tf_op jit(solution)/shard_map/ppermute | solution.py:77
  435.9 87.7 %all-gather.9.cloned.1.call-start = ((), (), s32[]{:S(2)}) async-start(), calls=%async_computation.2 | async-start | bytes 3145728 | tf_op jit(solution)/shard_map/all_gather | solution.py:1329
  462.8 27.3 %collective-permute-start.69 = (bf16[384,1024]{1,0:T(8,128)(2,1)}, bf16[384,1024]{1,0:T(8,128)(2,1)S(1)}, u32[]{:S(2)}, u32[]{:S(2)}) collective-permute-start(bf16[384,1024]{1,0:T(8,128)(2,1)} %add.391), channel_id=1, source_target_pairs={{2,0},{6,2},{10,6},{14,10},{12,14},{8,12},{4,8},{0,4},{3,1},{7,3},... | collective-permute-start | bytes 2359304 | tf_op jit(solution)/shard_map/ppermute | solution.py:162
  465.7 24.5 %collective-permute-start.68 = (bf16[384,1024]{1,0:T(8,128)(2,1)}, bf16[384,1024]{1,0:T(8,128)(2,1)S(1)}, u32[]{:S(2)}, u32[]{:S(2)}) collective-permute-start(bf16[384,1024]{1,0:T(8,128)(2,1)} %add.390), channel_id=1, source_target_pairs={{0,2},{2,6},{6,10},{10,14},{14,12},{12,8},{8,4},{4,0},{1,3},{3,7},... | collective-permute-start | bytes 2359304 | tf_op jit(solution)/shard_map/ppermute | solution.py:161
  492.2 14.4 %collective-permute-start.78 = (bf16[192,1024]{1,0:T(8,128)(2,1)S(1)}, bf16[192,1024]{1,0:T(8,128)(2,1)S(1)}, u32[]{:S(2)}, u32[]{:S(2)}) collective-permute-start(bf16[192,1024]{1,0:T(8,128)(2,1)S(1)} %bitcast.201), channel_id=1, source_target_pairs={{0,1},{1,0},{2,3},{3,2},{4,5},{5,4},{6,7},{7,6},{8,9},{9,8},{10,11... | collective-permute-start | bytes 1179656 | tf_op jit(solution)/shard_map/ppermute | solution.py:77
  500.5 12.2 %collective-permute-start.75 = (bf16[192,1024]{1,0:T(8,128)(2,1)S(1)}, bf16[192,1024]{1,0:T(8,128)(2,1)}, u32[]{:S(2)}, u32[]{:S(2)}) collective-permute-start(bf16[192,1024]{1,0:T(8,128)(2,1)S(1)} %collective-permute-done.74), channel_id=1, source_target_pairs={{0,2},{2,6},{6,10},{10,14},{14,12},{12,8},{8,4},{4,0},{1,3},{3,7},... | collective-permute-start | bytes 1179656 | tf_op jit(solution)/shard_map/ppermute | solution.py:139
  503.9 34.3 %collective-permute-start.71 = (bf16[384,1024]{1,0:T(8,128)(2,1)}, bf16[384,1024]{1,0:T(8,128)(2,1)}, u32[]{:S(2)}, u32[]{:S(2)}) collective-permute-start(bf16[384,1024]{1,0:T(8,128)(2,1)} %add.393), channel_id=1, source_target_pairs={{0,2},{2,6},{6,10},{10,14},{14,12},{12,8},{8,4},{4,0},{1,3},{3,7},... | collective-permute-start | bytes 2359304 | tf_op jit(solution)/shard_map/ppermute | solution.py:161
  507.3 31.5 %collective-permute-start.72 = (bf16[384,1024]{1,0:T(8,128)(2,1)}, bf16[384,1024]{1,0:T(8,128)(2,1)}, u32[]{:S(2)}, u32[]{:S(2)}) collective-permute-start(bf16[384,1024]{1,0:T(8,128)(2,1)} %add.395), channel_id=1, source_target_pairs={{2,0},{6,2},{10,6},{14,10},{12,14},{8,12},{4,8},{0,4},{3,1},{7,3},... | collective-permute-start | bytes 2359304 | tf_op jit(solution)/shard_map/ppermute | solution.py:162
  512.8 14.9 %collective-permute-start.86 = (bf16[192,1024]{1,0:T(8,128)(2,1)}, bf16[192,1024]{1,0:T(8,128)(2,1)}, u32[]{:S(2)}, u32[]{:S(2)}) collective-permute-start(bf16[192,1024]{1,0:T(8,128)(2,1)} %collective-permute-done.76), channel_id=1, source_target_pairs={{0,1},{1,0},{2,3},{3,2},{4,5},{5,4},{6,7},{7,6},{8,9},{9,8},{10,11... | collective-permute-start | bytes 1179656 | tf_op jit(solution)/shard_map/ppermute | solution.py:77
  512.8 22.9 %collective-permute-start.79 = (bf16[192,1024]{1,0:T(8,128)(2,1)}, bf16[192,1024]{1,0:T(8,128)(2,1)}, u32[]{:S(2)}, u32[]{:S(2)}) collective-permute-start(bf16[192,1024]{1,0:T(8,128)(2,1)} %collective-permute-done.77), channel_id=1, source_target_pairs={{2,0},{6,2},{10,6},{14,10},{12,14},{8,12},{4,8},{0,4},{3,1},{7,3},... | collective-permute-start | bytes 1179656 | tf_op jit(solution)/shard_map/ppermute | solution.py:140
  514.4 21.4 %collective-permute-start.84 = (bf16[192,1024]{1,0:T(8,128)(2,1)}, bf16[192,1024]{1,0:T(8,128)(2,1)}, u32[]{:S(2)}, u32[]{:S(2)}) collective-permute-start(bf16[192,1024]{1,0:T(8,128)(2,1)} %collective-permute-done.75), channel_id=1, source_target_pairs={{0,2},{2,6},{6,10},{10,14},{14,12},{12,8},{8,4},{4,0},{1,3},{3,7},... | collective-permute-start | bytes 1179656 | tf_op jit(solution)/shard_map/ppermute | solution.py:139
  527.7 18.2 %collective-permute-start.92 = (bf16[192,1024]{1,0:T(8,128)(2,1)}, bf16[192,1024]{1,0:T(8,128)(2,1)S(1)}, u32[]{:S(2)}, u32[]{:S(2)}) collective-permute-start(bf16[192,1024]{1,0:T(8,128)(2,1)} %collective-permute-done.75), channel_id=1, source_target_pairs={{0,1},{1,0},{2,3},{3,2},{4,5},{5,4},{6,7},{7,6},{8,9},{9,8},{10,11... | collective-permute-start | bytes 1179656 | tf_op jit(solution)/shard_map/ppermute | solution.py:77
  538.2 17.3 %collective-permute-start.87 = (bf16[96,1024]{1,0:T(8,128)(2,1)S(1)}, bf16[96,1024]{1,0:T(8,128)(2,1)S(1)}, u32[]{:S(2)}, u32[]{:S(2)}) collective-permute-start(bf16[96,1024]{1,0:T(8,128)(2,1)S(1)} %slice.307), channel_id=1, source_target_pairs={{0,2},{2,6},{6,10},{10,14},{14,12},{12,8},{8,4},{4,0},{1,3},{3,7},... | collective-permute-start | bytes 589832 | tf_op jit(solution)/shard_map/ppermute | solution.py:144
  545.0 18.3 %collective-permute-start.88 = (bf16[96,1024]{1,0:T(8,128)(2,1)S(1)}, bf16[96,1024]{1,0:T(8,128)(2,1)S(1)}, u32[]{:S(2)}, u32[]{:S(2)}) collective-permute-start(bf16[96,1024]{1,0:T(8,128)(2,1)S(1)} %slice.308), channel_id=1, source_target_pairs={{2,0},{6,2},{10,6},{14,10},{12,14},{8,12},{4,8},{0,4},{3,1},{7,3},... | collective-permute-start | bytes 589832 | tf_op jit(solution)/shard_map/ppermute | solution.py:145
  545.8 22.5 %collective-permute-start.90 = (bf16[192,1024]{1,0:T(8,128)(2,1)}, bf16[192,1024]{1,0:T(8,128)(2,1)S(1)}, u32[]{:S(2)}, u32[]{:S(2)}) collective-permute-start(bf16[192,1024]{1,0:T(8,128)(2,1)} %collective-permute-done.84), channel_id=1, source_target_pairs={{0,1},{1,0},{2,3},{3,2},{4,5},{5,4},{6,7},{7,6},{8,9},{9,8},{10,11... | collective-permute-start | bytes 1179656 | tf_op jit(solution)/shard_map/ppermute | solution.py:77
  545.9 22.5 %collective-permute-start.91 = (bf16[192,1024]{1,0:T(8,128)(2,1)}, bf16[192,1024]{1,0:T(8,128)(2,1)S(1)}, u32[]{:S(2)}, u32[]{:S(2)}) collective-permute-start(bf16[192,1024]{1,0:T(8,128)(2,1)} %collective-permute-done.79), channel_id=1, source_target_pairs={{0,1},{1,0},{2,3},{3,2},{4,5},{5,4},{6,7},{7,6},{8,9},{9,8},{10,11... | collective-permute-start | bytes 1179656 | tf_op jit(solution)/shard_map/ppermute | solution.py:77
  563.3 12.1 %collective-permute-start.89 = (bf16[192,1024]{1,0:T(8,128)(2,1)S(1)}, bf16[192,1024]{1,0:T(8,128)(2,1)S(1)}, u32[]{:S(2)}, u32[]{:S(2)}) collective-permute-start(bf16[192,1024]{1,0:T(8,128)(2,1)S(1)} %constant_dynamic-update-slice_fusion.4), channel_id=1, source_target_pairs={{0,1},{1,0},{2,3},{3,2},{4,5},{5,4},{6,7},{7,6},{8,9},{9,8},{10,11... | collective-permute-start | bytes 1179656 | tf_op jit(solution)/shard_map/ppermute | solution.py:77
  (172 other events, 2486.8 us)
Sparse Core Ops, SparseCore 0:
  35.5 38.5 all-gather.4
  76.2 21.3 all-gather.6
  436.0 21.9 all-gather.10
  459.4 39.9 all-gather.8

commit v2 on v1

--- a/solution.py
+++ b/solution.py
@@ -781,11 +781,12 @@
     refs = refs[6 + spill :]
     step_qkv, mean_qkv, square_qkv, step_out, mean_out, square_out = refs
     core = meta_ref[4]
-    top = qkv[0].shape[0]
+    top, out_rows = qkv[0].shape[0], out[0].shape[1]
 
     def run(mine_ref, other_ref):
         for shift in range(dp_size):
-            a, b = mine_ref[shift], other_ref[shift]
+            rows = slice(shift * (top + out_rows), (shift + 1) * (top + out_rows))
+            a, b = mine_ref[rows, :], other_ref[rows, :]
             whole = all_heads(a[:top], b[:top], core, dp_size).astype(f32)
             low = jnp.concatenate(
                 [
@@ -1044,6 +1045,7 @@
     cot_ring = RingGather(ring, cotangent)
     cot_ring.step()
     attn_in = after(attn_in, cot_ring.ends())
+    cot_ring.step()
     half_rows = out_weight.shape[0] // 2
     late_gate_up, late_down, late_out = after(
         (gate_up_weight[0], down_weight[0], out_weight), cot_ring.ends()
@@ -1052,7 +1054,6 @@
     own_gate_up = lax.all_gather(late_gate_up.astype(bf16), "dp", axis=0, tiled=True)
     own_down = lax.all_gather(late_down.astype(bf16), "dp", axis=0, tiled=True)
     expert_weights = [own_gate_up, swap(own_gate_up), own_down, swap(own_down)]
-    cot_ring.step(cosine, sine_signed)
     attn_other = swap(attn_in)
     attn_in2 = jnp.concatenate([attn_in, attn_other], axis=0)
     qkv_shards = after(qkv_shards, cot_ring.ends())
@@ -1065,6 +1066,15 @@
     prompt_kv = prompt_kv.reshape(2 * PROMPT_ROWS, 2 * k_width)
     prompt_kv = after(prompt_kv, cot_ring.ends())
     proj_out = gather_dp(after(out_core, qkv_shards), 0)
+    small_state = [
+        jnp.concatenate([a[None], f[None], r.T], axis=0)
+        for a, f, r in (
+            (attn_gain, ffn_gain, router_weight),
+            (mean_attn_gain, mean_ffn_gain, mean_router_weight),
+            (square_attn_gain, square_ffn_gain, square_router_weight),
+        )
+    ]
+    small_state = gather_dp(after(jnp.stack(small_state), prompt_kv), 2)
     kv_blocks, state = {}, None
     for arrived in ring.gather_steps(prompt_kv):
         kv_blocks.update(arrived)
@@ -1190,8 +1200,7 @@
             grad_mixed = after(grad_mixed, dkv_before)
         if 0 in places or (turn_no % 2 == 0 and mix_sum.place > 3):
             grad_mixed = after(grad_mixed, mix_sum.arrived())
-            if 0 not in places:
-                mix_sum.add(mix_parts, dkv)
+            mix_sum.add(mix_parts, dkv)
         dkv = attend_back(
             meta,
             queries,
@@ -1229,7 +1238,7 @@
     )
     parts = {r: dense_parts[k] for k, r in enumerate(ring.by_distance)}
     dense_sum = RingSum(ring, parts[ring.half])
-    dense_sum.add(parts)
+    dense_sum.add(parts, mix_sum.arrived())
     gate_up_new = adamw(
         gate_up_weight,
         mean_gate_up_weight,
@@ -1273,14 +1282,15 @@
     step_shard = shard_step(
         meta, shard_low, qkv_state, out_state, chips, dp_size, grad_scale
     )
-    carried = jnp.stack([shard_low, *dp_shards(step_shard)[1:]])
-    carried = after(carried, mix_sum.arrived())
+    small_rows = -(-small_grad.shape[0] // 16) * 16
+    small_low = jnp.pad(small_grad.astype(bf16), ((0, small_rows - small_grad.shape[0]), (0, 0)))
+    carried = jnp.concatenate([shard_low, *dp_shards(step_shard)[1:], small_low], axis=0)
+    input_grad = merge_rows(input_grad)
+    carried = after(carried, mix_sum.arrived(), input_grad)
     while mix_sum.place > 1:
         mix_sum.add(mix_parts, step_shard)
     output = hidden + mix_sum.finish(mix_parts[0])
-    carried = carried.reshape(dp_size * (qkv_rows + out_rows), width)
     dense_new = None
-    shape = (dp_size, qkv_rows + out_rows, width)
     dense_ring = RingGather(ring, carried)
     arrived, first_place, earlier = dict(dense_ring.blocks), 0, ()
     while arrived:
@@ -1291,8 +1301,8 @@
         dense_new = optimize(
             meta,
             first_place,
-            [m.reshape(shape) for m in arrived.values()],
-            [swap(m).reshape(shape) for m in arrived.values()],
+            list(arrived.values()),
+            [swap(m) for m in arrived.values()],
             qkv_state,
             out_state,
             dense_new,
@@ -1304,33 +1314,24 @@
         arrived = later
     dense_new = [a.reshape(-1, a.shape[-1]) for a in dense_new]
 
-    small_grad = after(small_grad, dense_ring.blocks[ring.half - 1])
-    for small_grad in total_stages(small_grad, ("chip",)):
-        pass
+    base = dp_size * (qkv_rows + out_rows)
+    count = small_grad.shape[0]
+    small_total = sum(
+        dense_ring.blocks[r][base : base + count].astype(f32) for r in ring.by_distance
+    )
+    decays = jnp.full((count, 1), decay_rate, f32).at[:2].set(0.0)
+    small_new = adamw(*small_state, small_total, grad_scale, decays)
     shard_cols = width // dp_size
-    small_shard = lax.dynamic_slice_in_dim(small_grad, dp * shard_cols, shard_cols, 1)
-    attn_new = adamw(
-        attn_gain, mean_attn_gain, square_attn_gain, small_shard[0], grad_scale, 0.0
-    )
-    ffn_new = adamw(ffn_gain, mean_ffn_gain, square_ffn_gain, small_shard[1], grad_scale, 0.0)
-    router_new = adamw(
-        router_weight,
-        mean_router_weight,
-        square_router_weight,
-        small_shard[2:].T,
-        grad_scale,
-        decay_rate,
-    )
-    small_step = jnp.concatenate(
-        [attn_new[0][None], ffn_new[0][None], router_new[0].T], axis=0
-    ).astype(bf16)
-    small_step = gather_dp(small_step, 1).astype(f32)
+    small_step = small_new[0]
+    small_mean, small_square = [
+        lax.dynamic_slice_in_dim(a, dp * shard_cols, shard_cols, 1) for a in small_new[1:]
+    ]
 
     step_gate_up = lax.all_gather(gate_up_new[0].astype(bf16), "dp", axis=1, tiled=True)
     step_down = lax.all_gather(down_new[0].astype(bf16), "dp", axis=1, tiled=True)
     return (
         merge_rows(output.astype(bf16)),
-        merge_rows(input_grad),
+        input_grad,
         small_step[0],
         dense_new[0],
         dense_new[3],
@@ -1338,18 +1339,18 @@
         small_step[2:].T,
         step_gate_up.astype(f32),
         step_down.astype(f32),
-        attn_new[1],
+        small_mean[0],
         dense_new[1],
         dense_new[4],
-        ffn_new[1],
-        router_new[1],
+        small_mean[1],
+        small_mean[2:].T,
         gate_up_new[1],
         down_new[1],
-        attn_new[2],
+        small_square[0],
         dense_new[2],
         dense_new[5],
-        ffn_new[2],
-        router_new[2],
+        small_square[1],
+        small_square[2:].T,
         gate_up_new[2],
         down_new[2],
     )

time: 598 us -> 600 us (level)
  waiting for transfers between devices: 146 us -> 155 us
    ppermute x1, waiting for transfers between devices: 9.33 us -> 1.24 us  [per_device(): shard = shard + lax.ppermute(sent.astype(bf16), 'dp', perm).astype(f32)]
    ppermute x16, waiting for transfers between devices: 31.5 us -> 39.2 us  [send(): self.behind = lax.ppermute(self.sent[1], 'chip', self.ring.backward)]
    ppermute x12, waiting for transfers between devices: 45.4 us -> 52.9 us  [step(): self.ahead = lax.ppermute(self.ahead, 'chip', ring.forward)]
    ppermute x5, waiting for transfers between devices: 14.7 us -> 21.4 us  [dp_shards(): pieces.append(lax.ppermute(values, 'dp', perm))]
    ppermute x5 -> x2, starting transfers between devices: 7.07 us -> 0.87 us  [total_stages(): lax.ppermute(values, axis, [(k, k ^ reach) for k in range(size)])]
    unnamed x275 -> x297, local copies, waits for them, and re-layouts: 15.4 us -> 18.4 us
  transfers between devices with their start and end apart: 98 -> 95, of which waited for: 38 -> 42; matrix products, arithmetic and copies ran while one was open for 21% -> 19% of each run, Pallas kernels for 30% -> 30%
where the time goes in v2:
time: 600 us; the launch traced here: 590 us
  Pallas kernels  193 us (32%)
  waiting for transfers between devices  155 us (26%)
  starting transfers between devices  79.6 us (13%)
  other arithmetic  63.2 us (11%)
  matrix products  44.8 us (7%)
  local copies, waits for them, and re-layouts  37.2 us (6%)
  between operations  17 us (3%)
    pallas_call x5, Pallas kernels, attend_back(): pl.pallas_call(functools.partial(attend_back_kernel, first_block, blocks,...  60.8 us
    pallas_call x5, Pallas kernels, run_experts(): pl.pallas_call(functools.partial(expert_kernel, count, tok, spill), grid_...  53.2 us
    ppermute x12, waiting for transfers between devices, step(): self.ahead = lax.ppermute(self.ahead, 'chip', ring.forward)  52.9 us
    pallas_call x5, Pallas kernels, attend(): pl.pallas_call(functools.partial(attend_kernel, first_block, blocks, firs...  40.7 us
    ppermute x16, waiting for transfers between devices, send(): self.behind = lax.ppermute(self.sent[1], 'chip', self.ring.backward)  39.2 us
    dot_general x7, matrix products, dot_tn(): lax.dot_general(left, right, (((0,), (0,)), ((), ())), preferred_element_...  37.1 us
    pallas_call x5, Pallas kernels, optimize(): pl.pallas_call(functools.partial(optimizer_kernel, blocks, dp_size, grad_...  28.3 us
    ppermute x16, starting transfers between devices, send(): self.ahead = lax.ppermute(self.sent[0], 'chip', self.ring.forward)  24.6 us
  transfers between devices with their start and end apart: 95, of which 42 were waited for; matrix products, arithmetic and copies ran while one was open for 19% of the time, Pallas kernels for 30%

profile of v2, /device:TPU:0, one launch (start us, length us, event | category | flops | bytes accessed | tf_op | source)
XLA Modules:
  0.0 589.7 jit_solution(7062742292663091077)
XLA Ops:
  9.7 3.0 collective-permute-start.2
  13.8 16.7 %collective-permute-done.2.refs_2_ = bf16[384,1024]{1,0:T(8,128)(2,1)} collective-permute-done((bf16[384,1024]{1,0:T(8,128)(2,1)S(1)}, bf16[384,1024]{1,0:T(8,128)(2,1)}, u32[]{:S(2)}, u32[]{:S(2)}) %collective-permute-start.2) | collective-permute-done | bytes 786464 | tf_op jit(solution)/shard_map/ppermute | solution.py:139
  34.3 2.2 copy-done
  41.9 7.6 %collective-permute-done.6.refs_2_ = bf16[384,1024]{1,0:T(8,128)(2,1)} collective-permute-done((bf16[384,1024]{1,0:T(8,128)(2,1)}, bf16[384,1024]{1,0:T(8,128)(2,1)}, u32[]{:S(2)}, u32[]{:S(2)}) %collective-permute-start.6) | collective-permute-done | bytes 786464 | tf_op jit(solution)/shard_map/ppermute | solution.py:139
  50.5 3.0 convert_element_type.191
  53.8 2.1 fusion.18.own_ref
  57.3 5.1 collective-permute-done.5.refs_1_
  65.4 2.4 select_convert_fusion
  71.7 2.1 convert_element_type.192
  76.2 4.4 project.1
  80.6 2.2 collective-permute-done.8.refs_2_
  86.0 7.5 %collective-permute-done.18 = bf16[256,1024]{1,0:T(8,128)(2,1)} collective-permute-done((bf16[256,1024]{1,0:T(8,128)(2,1)}, bf16[256,1024]{1,0:T(8,128)(2,1)}, u32[]{:S(2)}, u32[]{:S(2)}) %collective-permute-start.18) | collective-permute-done | bytes 524320 | tf_op jit(solution)/shard_map/ppermute | solution.py:205
  94.8 7.2 %attend.5 = (f32[6,2,128,512]{3,2,1,0:T(8,128)S(1)}, f32[6,2,8,512]{3,2,1,0:T(8,128)S(1)}) custom-call(s32[16]{0:T(128)S(1)} %concatenate.109.meta_ref, bf16[768,512]{1,0:T(8,128)(2,1)S(1)} %get-tuple-element.228.q_ref, bf16[512,512]{1,0:T(8,128)(2,1)S(1)} %bitcast.158, bf16[2,128,512]{2,1,0:T(8,128)(2,1)S(1)} %get-tuple-element.231.refs_1_), custom_call_target="tpu_custom_call" | custom-call | flops 4831838208 | bytes 12582912 | tf_op jit(solution)/shard_map/attend/pallas_call | solution.py:488
  104.1 8.8 %attend.6 = (f32[6,2,128,512]{3,2,1,0:T(8,128)S(1)}, f32[6,2,8,512]{3,2,1,0:T(8,128)S(1)}) custom-call(s32[16]{0:T(128)S(1)} %concatenate.109.meta_ref, bf16[768,512]{1,0:T(8,128)(2,1)S(1)} %get-tuple-element.228.q_ref, bf16[512,512]{1,0:T(8,128)(2,1)S(1)} %collective-permute-done.10.refs_0_, bf16[512,512]{1,0:T(8,128)(2,1)S(1)} %collective-permute-done.14.refs_1_, ...), custom_call_target="tpu_custom_call" | custom-call | flops 9663676416 | bytes 12582912 | tf_op jit(solution)/shard_map/attend/pallas_call | solution.py:488
  116.6 8.7 %attend.7 = (f32[6,2,128,512]{3,2,1,0:T(8,128)S(1)}, f32[6,2,8,512]{3,2,1,0:T(8,128)S(1)}) custom-call(s32[16]{0:T(128)S(1)} %concatenate.109.meta_ref, bf16[768,512]{1,0:T(8,128)(2,1)S(1)} %get-tuple-element.228.q_ref, bf16[512,512]{1,0:T(8,128)(2,1)S(1)} %collective-permute-done.11.refs_0_, bf16[512,512]{1,0:T(8,128)(2,1)S(1)} %collective-permute-done.15.refs_1_, ...), custom_call_target="tpu_custom_call" | custom-call | flops 9663676416 | bytes 12582912 | tf_op jit(solution)/shard_map/attend/pallas_call | solution.py:488
  129.0 8.8 %attend.8 = (f32[6,2,128,512]{3,2,1,0:T(8,128)S(1)}, f32[6,2,8,512]{3,2,1,0:T(8,128)S(1)}) custom-call(s32[16]{0:T(128)S(1)} %concatenate.109.meta_ref, bf16[768,512]{1,0:T(8,128)(2,1)S(1)} %get-tuple-element.228.q_ref, bf16[512,512]{1,0:T(8,128)(2,1)S(1)} %collective-permute-done.12.refs_0_, bf16[512,512]{1,0:T(8,128)(2,1)S(1)} %collective-permute-done.16.refs_1_, ...), custom_call_target="tpu_custom_call" | custom-call | flops 9663676416 | bytes 12582912 | tf_op jit(solution)/shard_map/attend/pallas_call | solution.py:488
  137.8 7.3 %attend.9 = (f32[768,512]{1,0:T(8,128)S(1)}, bf16[768,512]{1,0:T(8,128)(2,1)S(1)}, f32[8,768]{1,0:T(8,128)S(1)}) custom-call(s32[16]{0:T(128)S(1)} %concatenate.109.meta_ref, bf16[768,512]{1,0:T(8,128)(2,1)S(1)} %get-tuple-element.228.q_ref, bf16[512,512]{1,0:T(8,128)(2,1)S(1)} %constant_dynamic-update-slice_fusion.refs_0_, ...), custom_call_target="tpu_custom_call" | custom-call | flops 4831838208 | bytes 12582912 | tf_op jit(solution)/shard_map/attend/pallas_call | solution.py:488
  151.1 2.2 multiply_reduce_fusion.2
  157.0 5.9 experts.5
  162.9 12.3 %collective-permute-done.22.refs_0_ = bf16[400,1024]{1,0:T(8,128)(2,1)S(1)} collective-permute-done((bf16[400,1024]{1,0:T(8,128)(2,1)S(1)}, bf16[400,1024]{1,0:T(8,128)(2,1)S(1)}, u32[]{:S(2)}, u32[]{:S(2)}) %collective-permute-start.22) | collective-permute-done | bytes 819232 | tf_op jit(solution)/shard_map/ppermute | solution.py:139
  178.9 14.3 %experts.6 = (bf16[384,1024]{1,0:T(8,128)(2,1)S(1)}, bf16[384,1024]{1,0:T(8,128)(2,1)S(1)}, bf16[400,1024]{1,0:T(8,128)(2,1)S(1)}, bf16[400,1024]{1,0:T(8,128)(2...) custom-call(s32[16]{0:T(128)S(1)} %concatenate.109.meta_ref, ...), custom_call_target="tpu_custom_call", output_to_operand_aliasing={{4}: (9, {}), {5}: (10, {}), {6}: (11, {}), {7}: (12, {})} | custom-call | flops 9663676416 | bytes 22020096 | tf_op jit(solution)/shard_map/experts/pallas_call | solution.py:942
  199.5 14.0 %experts.7 = (bf16[384,1024]{1,0:T(8,128)(2,1)S(1)}, bf16[384,1024]{1,0:T(8,128)(2,1)S(1)}, bf16[400,1024]{1,0:T(8,128)(2,1)S(1)}, bf16[400,1024]{1,0:T(8,128)(2...) custom-call(s32[16]{0:T(128)S(1)} %concatenate.109.meta_ref, ...), custom_call_target="tpu_custom_call", output_to_operand_aliasing={{4}: (9, {}), {5}: (10, {}), {6}: (11, {}), {7}: (12, {})} | custom-call | flops 9663676416 | bytes 22020096 | tf_op jit(solution)/shard_map/experts/pallas_call | solution.py:942
  221.2 13.3 %experts.8 = (bf16[384,1024]{1,0:T(8,128)(2,1)S(1)}, bf16[384,1024]{1,0:T(8,128)(2,1)S(1)}, bf16[400,1024]{1,0:T(8,128)(2,1)S(1)}, bf16[400,1024]{1,0:T(8,128)(2...) custom-call(s32[16]{0:T(128)S(1)} %concatenate.109.meta_ref, ...), custom_call_target="tpu_custom_call", output_to_operand_aliasing={{4}: (9, {}), {5}: (10, {}), {6}: (11, {}), {7}: (12, {})} | custom-call | flops 9663676416 | bytes 22020096 | tf_op jit(solution)/shard_map/experts/pallas_call | solution.py:942
  235.0 5.7 experts.9
  243.0 8.9 %collective-permute-done.32 = bf16[192,1024]{1,0:T(8,128)(2,1)S(1)} collective-permute-done((bf16[192,1024]{1,0:T(8,128)(2,1)S(1)}, bf16[192,1024]{1,0:T(8,128)(2,1)S(1)}, u32[]{:S(2)}, u32[]{:S(2)}) %collective-permute-start.32) | collective-permute-done | bytes 393248 | tf_op jit(solution)/shard_map/ppermute | solution.py:161
  254.3 9.0 %fusion.15 = bf16[1024,1024]{1,0:T(8,128)(2,1)S(1)} fusion(bf16[3072,1024]{1,0:T(8,128)(2,1)S(1)} %copy-done.53, bf16[3072,2048]{1,0:T(8,128)(2,1)} %get-tuple-element.309), kind=kOutput, calls=%fused_computation.25 | convolution fusion | flops 6443499520 | bytes 14680064 | tf_op jit(solution)/shard_map/dot_general | solution.py:40
  263.3 7.3 %fusion.29 = bf16[512,1024]{1,0:T(8,128)(2,1)S(1)} fusion(bf16[3072,1024]{1,0:T(8,128)(2,1)} %get-tuple-element.311, bf16[3072,1024]{1,0:T(8,128)(2,1)} %get-tuple-element.310), kind=kOutput, calls=%fused_computation.52 | convolution fusion | flops 3221749760 | bytes 10485760 | tf_op jit(solution)/shard_map/dot_general | solution.py:40
  273.9 18.2 %collective-permute-done.37 = bf16[400,1024]{1,0:T(8,128)(2,1)S(1)} collective-permute-done((bf16[400,1024]{1,0:T(8,128)(2,1)S(1)}, bf16[400,1024]{1,0:T(8,128)(2,1)S(1)}, u32[]{:S(2)}, u32[]{:S(2)}) %collective-permute-start.37) | collective-permute-done | bytes 819232 | tf_op jit(solution)/shard_map/ppermute | solution.py:162
  294.1 1.9 collective-permute-start.40
  296.1 9.2 %add_convert_fusion = bf16[1024,1024]{1,0:T(8,128)(2,1)} fusion(bf16[1024,1024]{1,0:T(8,128)(2,1)} %copy-done.139, bf16[3072,1024]{1,0:T(8,128)(2,1)S(1)} %copy-done.53, bf16[3072,2048]{1,0:T(8,128)(2,1)S(1)} %bitcast.161), kind=kOutput, calls=%fused_computation.4 | convolution fusion | flops 6445596672 | bytes 16777216 | tf_op jit(solution)/shard_map/dot_general | solution.py:40
  305.3 6.3 %add_convert_fusion.1 = bf16[512,1024]{1,0:T(8,128)(2,1)} fusion(bf16[512,1024]{1,0:T(8,128)(2,1)S(1)} %copy-done.141, bf16[3072,1024]{1,0:T(8,128)(2,1)S(1)} %bitcast.164, bf16[3072,1024]{1,0:T(8,128)(2,1)} %get-tuple-element.310), kind=kOutput, calls=%fused_computation.24 | convolution fusion | flops 3222798336 | bytes 11534336 | tf_op jit(solution)/shard_map/dot_general | solution.py:40
  320.4 5.7 collective-permute-done.42
  328.1 2.2 collective-permute-done.44
  330.5 2.8 convolution_convert_fusion.2.do_ref
  333.3 7.7 %attend_back.5 = (bf16[512,512]{1,0:T(8,128)(2,1)S(1)}, f32[6,2,128,512]{3,2,1,0:T(8,128)S(1)}) custom-call(s32[16]{0:T(128)S(1)} %concatenate.109.meta_ref, bf16[768,512]{1,0:T(8,128)(2,1)S(1)} %copy-done.48, bf16[768,512]{1,0:T(8,128)(2,1)S(1)} %convolution_convert_fusion.2.do_ref, f32[768,512]{1,0:T(8,128)S(1)} %copy-done.52, ...), custom_call_target="tpu_custom_call" | custom-call | flops 11072962560 | bytes 16777216 | tf_op jit(solution)/shard_map/attend_back/pallas_call | solution.py:538
  345.8 13.3 %attend_back.6 = (bf16[512,512]{1,0:T(8,128)(2,1)S(1)}, bf16[512,512]{1,0:T(8,128)(2,1)S(1)}, f32[6,2,128,512]{3,2,1,0:T(8,128)S(1)}) custom-call(s32[16]{0:T(128)S(1)} %concatenate.109.meta_ref, bf16[768,512]{1,0:T(8,128)(2,1)S(1)} %copy-done.48, bf16[768,512]{1,0:T(8,128)(2,1)S(1)} %convolution_convert_fusion.2.do_ref, f32[768,512]{1,0:T(8,128)S(1)} %copy-done.52, ...), custom_call_target="tpu_custom_call" | custom-call | flops 22145925120 | bytes 16777216 | tf_op jit(solution)/shard_map/attend_back/pallas_call | solution.py:538
  363.7 13.2 %attend_back.7 = (bf16[512,512]{1,0:T(8,128)(2,1)S(1)}, bf16[512,512]{1,0:T(8,128)(2,1)S(1)}, f32[6,2,128,512]{3,2,1,0:T(8,128)S(1)}) custom-call(s32[16]{0:T(128)S(1)} %concatenate.109.meta_ref, bf16[768,512]{1,0:T(8,128)(2,1)S(1)} %copy-done.48, bf16[768,512]{1,0:T(8,128)(2,1)S(1)} %convolution_convert_fusion.2.do_ref, f32[768,512]{1,0:T(8,128)S(1)} %copy-done.52, ...), custom_call_target="tpu_custom_call" | custom-call | flops 22145925120 | bytes 16777216 | tf_op jit(solution)/shard_map/attend_back/pallas_call | solution.py:538
  381.0 13.3 %attend_back.8 = (bf16[512,512]{1,0:T(8,128)(2,1)S(1)}, bf16[512,512]{1,0:T(8,128)(2,1)S(1)}, f32[6,2,128,512]{3,2,1,0:T(8,128)S(1)}) custom-call(s32[16]{0:T(128)S(1)} %concatenate.109.meta_ref, bf16[768,512]{1,0:T(8,128)(2,1)S(1)} %copy-done.48, bf16[768,512]{1,0:T(8,128)(2,1)S(1)} %convolution_convert_fusion.2.do_ref, f32[768,512]{1,0:T(8,128)S(1)} %copy-done.52, ...), custom_call_target="tpu_custom_call" | custom-call | flops 22145925120 | bytes 16777216 | tf_op jit(solution)/shard_map/attend_back/pallas_call | solution.py:538
  400.9 13.4 %attend_back.9 = (bf16[512,512]{1,0:T(8,128)(2,1)S(1)}, bf16[768,512]{1,0:T(8,128)(2,1)S(1)}, f32[2,128,512]{2,1,0:T(8,128)S(1)}) custom-call(s32[16]{0:T(128)S(1)} %concatenate.109.meta_ref, bf16[768,512]{1,0:T(8,128)(2,1)S(1)} %copy-done.48, bf16[768,512]{1,0:T(8,128)(2,1)S(1)} %convolution_convert_fusion.2.do_ref, f32[768,512]{1,0:T(8,128)S(1)} %copy-done.52, ...), custom_call_target="tpu_custom_call" | custom-call | flops 11072962560 | bytes 16777216 | tf_op jit(solution)/shard_map/attend_back/pallas_call | solution.py:538
  414.4 9.4 %collective-permute-done.56 = bf16[512,512]{1,0:T(8,128)(2,1)S(1)} collective-permute-done((bf16[512,512]{1,0:T(8,128)(2,1)S(1)}, bf16[512,512]{1,0:T(8,128)(2,1)S(1)}, u32[]{:S(2)}, u32[]{:S(2)}) %collective-permute-start.56) | collective-permute-done | bytes 524320 | tf_op jit(solution)/shard_map/ppermute | solution.py:162
  425.7 3.2 convolution_convert_fusion
  430.6 1.8 fusion.98
  436.4 1.9 collective-permute-done.57
  441.6 3.4 fusion.14
  445.0 3.1 collective-permute-done.60
  449.6 2.1 add.371
  451.7 1.9 add.370
  453.7 3.7 fusion.35
  461.0 3.0 fusion.20
  464.0 2.9 collective-permute-done.64
  474.5 5.3 collective-permute-done.69
  489.7 3.4 shard_step.1
  493.6 2.1 fusion.23
  499.6 5.1 collective-permute-done.74
  508.5 8.8 %collective-permute-done.75.refs_0_ = bf16[224,1024]{1,0:T(8,128)(2,1)S(1)} collective-permute-done((bf16[224,1024]{1,0:T(8,128)(2,1)S(1)}, bf16[224,1024]{1,0:T(8,128)(2,1)S(1)}, u32[]{:S(2)}, u32[]{:S(2)}) %collective-permute-start.75) | collective-permute-done | bytes 458784 | tf_op jit(solution)/shard_map/ppermute | solution.py:139
  520.7 4.8 optimize.5
  532.3 3.7 collective-permute-done.72
  536.0 2.8 convert_element_type.237
  538.8 4.1 convert_element_type.235
  543.4 6.3 %optimize.6 = (f32[2,512,2048]{2,1,0:T(8,128)}, f32[512,2048]{1,0:T(8,128)}, f32[512,2048]{1,0:T(8,128)}, f32[2,2,256,1024]{3,2,1,0:T(8,128)}, f32[2,256,1024]{2,1,0:T(8,128)}, /*index=5*/f32[2,256,1024]{2,1,0:T(8,128)}) custom-call(s32[16]{0:T(128)} %copy-done.36, ...), custom_call_target="tpu_custom_call", output_to_operand_aliasing={{0}: (11, {}), {1}: (12, {}), {2}: (13, {}), {3}: (14, {}),... | custom-call | flops 7864320 | bytes 11796480 | tf_op jit(solution)/shard_map/optimize/pallas_call | solution.py:847
  552.0 1.9 add_convert_fusion.2
  557.8 6.2 %optimize.7 = (f32[2,512,2048]{2,1,0:T(8,128)}, f32[512,2048]{1,0:T(8,128)}, f32[512,2048]{1,0:T(8,128)}, f32[2,2,256,1024]{3,2,1,0:T(8,128)}, f32[2,256,1024]{2,1,0:T(8,128)}, /*index=5*/f32[2,256,1024]{2,1,0:T(8,128)}) custom-call(s32[16]{0:T(128)} %copy-done.36, ...), custom_call_target="tpu_custom_call", output_to_operand_aliasing={{0}: (11, {}), {1}: (12, {}), {2}: (13, {}), {3}: (14, {}),... | custom-call | flops 7864320 | bytes 11796480 | tf_op jit(solution)/shard_map/optimize/pallas_call | solution.py:847
  571.1 6.2 %optimize.8 = (f32[2,512,2048]{2,1,0:T(8,128)}, f32[512,2048]{1,0:T(8,128)}, f32[512,2048]{1,0:T(8,128)}, f32[2,2,256,1024]{3,2,1,0:T(8,128)}, f32[2,256,1024]{2,1,0:T(8,128)}, /*index=5*/f32[2,256,1024]{2,1,0:T(8,128)}) custom-call(s32[16]{0:T(128)} %copy-done.36, ...), custom_call_target="tpu_custom_call", output_to_operand_aliasing={{0}: (11, {}), {1}: (12, {}), {2}: (13, {}), {3}: (14, {}),... | custom-call | flops 7864320 | bytes 11796480 | tf_op jit(solution)/shard_map/optimize/pallas_call | solution.py:847
  578.1 4.8 optimize.9
  (612 shorter events, 171.9 us)
Async XLA Ops:
  7.2 141.6 %all-gather.5.cloned.1.call-start = ((), (), s32[]{:S(2)}) async-start(), calls=%async_computation | async-start | bytes 3145728 | tf_op jit(solution)/shard_map/all_gather | solution.py:1054
  9.7 20.7 %collective-permute-start.2 = (bf16[384,1024]{1,0:T(8,128)(2,1)S(1)}, bf16[384,1024]{1,0:T(8,128)(2,1)}, u32[]{:S(2)}, u32[]{:S(2)}) collective-permute-start(bf16[384,1024]{1,0:T(8,128)(2,1)S(1)} %pad_maximum_fusion.8.refs_1_), channel_id=1, source_target_pairs={{0,2},{2,6},{6,10},{10,14},{14,12},{12,8},{8,4},{4,0},{1,3},{3,7},... | collective-permute-start | bytes 2359304 | tf_op jit(solution)/shard_map/ppermute | solution.py:139
  12.7 19.4 %collective-permute-start.3 = (bf16[384,1024]{1,0:T(8,128)(2,1)S(1)}, bf16[384,1024]{1,0:T(8,128)(2,1)}, u32[]{:S(2)}, u32[]{:S(2)}) collective-permute-start(bf16[384,1024]{1,0:T(8,128)(2,1)S(1)} %pad_maximum_fusion.8.refs_1_), channel_id=1, source_target_pairs={{2,0},{6,2},{10,6},{14,10},{12,14},{8,12},{4,8},{0,4},{3,1},{7,3},... | collective-permute-start | bytes 2359304 | tf_op jit(solution)/shard_map/ppermute | solution.py:140
  30.5 19.0 %collective-permute-start.6 = (bf16[384,1024]{1,0:T(8,128)(2,1)}, bf16[384,1024]{1,0:T(8,128)(2,1)}, u32[]{:S(2)}, u32[]{:S(2)}) collective-permute-start(bf16[384,1024]{1,0:T(8,128)(2,1)} %collective-permute-done.2.refs_2_), channel_id=1, source_target_pairs={{0,2},{2,6},{6,10},{10,14},{14,12},{12,8},{8,4},{4,0},{1,3},{3,7},... | collective-permute-start | bytes 2359304 | tf_op jit(solution)/shard_map/ppermute | solution.py:139
  32.1 18.3 %collective-permute-start.7 = (bf16[384,1024]{1,0:T(8,128)(2,1)}, bf16[384,1024]{1,0:T(8,128)(2,1)S(1)}, u32[]{:S(2)}, u32[]{:S(2)}) collective-permute-start(bf16[384,1024]{1,0:T(8,128)(2,1)} %collective-permute-done.3.refs_3_), channel_id=1, source_target_pairs={{2,0},{6,2},{10,6},{14,10},{12,14},{8,12},{4,8},{0,4},{3,1},{7,3},... | collective-permute-start | bytes 2359304 | tf_op jit(solution)/shard_map/ppermute | solution.py:140
  32.5 21.2 %collective-permute-start.1 = (bf16[18,512]{1,0:T(8,128)(2,1)S(1)}, bf16[18,512]{1,0:T(8,128)(2,1)S(1)}, u32[]{:S(2)}, u32[]{:S(2)}) collective-permute-start(bf16[18,512]{1,0:T(8,128)(2,1)S(1)} %fusion.63), channel_id=1, source_target_pairs={{0,16},{16,0},{1,17},{17,1},{2,18},{18,2},{3,19},{19,3},{4,20},{20... | collective-permute-start | bytes 55304 | tf_op jit(solution)/shard_map/ppermute | solution.py:205
  34.3 36.8 %collective-permute-start = (s32[1]{0:T(128)}, s32[1]{0:T(128)}, u32[]{:S(2)}, u32[]{:S(2)}) collective-permute-start(s32[1]{0:T(128)} %param.31), channel_id=1, source_target_pairs={{0,1},{1,0},{2,3},{3,2},{4,5},{5,4},{6,7},{7,6},{8,9},{9,8},{10,11... | collective-permute-start | bytes 20 | tf_op jit(solution)/shard_map/ppermute | solution.py:77
  36.7 25.6 %collective-permute-start.5 = (bf16[512,1024]{1,0:T(8,128)(2,1)S(1)}, bf16[512,1024]{1,0:T(8,128)(2,1)S(1)}, u32[]{:S(2)}, u32[]{:S(2)}) collective-permute-start(bf16[512,1024]{1,0:T(8,128)(2,1)S(1)} %cast_core_columns.1.refs_0_), channel_id=1, source_target_pairs={{0,16},{16,0},{1,17},{17,1},{2,18},{18,2},{3,19},{19,3},{4,20},{20... | collective-permute-start | bytes 3145736 | tf_op jit(solution)/shard_map/ppermute | solution.py:205
  53.5 95.8 %all-gather.7.cloned.1.call-start = ((), (), s32[]{:S(2)}) async-start(), calls=%async_computation.1 | async-start | bytes 1572864 | tf_op jit(solution)/shard_map/all_gather | solution.py:1055
  55.9 18.0 %collective-permute-start.4 = (bf16[384,1024]{1,0:T(8,128)(2,1)}, bf16[384,1024]{1,0:T(8,128)(2,1)}, u32[]{:S(2)}, u32[]{:S(2)}) collective-permute-start(bf16[384,1024]{1,0:T(8,128)(2,1)} %fusion.18.own_ref), channel_id=1, source_target_pairs={{0,1},{1,0},{2,3},{3,2},{4,5},{5,4},{6,7},{7,6},{8,9},{9,8},{10,11... | collective-permute-start | bytes 2359304 | tf_op jit(solution)/shard_map/ppermute | solution.py:77
  63.3 19.4 %collective-permute-start.8 = (bf16[384,1024]{1,0:T(8,128)(2,1)}, bf16[384,1024]{1,0:T(8,128)(2,1)S(1)}, u32[]{:S(2)}, u32[]{:S(2)}) collective-permute-start(bf16[384,1024]{1,0:T(8,128)(2,1)} %collective-permute-done.6.refs_2_), channel_id=1, source_target_pairs={{0,2},{2,6},{6,10},{10,14},{14,12},{12,8},{8,4},{4,0},{1,3},{3,7},... | collective-permute-start | bytes 2359304 | tf_op jit(solution)/shard_map/ppermute | solution.py:139
  64.8 19.1 %collective-permute-start.9 = (bf16[384,1024]{1,0:T(8,128)(2,1)}, bf16[384,1024]{1,0:T(8,128)(2,1)S(1)}, u32[]{:S(2)}, u32[]{:S(2)}) collective-permute-start(bf16[384,1024]{1,0:T(8,128)(2,1)} %copy-done.28), channel_id=1, source_target_pairs={{2,0},{6,2},{10,6},{14,10},{12,14},{8,12},{4,8},{0,4},{3,1},{7,3},... | collective-permute-start | bytes 2359304 | tf_op jit(solution)/shard_map/ppermute | solution.py:140
  67.8 25.7 %collective-permute-start.18 = (bf16[256,1024]{1,0:T(8,128)(2,1)}, bf16[256,1024]{1,0:T(8,128)(2,1)}, u32[]{:S(2)}, u32[]{:S(2)}) collective-permute-start(bf16[256,1024]{1,0:T(8,128)(2,1)} %select_convert_fusion), channel_id=1, source_target_pairs={{0,16},{16,0},{1,17},{17,1},{2,18},{18,2},{3,19},{19,3},{4,20},{20... | collective-permute-start | bytes 1572872 | tf_op jit(solution)/shard_map/ppermute | solution.py:205
  73.9 462.1 %all-gather.11.cloned.1.call-start = ((), (), s32[]{:S(2)}) async-start(), calls=%async_computation.3 | async-start | bytes 1572864 | tf_op jit(solution)/shard_map/all_gather | solution.py:1331
  83.9 18.1 %collective-permute-start.10 = (bf16[512,512]{1,0:T(8,128)(2,1)S(1)}, bf16[512,512]{1,0:T(8,128)(2,1)S(1)}, u32[]{:S(2)}, u32[]{:S(2)}) collective-permute-start(bf16[512,512]{1,0:T(8,128)(2,1)S(1)} %bitcast.156), channel_id=1, source_target_pairs={{0,2},{2,6},{6,10},{10,14},{14,12},{12,8},{8,4},{4,0},{1,3},{3,7},... | collective-permute-start | bytes 1572872 | tf_op jit(solution)/shard_map/ppermute | solution.py:139
  85.5 18.1 %collective-permute-start.14 = (bf16[512,512]{1,0:T(8,128)(2,1)S(1)}, bf16[512,512]{1,0:T(8,128)(2,1)S(1)}, u32[]{:S(2)}, u32[]{:S(2)}) collective-permute-start(bf16[512,512]{1,0:T(8,128)(2,1)S(1)} %bitcast.157), channel_id=1, source_target_pairs={{2,0},{6,2},{10,6},{14,10},{12,14},{8,12},{4,8},{0,4},{3,1},{7,3},... | collective-permute-start | bytes 1572872 | tf_op jit(solution)/shard_map/ppermute | solution.py:140
  102.0 12.5 %collective-permute-start.11 = (bf16[512,512]{1,0:T(8,128)(2,1)S(1)}, bf16[512,512]{1,0:T(8,128)(2,1)S(1)}, u32[]{:S(2)}, u32[]{:S(2)}) collective-permute-start(bf16[512,512]{1,0:T(8,128)(2,1)S(1)} %collective-permute-done.10.refs_0_), channel_id=1, source_target_pairs={{0,2},{2,6},{6,10},{10,14},{14,12},{12,8},{8,4},{4,0},{1,3},{3,7},... | collective-permute-start | bytes 1572872 | tf_op jit(solution)/shard_map/ppermute | solution.py:139
  103.6 12.5 %collective-permute-start.15 = (bf16[512,512]{1,0:T(8,128)(2,1)S(1)}, bf16[512,512]{1,0:T(8,128)(2,1)S(1)}, u32[]{:S(2)}, u32[]{:S(2)}) collective-permute-start(bf16[512,512]{1,0:T(8,128)(2,1)S(1)} %collective-permute-done.14.refs_1_), channel_id=1, source_target_pairs={{2,0},{6,2},{10,6},{14,10},{12,14},{8,12},{4,8},{0,4},{3,1},{7,3},... | collective-permute-start | bytes 1572872 | tf_op jit(solution)/shard_map/ppermute | solution.py:140
  155.0 20.3 %collective-permute-start.22 = (bf16[400,1024]{1,0:T(8,128)(2,1)S(1)}, bf16[400,1024]{1,0:T(8,128)(2,1)S(1)}, u32[]{:S(2)}, u32[]{:S(2)}) collective-permute-start(bf16[400,1024]{1,0:T(8,128)(2,1)S(1)} %pad_maximum_fusion.3.refs_0_), channel_id=1, source_target_pairs={{0,2},{2,6},{6,10},{10,14},{14,12},{12,8},{8,4},{4,0},{1,3},{3,7},... | collective-permute-start | bytes 2457608 | tf_op jit(solution)/shard_map/ppermute | solution.py:139
  156.5 20.0 %collective-permute-start.23 = (bf16[400,1024]{1,0:T(8,128)(2,1)S(1)}, bf16[400,1024]{1,0:T(8,128)(2,1)S(1)}, u32[]{:S(2)}, u32[]{:S(2)}) collective-permute-start(bf16[400,1024]{1,0:T(8,128)(2,1)S(1)} %pad_maximum_fusion.3.refs_0_), channel_id=1, source_target_pairs={{2,0},{6,2},{10,6},{14,10},{12,14},{8,12},{4,8},{0,4},{3,1},{7,3},... | collective-permute-start | bytes 2457608 | tf_op jit(solution)/shard_map/ppermute | solution.py:140
  176.5 19.1 %collective-permute-start.24 = (bf16[400,1024]{1,0:T(8,128)(2,1)S(1)}, bf16[400,1024]{1,0:T(8,128)(2,1)S(1)}, u32[]{:S(2)}, u32[]{:S(2)}) collective-permute-start(bf16[400,1024]{1,0:T(8,128)(2,1)S(1)} %collective-permute-done.22.refs_0_), channel_id=1, source_target_pairs={{0,2},{2,6},{6,10},{10,14},{14,12},{12,8},{8,4},{4,0},{1,3},{3,7},... | collective-permute-start | bytes 2457608 | tf_op jit(solution)/shard_map/ppermute | solution.py:139
  178.1 19.2 %collective-permute-start.25 = (bf16[400,1024]{1,0:T(8,128)(2,1)S(1)}, bf16[400,1024]{1,0:T(8,128)(2,1)S(1)}, u32[]{:S(2)}, u32[]{:S(2)}) collective-permute-start(bf16[400,1024]{1,0:T(8,128)(2,1)S(1)} %collective-permute-done.23.refs_1_), channel_id=1, source_target_pairs={{2,0},{6,2},{10,6},{14,10},{12,14},{8,12},{4,8},{0,4},{3,1},{7,3},... | collective-permute-start | bytes 2457608 | tf_op jit(solution)/shard_map/ppermute | solution.py:140
  197.3 17.9 %collective-permute-start.26 = (bf16[400,1024]{1,0:T(8,128)(2,1)S(1)}, bf16[400,1024]{1,0:T(8,128)(2,1)S(1)}, u32[]{:S(2)}, u32[]{:S(2)}) collective-permute-start(bf16[400,1024]{1,0:T(8,128)(2,1)S(1)} %collective-permute-done.24.refs_0_), channel_id=1, source_target_pairs={{0,2},{2,6},{6,10},{10,14},{14,12},{12,8},{8,4},{4,0},{1,3},{3,7},... | collective-permute-start | bytes 2457608 | tf_op jit(solution)/shard_map/ppermute | solution.py:139
  198.9 17.8 %collective-permute-start.27 = (bf16[400,1024]{1,0:T(8,128)(2,1)S(1)}, bf16[400,1024]{1,0:T(8,128)(2,1)S(1)}, u32[]{:S(2)}, u32[]{:S(2)}) collective-permute-start(bf16[400,1024]{1,0:T(8,128)(2,1)S(1)} %collective-permute-done.25.refs_1_), channel_id=1, source_target_pairs={{2,0},{6,2},{10,6},{14,10},{12,14},{8,12},{4,8},{0,4},{3,1},{7,3},... | collective-permute-start | bytes 2457608 | tf_op jit(solution)/shard_map/ppermute | solution.py:140
  216.8 17.7 %collective-permute-start.30 = (bf16[192,1024]{1,0:T(8,128)(2,1)S(1)}, bf16[192,1024]{1,0:T(8,128)(2,1)S(1)}, u32[]{:S(2)}, u32[]{:S(2)}) collective-permute-start(bf16[192,1024]{1,0:T(8,128)(2,1)S(1)} %slice.290), channel_id=1, source_target_pairs={{0,2},{2,6},{6,10},{10,14},{14,12},{12,8},{8,4},{4,0},{1,3},{3,7},... | collective-permute-start | bytes 1179656 | tf_op jit(solution)/shard_map/ppermute | solution.py:144
  218.5 16.0 %collective-permute-start.31 = (bf16[192,1024]{1,0:T(8,128)(2,1)S(1)}, bf16[192,1024]{1,0:T(8,128)(2,1)S(1)}, u32[]{:S(2)}, u32[]{:S(2)}) collective-permute-start(bf16[192,1024]{1,0:T(8,128)(2,1)S(1)} %slice.291), channel_id=1, source_target_pairs={{2,0},{6,2},{10,6},{14,10},{12,14},{8,12},{4,8},{0,4},{3,1},{7,3},... | collective-permute-start | bytes 1179656 | tf_op jit(solution)/shard_map/ppermute | solution.py:145
  218.9 16.0 %collective-permute-start.29 = (bf16[208,1024]{1,0:T(8,128)(2,1)S(1)}, bf16[208,1024]{1,0:T(8,128)(2,1)S(1)}, u32[]{:S(2)}, u32[]{:S(2)}) collective-permute-start(bf16[208,1024]{1,0:T(8,128)(2,1)S(1)} %slice.289), channel_id=1, source_target_pairs={{2,0},{6,2},{10,6},{14,10},{12,14},{8,12},{4,8},{0,4},{3,1},{7,3},... | collective-permute-start | bytes 1277960 | tf_op jit(solution)/shard_map/ppermute | solution.py:145
  219.4 15.2 %collective-permute-start.28 = (bf16[192,1024]{1,0:T(8,128)(2,1)S(1)}, bf16[192,1024]{1,0:T(8,128)(2,1)S(1)}, u32[]{:S(2)}, u32[]{:S(2)}) collective-permute-start(bf16[192,1024]{1,0:T(8,128)(2,1)S(1)} %slice.288), channel_id=1, source_target_pairs={{0,2},{2,6},{6,10},{10,14},{14,12},{12,8},{8,4},{4,0},{1,3},{3,7},... | collective-permute-start | bytes 1179656 | tf_op jit(solution)/shard_map/ppermute | solution.py:144
  252.1 18.5 %collective-permute-start.35 = (bf16[400,1024]{1,0:T(8,128)(2,1)S(1)}, bf16[400,1024]{1,0:T(8,128)(2,1)S(1)}, u32[]{:S(2)}, u32[]{:S(2)}) collective-permute-start(bf16[400,1024]{1,0:T(8,128)(2,1)S(1)} %pad_maximum_fusion.6), channel_id=1, source_target_pairs={{2,0},{6,2},{10,6},{14,10},{12,14},{8,12},{4,8},{0,4},{3,1},{7,3},... | collective-permute-start | bytes 2457608 | tf_op jit(solution)/shard_map/ppermute | solution.py:162
  252.6 18.1 %collective-permute-start.34 = (bf16[400,1024]{1,0:T(8,128)(2,1)S(1)}, bf16[400,1024]{1,0:T(8,128)(2,1)S(1)}, u32[]{:S(2)}, u32[]{:S(2)}) collective-permute-start(bf16[400,1024]{1,0:T(8,128)(2,1)S(1)} %pad_maximum_fusion.5), channel_id=1, source_target_pairs={{0,2},{2,6},{6,10},{10,14},{14,12},{12,8},{8,4},{4,0},{1,3},{3,7},... | collective-permute-start | bytes 2457608 | tf_op jit(solution)/shard_map/ppermute | solution.py:161
  271.3 20.9 %collective-permute-start.38 = (bf16[1024,1024]{1,0:T(8,128)(2,1)S(1)}, bf16[1024,1024]{1,0:T(8,128)(2,1)S(1)}, u32[]{:S(2)}, u32[]{:S(2)}) collective-permute-start(bf16[1024,1024]{1,0:T(8,128)(2,1)S(1)} %fusion.15), channel_id=1, source_target_pairs={{0,1},{1,0},{2,3},{3,2},{4,5},{5,4},{6,7},{7,6},{8,9},{9,8},{10,11... | collective-permute-start | bytes 6291464 | tf_op jit(solution)/shard_map/ppermute | solution.py:77
  271.4 20.8 %collective-permute-start.39 = (bf16[512,1024]{1,0:T(8,128)(2,1)S(1)}, bf16[512,1024]{1,0:T(8,128)(2,1)S(1)}, u32[]{:S(2)}, u32[]{:S(2)}) collective-permute-start(bf16[512,1024]{1,0:T(8,128)(2,1)S(1)} %fusion.29), channel_id=1, source_target_pairs={{0,1},{1,0},{2,3},{3,2},{4,5},{5,4},{6,7},{7,6},{8,9},{9,8},{10,11... | collective-permute-start | bytes 3145736 | tf_op jit(solution)/shard_map/ppermute | solution.py:77
  271.9 20.2 %collective-permute-start.37 = (bf16[400,1024]{1,0:T(8,128)(2,1)S(1)}, bf16[400,1024]{1,0:T(8,128)(2,1)S(1)}, u32[]{:S(2)}, u32[]{:S(2)}) collective-permute-start(bf16[400,1024]{1,0:T(8,128)(2,1)S(1)} %add.338), channel_id=1, source_target_pairs={{2,0},{6,2},{10,6},{14,10},{12,14},{8,12},{4,8},{0,4},{3,1},{7,3},... | collective-permute-start | bytes 2457608 | tf_op jit(solution)/shard_map/ppermute | solution.py:162
  272.2 19.9 %collective-permute-start.36 = (bf16[400,1024]{1,0:T(8,128)(2,1)S(1)}, bf16[400,1024]{1,0:T(8,128)(2,1)S(1)}, u32[]{:S(2)}, u32[]{:S(2)}) collective-permute-start(bf16[400,1024]{1,0:T(8,128)(2,1)S(1)} %add.337), channel_id=1, source_target_pairs={{0,2},{2,6},{6,10},{10,14},{14,12},{12,8},{8,4},{4,0},{1,3},{3,7},... | collective-permute-start | bytes 2457608 | tf_op jit(solution)/shard_map/ppermute | solution.py:161
  293.1 19.4 %collective-permute-start.41 = (bf16[400,1024]{1,0:T(8,128)(2,1)S(1)}, bf16[400,1024]{1,0:T(8,128)(2,1)}, u32[]{:S(2)}, u32[]{:S(2)}) collective-permute-start(bf16[400,1024]{1,0:T(8,128)(2,1)S(1)} %add.340), channel_id=1, source_target_pairs={{2,0},{6,2},{10,6},{14,10},{12,14},{8,12},{4,8},{0,4},{3,1},{7,3},... | collective-permute-start | bytes 2457608 | tf_op jit(solution)/shard_map/ppermute | solution.py:162
  294.1 19.6 %collective-permute-start.40 = (bf16[400,1024]{1,0:T(8,128)(2,1)S(1)}, bf16[400,1024]{1,0:T(8,128)(2,1)S(1)}, u32[]{:S(2)}, u32[]{:S(2)}) collective-permute-start(bf16[400,1024]{1,0:T(8,128)(2,1)S(1)} %add.339), channel_id=1, source_target_pairs={{0,2},{2,6},{6,10},{10,14},{14,12},{12,8},{8,4},{4,0},{1,3},{3,7},... | collective-permute-start | bytes 2457608 | tf_op jit(solution)/shard_map/ppermute | solution.py:161
  341.1 20.3 %collective-permute-start.47 = (bf16[256,512]{1,0:T(8,128)(2,1)S(1)}, bf16[256,512]{1,0:T(8,128)(2,1)S(1)}, u32[]{:S(2)}, u32[]{:S(2)}) collective-permute-start(bf16[256,512]{1,0:T(8,128)(2,1)S(1)} %get-tuple-element.459), channel_id=1, source_target_pairs={{0,2},{2,6},{6,10},{10,14},{14,12},{12,8},{8,4},{4,0},{1,3},{3,7},... | collective-permute-start | bytes 786440 | tf_op jit(solution)/shard_map/ppermute | solution.py:161
  342.4 19.0 %collective-permute-start.48 = (bf16[256,512]{1,0:T(8,128)(2,1)S(1)}, bf16[256,512]{1,0:T(8,128)(2,1)S(1)}, u32[]{:S(2)}, u32[]{:S(2)}) collective-permute-start(bf16[256,512]{1,0:T(8,128)(2,1)S(1)} %get-tuple-element.458), channel_id=1, source_target_pairs={{2,0},{6,2},{10,6},{14,10},{12,14},{8,12},{4,8},{0,4},{3,1},{7,3},... | collective-permute-start | bytes 786440 | tf_op jit(solution)/shard_map/ppermute | solution.py:162
  343.3 50.9 %collective-permute-start.46 = (bf16[384,1024]{1,0:T(8,128)(2,1)S(1)}, bf16[384,1024]{1,0:T(8,128)(2,1)S(1)}, u32[]{:S(2)}, u32[]{:S(2)}) collective-permute-start(bf16[384,1024]{1,0:T(8,128)(2,1)S(1)} %pad_maximum_fusion.11), channel_id=1, source_target_pairs={{2,0},{6,2},{10,6},{14,10},{12,14},{8,12},{4,8},{0,4},{3,1},{7,3},... | collective-permute-start | bytes 2359304 | tf_op jit(solution)/shard_map/ppermute | solution.py:162
  344.1 50.2 %collective-permute-start.45 = (bf16[384,1024]{1,0:T(8,128)(2,1)S(1)}, bf16[384,1024]{1,0:T(8,128)(2,1)S(1)}, u32[]{:S(2)}, u32[]{:S(2)}) collective-permute-start(bf16[384,1024]{1,0:T(8,128)(2,1)S(1)} %pad_maximum_fusion.10), channel_id=1, source_target_pairs={{0,2},{2,6},{6,10},{10,14},{14,12},{12,8},{8,4},{4,0},{1,3},{3,7},... | collective-permute-start | bytes 2359304 | tf_op jit(solution)/shard_map/ppermute | solution.py:161
  359.3 82.3 %collective-permute-start.61 = (bf16[512,1024]{1,0:T(8,128)(2,1)S(1)}, bf16[512,1024]{1,0:T(8,128)(2,1)S(1)}, u32[]{:S(2)}, u32[]{:S(2)}) collective-permute-start(bf16[512,1024]{1,0:T(8,128)(2,1)S(1)} %get-tuple-element.440), channel_id=1, source_target_pairs={{0,16},{16,0},{1,17},{17,1},{2,18},{18,2},{3,19},{19,3},{4,20},{20... | collective-permute-start | bytes 3145736 | tf_op jit(solution)/shard_map/ppermute | solution.py:1174
  361.5 17.1 %collective-permute-start.50 = (bf16[512,512]{1,0:T(8,128)(2,1)S(1)}, bf16[512,512]{1,0:T(8,128)(2,1)S(1)}, u32[]{:S(2)}, u32[]{:S(2)}) collective-permute-start(bf16[512,512]{1,0:T(8,128)(2,1)S(1)} %pad_maximum_fusion.16), channel_id=1, source_target_pairs={{2,0},{6,2},{10,6},{14,10},{12,14},{8,12},{4,8},{0,4},{3,1},{7,3},... | collective-permute-start | bytes 1572872 | tf_op jit(solution)/shard_map/ppermute | solution.py:162
  362.2 16.4 %collective-permute-start.49 = (bf16[512,512]{1,0:T(8,128)(2,1)S(1)}, bf16[512,512]{1,0:T(8,128)(2,1)S(1)}, u32[]{:S(2)}, u32[]{:S(2)}) collective-permute-start(bf16[512,512]{1,0:T(8,128)(2,1)S(1)} %pad_maximum_fusion.15), channel_id=1, source_target_pairs={{0,2},{2,6},{6,10},{10,14},{14,12},{12,8},{8,4},{4,0},{1,3},{3,7},... | collective-permute-start | bytes 1572872 | tf_op jit(solution)/shard_map/ppermute | solution.py:161
  378.7 19.4 %collective-permute-start.54 = (bf16[512,512]{1,0:T(8,128)(2,1)S(1)}, bf16[512,512]{1,0:T(8,128)(2,1)S(1)}, u32[]{:S(2)}, u32[]{:S(2)}) collective-permute-start(bf16[512,512]{1,0:T(8,128)(2,1)S(1)} %add.355), channel_id=1, source_target_pairs={{2,0},{6,2},{10,6},{14,10},{12,14},{8,12},{4,8},{0,4},{3,1},{7,3},... | collective-permute-start | bytes 1572872 | tf_op jit(solution)/shard_map/ppermute | solution.py:162
  379.6 18.5 %collective-permute-start.53 = (bf16[512,512]{1,0:T(8,128)(2,1)S(1)}, bf16[512,512]{1,0:T(8,128)(2,1)S(1)}, u32[]{:S(2)}, u32[]{:S(2)}) collective-permute-start(bf16[512,512]{1,0:T(8,128)(2,1)S(1)} %add.354), channel_id=1, source_target_pairs={{0,2},{2,6},{6,10},{10,14},{14,12},{12,8},{8,4},{4,0},{1,3},{3,7},... | collective-permute-start | bytes 1572872 | tf_op jit(solution)/shard_map/ppermute | solution.py:161
  394.6 41.1 %collective-permute-start.52 = (bf16[384,1024]{1,0:T(8,128)(2,1)S(1)}, bf16[384,1024]{1,0:T(8,128)(2,1)S(1)}, u32[]{:S(2)}, u32[]{:S(2)}) collective-permute-start(bf16[384,1024]{1,0:T(8,128)(2,1)S(1)} %add.353), channel_id=1, source_target_pairs={{2,0},{6,2},{10,6},{14,10},{12,14},{8,12},{4,8},{0,4},{3,1},{7,3},... | collective-permute-start | bytes 2359304 | tf_op jit(solution)/shard_map/ppermute | solution.py:162
  395.7 40.7 %collective-permute-start.51 = (bf16[384,1024]{1,0:T(8,128)(2,1)S(1)}, bf16[384,1024]{1,0:T(8,128)(2,1)S(1)}, u32[]{:S(2)}, u32[]{:S(2)}) collective-permute-start(bf16[384,1024]{1,0:T(8,128)(2,1)S(1)} %add.352), channel_id=1, source_target_pairs={{0,2},{2,6},{6,10},{10,14},{14,12},{12,8},{8,4},{4,0},{1,3},{3,7},... | collective-permute-start | bytes 2359304 | tf_op jit(solution)/shard_map/ppermute | solution.py:161
  398.3 25.5 %collective-permute-start.56 = (bf16[512,512]{1,0:T(8,128)(2,1)S(1)}, bf16[512,512]{1,0:T(8,128)(2,1)S(1)}, u32[]{:S(2)}, u32[]{:S(2)}) collective-permute-start(bf16[512,512]{1,0:T(8,128)(2,1)S(1)} %add.357), channel_id=1, source_target_pairs={{2,0},{6,2},{10,6},{14,10},{12,14},{8,12},{4,8},{0,4},{3,1},{7,3},... | collective-permute-start | bytes 1572872 | tf_op jit(solution)/shard_map/ppermute | solution.py:162
  399.2 25.6 %collective-permute-start.55 = (bf16[512,512]{1,0:T(8,128)(2,1)S(1)}, bf16[512,512]{1,0:T(8,128)(2,1)S(1)}, u32[]{:S(2)}, u32[]{:S(2)}) collective-permute-start(bf16[512,512]{1,0:T(8,128)(2,1)S(1)} %add.356), channel_id=1, source_target_pairs={{0,2},{2,6},{6,10},{10,14},{14,12},{12,8},{8,4},{4,0},{1,3},{3,7},... | collective-permute-start | bytes 1572872 | tf_op jit(solution)/shard_map/ppermute | solution.py:161
  435.8 17.8 %collective-permute-start.65 = (bf16[256,1024]{1,0:T(8,128)(2,1)}, bf16[256,1024]{1,0:T(8,128)(2,1)}, u32[]{:S(2)}, u32[]{:S(2)}) collective-permute-start(bf16[256,1024]{1,0:T(8,128)(2,1)} %get-tuple-element.444), channel_id=1, source_target_pairs={{0,16},{16,0},{1,17},{17,1},{2,18},{18,2},{3,19},{19,3},{4,20},{20... | collective-permute-start | bytes 1572872 | tf_op jit(solution)/shard_map/ppermute | solution.py:1174
  436.4 12.4 %collective-permute-start.62 = (bf16[384,1024]{1,0:T(8,128)(2,1)S(1)}, bf16[384,1024]{1,0:T(8,128)(2,1)}, u32[]{:S(2)}, u32[]{:S(2)}) collective-permute-start(bf16[384,1024]{1,0:T(8,128)(2,1)S(1)} %slice.449), channel_id=1, source_target_pairs={{0,1},{1,0},{2,3},{3,2},{4,5},{5,4},{6,7},{7,6},{8,9},{9,8},{10,11... | collective-permute-start | bytes 2359304 | tf_op jit(solution)/shard_map/ppermute | solution.py:77
  457.4 81.4 %all-gather.9.cloned.1.call-start = ((), (), s32[]{:S(2)}) async-start(), calls=%async_computation.2 | async-start | bytes 3145728 | tf_op jit(solution)/shard_map/all_gather | solution.py:1330
  484.5 21.2 %collective-permute-start.70 = (bf16[384,1024]{1,0:T(8,128)(2,1)}, bf16[384,1024]{1,0:T(8,128)(2,1)}, u32[]{:S(2)}, u32[]{:S(2)}) collective-permute-start(bf16[384,1024]{1,0:T(8,128)(2,1)} %add.385), channel_id=1, source_target_pairs={{0,2},{2,6},{6,10},{10,14},{14,12},{12,8},{8,4},{4,0},{1,3},{3,7},... | collective-permute-start | bytes 2359304 | tf_op jit(solution)/shard_map/ppermute | solution.py:161
  487.4 19.0 %collective-permute-start.71 = (bf16[384,1024]{1,0:T(8,128)(2,1)}, bf16[384,1024]{1,0:T(8,128)(2,1)}, u32[]{:S(2)}, u32[]{:S(2)}) collective-permute-start(bf16[384,1024]{1,0:T(8,128)(2,1)} %add.387), channel_id=1, source_target_pairs={{2,0},{6,2},{10,6},{14,10},{12,14},{8,12},{4,8},{0,4},{3,1},{7,3},... | collective-permute-start | bytes 2359304 | tf_op jit(solution)/shard_map/ppermute | solution.py:162
  519.4 23.5 %collective-permute-start.82 = (bf16[224,1024]{1,0:T(8,128)(2,1)S(1)}, bf16[224,1024]{1,0:T(8,128)(2,1)}, u32[]{:S(2)}, u32[]{:S(2)}) collective-permute-start(bf16[224,1024]{1,0:T(8,128)(2,1)S(1)} %collective-permute-done.75.refs_0_), channel_id=1, source_target_pairs={{0,1},{1,0},{2,3},{3,2},{4,5},{5,4},{6,7},{7,6},{8,9},{9,8},{10,11... | collective-permute-start | bytes 1376264 | tf_op jit(solution)/shard_map/ppermute | solution.py:77
  519.4 24.0 %collective-permute-start.83 = (bf16[224,1024]{1,0:T(8,128)(2,1)}, bf16[224,1024]{1,0:T(8,128)(2,1)}, u32[]{:S(2)}, u32[]{:S(2)}) collective-permute-start(bf16[224,1024]{1,0:T(8,128)(2,1)} %collective-permute-done.76.refs_1_), channel_id=1, source_target_pairs={{0,1},{1,0},{2,3},{3,2},{4,5},{5,4},{6,7},{7,6},{8,9},{9,8},{10,11... | collective-permute-start | bytes 1376264 | tf_op jit(solution)/shard_map/ppermute | solution.py:77
  528.7 21.0 %collective-permute-start.80 = (bf16[224,1024]{1,0:T(8,128)(2,1)}, bf16[224,1024]{1,0:T(8,128)(2,1)S(1)}, u32[]{:S(2)}, u32[]{:S(2)}) collective-permute-start(bf16[224,1024]{1,0:T(8,128)(2,1)} %collective-permute-done.77.refs_0_), channel_id=1, source_target_pairs={{0,2},{2,6},{6,10},{10,14},{14,12},{12,8},{8,4},{4,0},{1,3},{3,7},... | collective-permute-start | bytes 1376264 | tf_op jit(solution)/shard_map/ppermute | solution.py:139
  530.2 19.6 %collective-permute-start.81 = (bf16[224,1024]{1,0:T(8,128)(2,1)}, bf16[224,1024]{1,0:T(8,128)(2,1)S(1)}, u32[]{:S(2)}, u32[]{:S(2)}) collective-permute-start(bf16[224,1024]{1,0:T(8,128)(2,1)} %collective-permute-done.78.refs_1_), channel_id=1, source_target_pairs={{2,0},{6,2},{10,6},{14,10},{12,14},{8,12},{4,8},{0,4},{3,1},{7,3},... | collective-permute-start | bytes 1376264 | tf_op jit(solution)/shard_map/ppermute | solution.py:140
  542.9 13.6 %collective-permute-start.89 = (bf16[224,1024]{1,0:T(8,128)(2,1)}, bf16[224,1024]{1,0:T(8,128)(2,1)}, u32[]{:S(2)}, u32[]{:S(2)}) collective-permute-start(bf16[224,1024]{1,0:T(8,128)(2,1)} %collective-permute-done.77.refs_0_), channel_id=1, source_target_pairs={{0,1},{1,0},{2,3},{3,2},{4,5},{5,4},{6,7},{7,6},{8,9},{9,8},{10,11... | collective-permute-start | bytes 1376264 | tf_op jit(solution)/shard_map/ppermute | solution.py:77
  542.9 14.1 %collective-permute-start.90 = (bf16[224,1024]{1,0:T(8,128)(2,1)}, bf16[224,1024]{1,0:T(8,128)(2,1)S(1)}, u32[]{:S(2)}, u32[]{:S(2)}) collective-permute-start(bf16[224,1024]{1,0:T(8,128)(2,1)} %collective-permute-done.78.refs_1_), channel_id=1, source_target_pairs={{0,1},{1,0},{2,3},{3,2},{4,5},{5,4},{6,7},{7,6},{8,9},{9,8},{10,11... | collective-permute-start | bytes 1376264 | tf_op jit(solution)/shard_map/ppermute | solution.py:77
  550.6 13.5 %collective-permute-start.85 = (bf16[112,1024]{1,0:T(8,128)(2,1)}, bf16[112,1024]{1,0:T(8,128)(2,1)}, u32[]{:S(2)}, u32[]{:S(2)}) collective-permute-start(bf16[112,1024]{1,0:T(8,128)(2,1)} %slice.348), channel_id=1, source_target_pairs={{0,2},{2,6},{6,10},{10,14},{14,12},{12,8},{8,4},{4,0},{1,3},{3,7},... | collective-permute-start | bytes 688136 | tf_op jit(solution)/shard_map/ppermute | solution.py:144
  556.5 13.7 %collective-permute-start.87 = (bf16[224,1024]{1,0:T(8,128)(2,1)S(1)}, bf16[224,1024]{1,0:T(8,128)(2,1)S(1)}, u32[]{:S(2)}, u32[]{:S(2)}) collective-permute-start(bf16[224,1024]{1,0:T(8,128)(2,1)S(1)} %collective-permute-done.80.refs_0_), channel_id=1, source_target_pairs={{0,1},{1,0},{2,3},{3,2},{4,5},{5,4},{6,7},{7,6},{8,9},{9,8},{10,11... | collective-permute-start | bytes 1376264 | tf_op jit(solution)/shard_map/ppermute | solution.py:77
  556.5 13.7 %collective-permute-start.88 = (bf16[224,1024]{1,0:T(8,128)(2,1)S(1)}, bf16[224,1024]{1,0:T(8,128)(2,1)S(1)}, u32[]{:S(2)}, u32[]{:S(2)}) collective-permute-start(bf16[224,1024]{1,0:T(8,128)(2,1)S(1)} %collective-permute-done.81.refs_1_), channel_id=1, source_target_pairs={{0,1},{1,0},{2,3},{3,2},{4,5},{5,4},{6,7},{7,6},{8,9},{9,8},{10,11... | collective-permute-start | bytes 1376264 | tf_op jit(solution)/shard_map/ppermute | solution.py:77
  565.0 12.3 %collective-permute-start.86 = (bf16[224,1024]{1,0:T(8,128)(2,1)S(1)}, bf16[224,1024]{1,0:T(8,128)(2,1)S(1)}, u32[]{:S(2)}, u32[]{:S(2)}) collective-permute-start(bf16[224,1024]{1,0:T(8,128)(2,1)S(1)} %constant_dynamic-update-slice_fusion.4.refs_0_), channel_id=1, source_target_pairs={{0,1},{1,0},{2,3},{3,2},{4,5},{5,4},{6,7},{7,6},{8,9},{9,8},{10,11... | collective-permute-start | bytes 1376264 | tf_op jit(solution)/shard_map/ppermute | solution.py:77
  (181 other events, 2422.3 us)
Sparse Core Ops, SparseCore 0:
  53.6 44.6 all-gather.4
  100.5 21.3 all-gather.6
  457.5 21.4 all-gather.10
  480.4 38.2 all-gather.8

commit v3 on v2

--- a/solution.py
+++ b/solution.py
@@ -1030,6 +1030,14 @@
 
     scale_attn = lax.rsqrt(jnp.mean(tok_float * tok_float, axis=-1, keepdims=True) + norm_eps)
     attn_in = (tok_float * scale_attn * gain_attn).astype(bf16)
+    cot_ring = RingGather(ring, cotangent)
+    cot_ring.step()
+    attn_in = after(attn_in, cot_ring.ends())
+    cot_ring.step()
+    attn_other = swap(attn_in)
+    qkv_shards = after(qkv_shards, cot_ring.ends())
+    while cot_ring.place < ring.half - 1:
+        cot_ring.step()
     within = jnp.arange(PROMPT_DEV, dtype=jnp.int32)
     prompt_pos = member_pair[:, None] * PROMPT_DEV + within
     cont_pos = jnp.broadcast_to(prompt_len + within, (2, CLEN))
@@ -1042,46 +1050,39 @@
     cosine_part, sine_part = jnp.cos(angles), jnp.sin(angles)
     cosine = jnp.concatenate([cosine_part] * 4, axis=1)
     sine_signed = jnp.concatenate([-sine_part, sine_part] * 2, axis=1)
-    cot_ring = RingGather(ring, cotangent)
-    cot_ring.step()
-    attn_in = after(attn_in, cot_ring.ends())
-    cot_ring.step()
+    rows2 = 2 * tok_count
+    queries, prompt_kv, cont_kv = project(
+        meta, attn_in, attn_other, qkv_shards, cosine, sine_signed
+    )
+    prompt_kv = prompt_kv.reshape(2 * PROMPT_ROWS, 2 * k_width)
+    prompt_kv = after(prompt_kv, cot_ring.ends())
     half_rows = out_weight.shape[0] // 2
     late_gate_up, late_down, late_out = after(
-        (gate_up_weight[0], down_weight[0], out_weight), cot_ring.ends()
+        (gate_up_weight[0], down_weight[0], out_weight), prompt_kv
     )
     out_core = pick_core(late_out[:half_rows], late_out[half_rows:]).astype(bf16)
     own_gate_up = lax.all_gather(late_gate_up.astype(bf16), "dp", axis=0, tiled=True)
     own_down = lax.all_gather(late_down.astype(bf16), "dp", axis=0, tiled=True)
     expert_weights = [own_gate_up, swap(own_gate_up), own_down, swap(own_down)]
-    attn_other = swap(attn_in)
     attn_in2 = jnp.concatenate([attn_in, attn_other], axis=0)
-    qkv_shards = after(qkv_shards, cot_ring.ends())
-    while cot_ring.place < ring.half - 1:
-        cot_ring.step()
-    rows2 = 2 * tok_count
-    queries, prompt_kv, cont_kv = project(
-        meta, attn_in, attn_other, qkv_shards, cosine, sine_signed
-    )
-    prompt_kv = prompt_kv.reshape(2 * PROMPT_ROWS, 2 * k_width)
-    prompt_kv = after(prompt_kv, cot_ring.ends())
-    proj_out = gather_dp(after(out_core, qkv_shards), 0)
-    small_state = [
-        jnp.concatenate([a[None], f[None], r.T], axis=0)
-        for a, f, r in (
-            (attn_gain, ffn_gain, router_weight),
-            (mean_attn_gain, mean_ffn_gain, mean_router_weight),
-            (square_attn_gain, square_ffn_gain, square_router_weight),
-        )
-    ]
-    small_state = gather_dp(after(jnp.stack(small_state), prompt_kv), 2)
+    proj_qkv = join_dp(after(qkv_shards, prompt_kv), 0)
+    proj_out = gather_dp(after(out_core, prompt_kv), 0)
     kv_blocks, state = {}, None
     for arrived in ring.gather_steps(prompt_kv):
         kv_blocks.update(arrived)
         if 2 in arrived:
-            proj_qkv = join_dp(after(qkv_shards, state), 0)
+            state, proj_qkv = after((state, proj_qkv))
+            small_state = [
+                jnp.concatenate([a[None], f[None], r.T], axis=0)
+                for a, f, r in (
+                    (attn_gain, ffn_gain, router_weight),
+                    (mean_attn_gain, mean_ffn_gain, mean_router_weight),
+                    (square_attn_gain, square_ffn_gain, square_router_weight),
+                )
+            ]
+            small_state = gather_dp(after(jnp.stack(small_state), state), 2)
         if ring.half in arrived:
-            state, proj_qkv = after((state, proj_qkv))
+            state, small_state = after((state, small_state))
         state = attend(
             meta,
             queries,
@@ -1292,12 +1293,12 @@
     output = hidden + mix_sum.finish(mix_parts[0])
     dense_new = None
     dense_ring = RingGather(ring, carried)
-    arrived, first_place, earlier = dict(dense_ring.blocks), 0, ()
+    arrived, first_place, earlier = dict(dense_ring.blocks), 0, [(), ()]
     while arrived:
         later = {}
         if dense_ring.place < ring.half:
-            later = dense_ring.step(*earlier)
-        earlier = tuple(dense_new or ())
+            later = dense_ring.step(*earlier.pop(0))
+        earlier.append(tuple(dense_new or ()))
         dense_new = optimize(
             meta,
             first_place,
@@ -1311,6 +1312,8 @@
             grad_scale,
         )
         first_place += len(arrived)
+        if ring.half - 2 in arrived:
+            dense_most = dense_new
         arrived = later
     dense_new = [a.reshape(-1, a.shape[-1]) for a in dense_new]
 
@@ -1329,6 +1332,7 @@
 
     step_gate_up = lax.all_gather(gate_up_new[0].astype(bf16), "dp", axis=1, tiled=True)
     step_down = lax.all_gather(down_new[0].astype(bf16), "dp", axis=1, tiled=True)
+    step_gate_up, step_down = after((step_gate_up, step_down), dense_most)
     return (
         merge_rows(output.astype(bf16)),
         input_grad,

time: 600 us -> 597 us (level)
  waiting for transfers between devices: 155 us -> 143 us
  starting transfers between devices: 79.6 us -> 86.1 us
    ppermute x5, waiting for transfers between devices: 21.4 us -> 9.58 us  [dp_shards(): pieces.append(lax.ppermute(values, 'dp', perm))]
    ppermute x12, waiting for transfers between devices: 52.9 us -> 60.6 us  [step(): self.ahead = lax.ppermute(self.ahead, 'chip', ring.forward)]
    unnamed x297 -> x279, local copies, waits for them, and re-layouts: 18.4 us -> 18.5 us
  transfers between devices with their start and end apart: 95 -> 95, of which waited for: 42 -> 39; matrix products, arithmetic and copies ran while one was open for 19% -> 20% of each run, Pallas kernels for 30% -> 30%
where the time goes in v3:
time: 597 us; the launch traced here: 587 us
  Pallas kernels  197 us (33%)
  waiting for transfers between devices  143 us (24%)
  starting transfers between devices  86.1 us (14%)
  other arithmetic  62.4 us (10%)
  matrix products  43.2 us (7%)
  local copies, waits for them, and re-layouts  39 us (7%)
  between operations  16.8 us (3%)
    pallas_call x5, Pallas kernels, attend_back(): pl.pallas_call(functools.partial(attend_back_kernel, first_block, blocks,...  62.1 us
    ppermute x12, waiting for transfers between devices, step(): self.ahead = lax.ppermute(self.ahead, 'chip', ring.forward)  60.6 us
    pallas_call x5, Pallas kernels, run_experts(): pl.pallas_call(functools.partial(expert_kernel, count, tok, spill), grid_...  54.3 us
    pallas_call x5, Pallas kernels, attend(): pl.pallas_call(functools.partial(attend_kernel, first_block, blocks, firs...  41.7 us
    ppermute x16, waiting for transfers between devices, send(): self.behind = lax.ppermute(self.sent[1], 'chip', self.ring.backward)  40 us
    dot_general x7, matrix products, dot_tn(): lax.dot_general(left, right, (((0,), (0,)), ((), ())), preferred_element_...  37.3 us
    pallas_call x5, Pallas kernels, optimize(): pl.pallas_call(functools.partial(optimizer_kernel, blocks, dp_size, grad_...  28.3 us
    ppermute x16, starting transfers between devices, send(): self.ahead = lax.ppermute(self.sent[0], 'chip', self.ring.forward)  23.9 us
  transfers between devices with their start and end apart: 95, of which 39 were waited for; matrix products, arithmetic and copies ran while one was open for 20% of the time, Pallas kernels for 30%

profile of v3, /device:TPU:0, one launch (start us, length us, event | category | flops | bytes accessed | tf_op | source)
XLA Modules:
  0.0 587.2 jit_solution(15227249125763850037)
XLA Ops:
  10.5 2.9 collective-permute-start.2
  13.5 2.0 collective-permute-start.1
  15.6 2.2 copy-done
  21.6 9.4 %collective-permute-done.2.refs_2_ = bf16[384,1024]{1,0:T(8,128)(2,1)S(1)} collective-permute-done((bf16[384,1024]{1,0:T(8,128)(2,1)S(1)}, bf16[384,1024]{1,0:T(8,128)(2,1)S(1)}, u32[]{:S(2)}, u32[]{:S(2)}) %collective-permute-start.2) | collective-permute-done | bytes 786464 | tf_op jit(solution)/shard_map/ppermute | solution.py:139
  34.9 15.0 %collective-permute-done.6.refs_2_ = bf16[384,1024]{1,0:T(8,128)(2,1)} collective-permute-done((bf16[384,1024]{1,0:T(8,128)(2,1)S(1)}, bf16[384,1024]{1,0:T(8,128)(2,1)}, u32[]{:S(2)}, u32[]{:S(2)}) %collective-permute-start.6) | collective-permute-done | bytes 786464 | tf_op jit(solution)/shard_map/ppermute | solution.py:139
  60.0 4.8 project.1
  74.5 2.4 select_convert_fusion
  82.9 7.2 %attend.5 = (f32[6,2,128,512]{3,2,1,0:T(8,128)S(1)}, f32[6,2,8,512]{3,2,1,0:T(8,128)S(1)}) custom-call(s32[16]{0:T(128)S(1)} %concatenate.109.meta_ref, bf16[768,512]{1,0:T(8,128)(2,1)S(1)} %copy-done.43, bf16[512,512]{1,0:T(8,128)(2,1)S(1)} %bitcast.152, bf16[2,128,512]{2,1,0:T(8,128)(2,1)S(1)} %copy-done.47), custom_call_target="tpu_custom_call" | custom-call | flops 4831838208 | bytes 12582912 | tf_op jit(solution)/shard_map/attend/pallas_call | solution.py:488
  90.1 9.8 %attend.6 = (f32[6,2,128,512]{3,2,1,0:T(8,128)S(1)}, f32[6,2,8,512]{3,2,1,0:T(8,128)S(1)}) custom-call(s32[16]{0:T(128)S(1)} %concatenate.109.meta_ref, bf16[768,512]{1,0:T(8,128)(2,1)S(1)} %copy-done.43, bf16[512,512]{1,0:T(8,128)(2,1)S(1)} %collective-permute-done.10.refs_0_, bf16[512,512]{1,0:T(8,128)(2,1)} %collective-permute-done.14.refs_1_, ...), custom_call_target="tpu_custom_call" | custom-call | flops 9663676416 | bytes 12582912 | tf_op jit(solution)/shard_map/attend/pallas_call | solution.py:488
  103.8 4.6 collective-permute-done.18
  114.1 8.7 %attend.7 = (f32[6,2,128,512]{3,2,1,0:T(8,128)S(1)}, f32[6,2,8,512]{3,2,1,0:T(8,128)S(1)}) custom-call(s32[16]{0:T(128)S(1)} %concatenate.109.meta_ref, bf16[768,512]{1,0:T(8,128)(2,1)S(1)} %copy-done.44, bf16[512,512]{1,0:T(8,128)(2,1)S(1)} %collective-permute-done.11.refs_0_, bf16[512,512]{1,0:T(8,128)(2,1)S(1)} %collective-permute-done.15.refs_1_, ...), custom_call_target="tpu_custom_call" | custom-call | flops 9663676416 | bytes 12582912 | tf_op jit(solution)/shard_map/attend/pallas_call | solution.py:488
  126.0 8.7 %attend.8 = (f32[6,2,128,512]{3,2,1,0:T(8,128)S(1)}, f32[6,2,8,512]{3,2,1,0:T(8,128)S(1)}) custom-call(s32[16]{0:T(128)S(1)} %concatenate.109.meta_ref, bf16[768,512]{1,0:T(8,128)(2,1)S(1)} %copy-done.44, bf16[512,512]{1,0:T(8,128)(2,1)S(1)} %collective-permute-done.12.refs_0_, bf16[512,512]{1,0:T(8,128)(2,1)S(1)} %collective-permute-done.16.refs_1_, ...), custom_call_target="tpu_custom_call" | custom-call | flops 9663676416 | bytes 12582912 | tf_op jit(solution)/shard_map/attend/pallas_call | solution.py:488
  134.9 7.3 %attend.9 = (f32[768,512]{1,0:T(8,128)S(1)}, bf16[768,512]{1,0:T(8,128)(2,1)S(1)}, f32[8,768]{1,0:T(8,128)S(1)}) custom-call(s32[16]{0:T(128)S(1)} %concatenate.109.meta_ref, bf16[768,512]{1,0:T(8,128)(2,1)S(1)} %copy-done.44, bf16[512,512]{1,0:T(8,128)(2,1)S(1)} %constant_dynamic-update-slice_fusion.refs_0_, ...), custom_call_target="tpu_custom_call" | custom-call | flops 4831838208 | bytes 12582912 | tf_op jit(solution)/shard_map/attend/pallas_call | solution.py:488
  148.1 2.2 multiply_reduce_fusion.2
  154.2 6.1 %experts.5 = (bf16[384,1024]{1,0:T(8,128)(2,1)S(1)}, bf16[400,1024]{1,0:T(8,128)(2,1)S(1)}, bf16[3072,1024]{1,0:T(8,128)(2,1)}, bf16[3072,1024]{1,0:T(8,128)(2,1...) custom-call(s32[16]{0:T(128)S(1)} %concatenate.109.meta_ref, bf16[400,1024]{1,0:T(8,128)(2,1)S(1)} %pad_maximum_fusion.3.refs_0_, ...), custom_call_target="tpu_custom_call" | custom-call | flops 4831838208 | bytes 14155776 | tf_op jit(solution)/shard_map/experts/pallas_call | solution.py:942
  160.3 12.3 %collective-permute-done.23.refs_0_ = bf16[400,1024]{1,0:T(8,128)(2,1)S(1)} collective-permute-done((bf16[400,1024]{1,0:T(8,128)(2,1)S(1)}, bf16[400,1024]{1,0:T(8,128)(2,1)S(1)}, u32[]{:S(2)}, u32[]{:S(2)}) %collective-permute-start.23) | collective-permute-done | bytes 819232 | tf_op jit(solution)/shard_map/ppermute | solution.py:139
  176.2 14.4 %experts.6 = (bf16[384,1024]{1,0:T(8,128)(2,1)S(1)}, bf16[384,1024]{1,0:T(8,128)(2,1)S(1)}, bf16[400,1024]{1,0:T(8,128)(2,1)S(1)}, bf16[400,1024]{1,0:T(8,128)(2...) custom-call(s32[16]{0:T(128)S(1)} %concatenate.109.meta_ref, ...), custom_call_target="tpu_custom_call", output_to_operand_aliasing={{4}: (9, {}), {5}: (10, {}), {6}: (11, {}), {7}: (12, {})} | custom-call | flops 9663676416 | bytes 22020096 | tf_op jit(solution)/shard_map/experts/pallas_call | solution.py:942
  196.8 14.5 %experts.7 = (bf16[384,1024]{1,0:T(8,128)(2,1)S(1)}, bf16[384,1024]{1,0:T(8,128)(2,1)S(1)}, bf16[400,1024]{1,0:T(8,128)(2,1)S(1)}, bf16[400,1024]{1,0:T(8,128)(2...) custom-call(s32[16]{0:T(128)S(1)} %concatenate.109.meta_ref, ...), custom_call_target="tpu_custom_call", output_to_operand_aliasing={{4}: (9, {}), {5}: (10, {}), {6}: (11, {}), {7}: (12, {})} | custom-call | flops 9663676416 | bytes 22020096 | tf_op jit(solution)/shard_map/experts/pallas_call | solution.py:942
  218.5 13.5 %experts.8 = (bf16[384,1024]{1,0:T(8,128)(2,1)S(1)}, bf16[384,1024]{1,0:T(8,128)(2,1)S(1)}, bf16[400,1024]{1,0:T(8,128)(2,1)S(1)}, bf16[400,1024]{1,0:T(8,128)(2...) custom-call(s32[16]{0:T(128)S(1)} %concatenate.109.meta_ref, ...), custom_call_target="tpu_custom_call", output_to_operand_aliasing={{4}: (9, {}), {5}: (10, {}), {6}: (11, {}), {7}: (12, {})} | custom-call | flops 9663676416 | bytes 22020096 | tf_op jit(solution)/shard_map/experts/pallas_call | solution.py:942
  232.2 5.8 experts.9
  240.3 9.0 %collective-permute-done.33 = bf16[192,1024]{1,0:T(8,128)(2,1)S(1)} collective-permute-done((bf16[192,1024]{1,0:T(8,128)(2,1)S(1)}, bf16[192,1024]{1,0:T(8,128)(2,1)S(1)}, u32[]{:S(2)}, u32[]{:S(2)}) %collective-permute-start.33) | collective-permute-done | bytes 393248 | tf_op jit(solution)/shard_map/ppermute | solution.py:161
  251.7 9.0 %fusion.15 = bf16[1024,1024]{1,0:T(8,128)(2,1)S(1)} fusion(bf16[3072,1024]{1,0:T(8,128)(2,1)S(1)} %copy-done.51, bf16[3072,2048]{1,0:T(8,128)(2,1)} %get-tuple-element.315), kind=kOutput, calls=%fused_computation.25 | convolution fusion | flops 6443499520 | bytes 14680064 | tf_op jit(solution)/shard_map/dot_general | solution.py:40
  260.7 7.3 %fusion.29 = bf16[512,1024]{1,0:T(8,128)(2,1)S(1)} fusion(bf16[3072,1024]{1,0:T(8,128)(2,1)} %get-tuple-element.317, bf16[3072,1024]{1,0:T(8,128)(2,1)} %get-tuple-element.316), kind=kOutput, calls=%fused_computation.52 | convolution fusion | flops 3221749760 | bytes 10485760 | tf_op jit(solution)/shard_map/dot_general | solution.py:40
  271.3 18.2 %collective-permute-done.38 = bf16[400,1024]{1,0:T(8,128)(2,1)S(1)} collective-permute-done((bf16[400,1024]{1,0:T(8,128)(2,1)S(1)}, bf16[400,1024]{1,0:T(8,128)(2,1)S(1)}, u32[]{:S(2)}, u32[]{:S(2)}) %collective-permute-start.38) | collective-permute-done | bytes 819232 | tf_op jit(solution)/shard_map/ppermute | solution.py:162
  291.2 1.9 collective-permute-start.41
  293.1 9.2 %add_convert_fusion = bf16[1024,1024]{1,0:T(8,128)(2,1)} fusion(bf16[1024,1024]{1,0:T(8,128)(2,1)} %copy-done.132, bf16[3072,1024]{1,0:T(8,128)(2,1)S(1)} %copy-done.51, bf16[3072,2048]{1,0:T(8,128)(2,1)S(1)} %bitcast.155), kind=kOutput, calls=%fused_computation.4 | convolution fusion | flops 6445596672 | bytes 16777216 | tf_op jit(solution)/shard_map/dot_general | solution.py:40
  302.3 6.3 %add_convert_fusion.1 = bf16[512,1024]{1,0:T(8,128)(2,1)} fusion(bf16[512,1024]{1,0:T(8,128)(2,1)S(1)} %collective-permute-done.40, bf16[3072,1024]{1,0:T(8,128)(2,1)S(1)} %bitcast.158, bf16[3072,1024]{1,0:T(8,128)(2,1)} %get-tuple-element.316), kind=kOutput, calls=%fused_computation.24 | convolution fusion | flops 3222798336 | bytes 11534336 | tf_op jit(solution)/shard_map/dot_general | solution.py:40
  316.3 5.6 collective-permute-done.43
  323.8 2.2 collective-permute-done.45
  328.4 7.7 %attend_back.5 = (bf16[512,512]{1,0:T(8,128)(2,1)S(1)}, f32[6,2,128,512]{3,2,1,0:T(8,128)S(1)}) custom-call(s32[16]{0:T(128)S(1)} %concatenate.109.meta_ref, bf16[768,512]{1,0:T(8,128)(2,1)S(1)} %copy-done.45, bf16[768,512]{1,0:T(8,128)(2,1)S(1)} %convolution_convert_fusion.2.do_ref, f32[768,512]{1,0:T(8,128)S(1)} %copy-done.50, ...), custom_call_target="tpu_custom_call" | custom-call | flops 11072962560 | bytes 16777216 | tf_op jit(solution)/shard_map/attend_back/pallas_call | solution.py:538
  340.9 13.3 %attend_back.6 = (bf16[512,512]{1,0:T(8,128)(2,1)S(1)}, bf16[512,512]{1,0:T(8,128)(2,1)S(1)}, f32[6,2,128,512]{3,2,1,0:T(8,128)S(1)}) custom-call(s32[16]{0:T(128)S(1)} %concatenate.109.meta_ref, bf16[768,512]{1,0:T(8,128)(2,1)S(1)} %copy-done.45, bf16[768,512]{1,0:T(8,128)(2,1)S(1)} %convolution_convert_fusion.2.do_ref, f32[768,512]{1,0:T(8,128)S(1)} %copy-done.50, ...), custom_call_target="tpu_custom_call" | custom-call | flops 22145925120 | bytes 16777216 | tf_op jit(solution)/shard_map/attend_back/pallas_call | solution.py:538
  355.4 2.2 collective-permute-start.62
  361.0 13.3 %attend_back.7 = (bf16[512,512]{1,0:T(8,128)(2,1)S(1)}, bf16[512,512]{1,0:T(8,128)(2,1)S(1)}, f32[6,2,128,512]{3,2,1,0:T(8,128)S(1)}) custom-call(s32[16]{0:T(128)S(1)} %concatenate.109.meta_ref, bf16[768,512]{1,0:T(8,128)(2,1)S(1)} %copy-done.45, bf16[768,512]{1,0:T(8,128)(2,1)S(1)} %convolution_convert_fusion.2.do_ref, f32[768,512]{1,0:T(8,128)S(1)} %copy-done.50, ...), custom_call_target="tpu_custom_call" | custom-call | flops 22145925120 | bytes 16777216 | tf_op jit(solution)/shard_map/attend_back/pallas_call | solution.py:538
  376.7 14.4 %attend_back.8 = (bf16[512,512]{1,0:T(8,128)(2,1)S(1)}, bf16[512,512]{1,0:T(8,128)(2,1)S(1)}, f32[6,2,128,512]{3,2,1,0:T(8,128)S(1)}) custom-call(s32[16]{0:T(128)S(1)} %concatenate.109.meta_ref, bf16[768,512]{1,0:T(8,128)(2,1)S(1)} %copy-done.45, bf16[768,512]{1,0:T(8,128)(2,1)S(1)} %convolution_convert_fusion.2.do_ref, f32[768,512]{1,0:T(8,128)S(1)} %copy-done.50, ...), custom_call_target="tpu_custom_call" | custom-call | flops 22145925120 | bytes 16777216 | tf_op jit(solution)/shard_map/attend_back/pallas_call | solution.py:538
  396.1 1.8 collective-permute-start.56
  397.9 13.5 %attend_back.9 = (bf16[512,512]{1,0:T(8,128)(2,1)S(1)}, bf16[768,512]{1,0:T(8,128)(2,1)S(1)}, f32[2,128,512]{2,1,0:T(8,128)S(1)}) custom-call(s32[16]{0:T(128)S(1)} %concatenate.109.meta_ref, bf16[768,512]{1,0:T(8,128)(2,1)S(1)} %copy-done.45, bf16[768,512]{1,0:T(8,128)(2,1)S(1)} %convolution_convert_fusion.2.do_ref, f32[768,512]{1,0:T(8,128)S(1)} %copy-done.50, ...), custom_call_target="tpu_custom_call" | custom-call | flops 11072962560 | bytes 16777216 | tf_op jit(solution)/shard_map/attend_back/pallas_call | solution.py:538
  411.4 8.8 %collective-permute-done.57 = bf16[512,512]{1,0:T(8,128)(2,1)S(1)} collective-permute-done((bf16[512,512]{1,0:T(8,128)(2,1)S(1)}, bf16[512,512]{1,0:T(8,128)(2,1)S(1)}, u32[]{:S(2)}, u32[]{:S(2)}) %collective-permute-start.57) | collective-permute-done | bytes 524320 | tf_op jit(solution)/shard_map/ppermute | solution.py:162
  422.2 3.2 convolution_convert_fusion
  427.1 1.8 fusion.86
  432.3 2.3 collective-permute-start.66
  438.2 4.7 fusion.14
  442.8 3.5 collective-permute-done.61
  447.5 2.1 add.371
  449.6 1.9 add.370
  451.6 3.7 fusion.35
  458.9 2.5 fusion.20
  461.5 4.6 collective-permute-done.65
  472.2 2.1 collective-permute-start.70
  474.3 3.4 collective-permute-done.70
  480.2 1.8 collective-permute-start.73
  487.4 3.3 shard_step.1
  492.1 2.2 fusion.23
  497.2 4.9 collective-permute-done.74
  502.2 2.2 collective-permute-done.72
  506.4 8.4 %collective-permute-done.75.refs_0_ = bf16[224,1024]{1,0:T(8,128)(2,1)} collective-permute-done((bf16[224,1024]{1,0:T(8,128)(2,1)S(1)}, bf16[224,1024]{1,0:T(8,128)(2,1)}, u32[]{:S(2)}, u32[]{:S(2)}) %collective-permute-start.75) | collective-permute-done | bytes 458784 | tf_op jit(solution)/shard_map/ppermute | solution.py:139
  516.9 8.7 %collective-permute-done.77.refs_0_ = bf16[224,1024]{1,0:T(8,128)(2,1)} collective-permute-done((bf16[224,1024]{1,0:T(8,128)(2,1)}, bf16[224,1024]{1,0:T(8,128)(2,1)}, u32[]{:S(2)}, u32[]{:S(2)}) %collective-permute-start.77) | collective-permute-done | bytes 458784 | tf_op jit(solution)/shard_map/ppermute | solution.py:139
  528.9 4.9 optimize.5
  535.4 1.8 collective-permute-start.83
  537.2 1.9 add_convert_fusion.2
  542.3 6.2 %optimize.6 = (f32[2,512,2048]{2,1,0:T(8,128)}, f32[512,2048]{1,0:T(8,128)}, f32[512,2048]{1,0:T(8,128)}, f32[2,2,256,1024]{3,2,1,0:T(8,128)}, f32[2,256,1024]{2,1,0:T(8,128)}, /*index=5*/f32[2,256,1024]{2,1,0:T(8,128)}) custom-call(s32[16]{0:T(128)} %copy-done.33, ...), custom_call_target="tpu_custom_call", output_to_operand_aliasing={{0}: (11, {}), {1}: (12, {}), {2}: (13, {}), {3}: (14, {}),... | custom-call | flops 7864320 | bytes 11796480 | tf_op jit(solution)/shard_map/optimize/pallas_call | solution.py:847
  549.3 6.2 %optimize.7 = (f32[2,512,2048]{2,1,0:T(8,128)}, f32[512,2048]{1,0:T(8,128)}, f32[512,2048]{1,0:T(8,128)}, f32[2,2,256,1024]{3,2,1,0:T(8,128)}, f32[2,256,1024]{2,1,0:T(8,128)}, /*index=5*/f32[2,256,1024]{2,1,0:T(8,128)}) custom-call(s32[16]{0:T(128)} %copy-done.33, ...), custom_call_target="tpu_custom_call", output_to_operand_aliasing={{0}: (11, {}), {1}: (12, {}), {2}: (13, {}), {3}: (14, {}),... | custom-call | flops 7864320 | bytes 11796480 | tf_op jit(solution)/shard_map/optimize/pallas_call | solution.py:847
  555.6 4.2 convert_element_type.236
  568.7 6.2 %optimize.8 = (f32[2,512,2048]{2,1,0:T(8,128)}, f32[512,2048]{1,0:T(8,128)}, f32[512,2048]{1,0:T(8,128)}, f32[2,2,256,1024]{3,2,1,0:T(8,128)}, f32[2,256,1024]{2,1,0:T(8,128)}, /*index=5*/f32[2,256,1024]{2,1,0:T(8,128)}) custom-call(s32[16]{0:T(128)} %copy-done.33, ...), custom_call_target="tpu_custom_call", output_to_operand_aliasing={{0}: (11, {}), {1}: (12, {}), {2}: (13, {}), {3}: (14, {}),... | custom-call | flops 7864320 | bytes 11796480 | tf_op jit(solution)/shard_map/optimize/pallas_call | solution.py:847
  575.7 4.8 optimize.9
  (595 shorter events, 169.2 us)
Async XLA Ops:
  7.2 138.6 %all-gather.5.cloned.1.call-start = ((), (), s32[]{:S(2)}) async-start(), calls=%async_computation | async-start | bytes 3145728 | tf_op jit(solution)/shard_map/all_gather | solution.py:1064
  10.5 20.6 %collective-permute-start.2 = (bf16[384,1024]{1,0:T(8,128)(2,1)S(1)}, bf16[384,1024]{1,0:T(8,128)(2,1)S(1)}, u32[]{:S(2)}, u32[]{:S(2)}) collective-permute-start(bf16[384,1024]{1,0:T(8,128)(2,1)S(1)} %pad_maximum_fusion.8.refs_1_), channel_id=1, source_target_pairs={{0,2},{2,6},{6,10},{10,14},{14,12},{12,8},{8,4},{4,0},{1,3},{3,7},... | collective-permute-start | bytes 2359304 | tf_op jit(solution)/shard_map/ppermute | solution.py:139
  13.4 19.3 %collective-permute-start.3 = (bf16[384,1024]{1,0:T(8,128)(2,1)S(1)}, bf16[384,1024]{1,0:T(8,128)(2,1)}, u32[]{:S(2)}, u32[]{:S(2)}) collective-permute-start(bf16[384,1024]{1,0:T(8,128)(2,1)S(1)} %pad_maximum_fusion.8.refs_1_), channel_id=1, source_target_pairs={{2,0},{6,2},{10,6},{14,10},{12,14},{8,12},{4,8},{0,4},{3,1},{7,3},... | collective-permute-start | bytes 2359304 | tf_op jit(solution)/shard_map/ppermute | solution.py:140
  13.5 20.2 %collective-permute-start.1 = (bf16[18,512]{1,0:T(8,128)(2,1)S(1)}, bf16[18,512]{1,0:T(8,128)(2,1)S(1)}, u32[]{:S(2)}, u32[]{:S(2)}) collective-permute-start(bf16[18,512]{1,0:T(8,128)(2,1)S(1)} %fusion.53), channel_id=1, source_target_pairs={{0,16},{16,0},{1,17},{17,1},{2,18},{18,2},{3,19},{19,3},{4,20},{20... | collective-permute-start | bytes 55304 | tf_op jit(solution)/shard_map/ppermute | solution.py:205
  15.6 42.0 %collective-permute-start = (s32[1]{0:T(128)}, s32[1]{0:T(128)}, u32[]{:S(2)}, u32[]{:S(2)}) collective-permute-start(s32[1]{0:T(128)} %param.31), channel_id=1, source_target_pairs={{0,1},{1,0},{2,3},{3,2},{4,5},{5,4},{6,7},{7,6},{8,9},{9,8},{10,11... | collective-permute-start | bytes 20 | tf_op jit(solution)/shard_map/ppermute | solution.py:77
  18.0 41.0 %collective-permute-start.5 = (bf16[512,1024]{1,0:T(8,128)(2,1)S(1)}, bf16[512,1024]{1,0:T(8,128)(2,1)}, u32[]{:S(2)}, u32[]{:S(2)}) collective-permute-start(bf16[512,1024]{1,0:T(8,128)(2,1)S(1)} %cast_core_columns.1.refs_0_), channel_id=1, source_target_pairs={{0,16},{16,0},{1,17},{17,1},{2,18},{18,2},{3,19},{19,3},{4,20},{20... | collective-permute-start | bytes 3145736 | tf_op jit(solution)/shard_map/ppermute | solution.py:205
  31.0 18.9 %collective-permute-start.6 = (bf16[384,1024]{1,0:T(8,128)(2,1)S(1)}, bf16[384,1024]{1,0:T(8,128)(2,1)}, u32[]{:S(2)}, u32[]{:S(2)}) collective-permute-start(bf16[384,1024]{1,0:T(8,128)(2,1)S(1)} %collective-permute-done.2.refs_2_), channel_id=1, source_target_pairs={{0,2},{2,6},{6,10},{10,14},{14,12},{12,8},{8,4},{4,0},{1,3},{3,7},... | collective-permute-start | bytes 2359304 | tf_op jit(solution)/shard_map/ppermute | solution.py:139
  32.7 18.6 %collective-permute-start.7 = (bf16[384,1024]{1,0:T(8,128)(2,1)}, bf16[384,1024]{1,0:T(8,128)(2,1)}, u32[]{:S(2)}, u32[]{:S(2)}) collective-permute-start(bf16[384,1024]{1,0:T(8,128)(2,1)} %collective-permute-done.3.refs_3_), channel_id=1, source_target_pairs={{2,0},{6,2},{10,6},{14,10},{12,14},{8,12},{4,8},{0,4},{3,1},{7,3},... | collective-permute-start | bytes 2359304 | tf_op jit(solution)/shard_map/ppermute | solution.py:140
  34.9 24.1 %collective-permute-start.4 = (bf16[384,1024]{1,0:T(8,128)(2,1)}, bf16[384,1024]{1,0:T(8,128)(2,1)}, u32[]{:S(2)}, u32[]{:S(2)}) collective-permute-start(bf16[384,1024]{1,0:T(8,128)(2,1)} %fusion.18.own_ref), channel_id=1, source_target_pairs={{0,1},{1,0},{2,3},{3,2},{4,5},{5,4},{6,7},{7,6},{8,9},{9,8},{10,11... | collective-permute-start | bytes 2359304 | tf_op jit(solution)/shard_map/ppermute | solution.py:77
  50.0 18.1 %collective-permute-start.8 = (bf16[384,1024]{1,0:T(8,128)(2,1)}, bf16[384,1024]{1,0:T(8,128)(2,1)S(1)}, u32[]{:S(2)}, u32[]{:S(2)}) collective-permute-start(bf16[384,1024]{1,0:T(8,128)(2,1)} %collective-permute-done.6.refs_2_), channel_id=1, source_target_pairs={{0,2},{2,6},{6,10},{10,14},{14,12},{12,8},{8,4},{4,0},{1,3},{3,7},... | collective-permute-start | bytes 2359304 | tf_op jit(solution)/shard_map/ppermute | solution.py:139
  51.3 17.5 %collective-permute-start.9 = (bf16[384,1024]{1,0:T(8,128)(2,1)}, bf16[384,1024]{1,0:T(8,128)(2,1)S(1)}, u32[]{:S(2)}, u32[]{:S(2)}) collective-permute-start(bf16[384,1024]{1,0:T(8,128)(2,1)} %collective-permute-done.7.refs_3_), channel_id=1, source_target_pairs={{2,0},{6,2},{10,6},{14,10},{12,14},{8,12},{4,8},{0,4},{3,1},{7,3},... | collective-permute-start | bytes 2359304 | tf_op jit(solution)/shard_map/ppermute | solution.py:140
  70.1 76.3 %all-gather.7.cloned.1.call-start = ((), (), s32[]{:S(2)}) async-start(), calls=%async_computation.1 | async-start | bytes 1572864 | tf_op jit(solution)/shard_map/all_gather | solution.py:1065
  72.5 17.6 %collective-permute-start.10 = (bf16[512,512]{1,0:T(8,128)(2,1)S(1)}, bf16[512,512]{1,0:T(8,128)(2,1)S(1)}, u32[]{:S(2)}, u32[]{:S(2)}) collective-permute-start(bf16[512,512]{1,0:T(8,128)(2,1)S(1)} %bitcast.150), channel_id=1, source_target_pairs={{0,2},{2,6},{6,10},{10,14},{14,12},{12,8},{8,4},{4,0},{1,3},{3,7},... | collective-permute-start | bytes 1572872 | tf_op jit(solution)/shard_map/ppermute | solution.py:139
  74.0 16.0 %collective-permute-start.14 = (bf16[512,512]{1,0:T(8,128)(2,1)S(1)}, bf16[512,512]{1,0:T(8,128)(2,1)}, u32[]{:S(2)}, u32[]{:S(2)}) collective-permute-start(bf16[512,512]{1,0:T(8,128)(2,1)S(1)} %bitcast.151), channel_id=1, source_target_pairs={{2,0},{6,2},{10,6},{14,10},{12,14},{8,12},{4,8},{0,4},{3,1},{7,3},... | collective-permute-start | bytes 1572872 | tf_op jit(solution)/shard_map/ppermute | solution.py:140
  76.9 25.6 %collective-permute-start.19 = (bf16[256,1024]{1,0:T(8,128)(2,1)}, bf16[256,1024]{1,0:T(8,128)(2,1)}, u32[]{:S(2)}, u32[]{:S(2)}) collective-permute-start(bf16[256,1024]{1,0:T(8,128)(2,1)} %select_convert_fusion), channel_id=1, source_target_pairs={{0,16},{16,0},{1,17},{17,1},{2,18},{18,2},{3,19},{19,3},{4,20},{20... | collective-permute-start | bytes 1572872 | tf_op jit(solution)/shard_map/ppermute | solution.py:205
  82.4 473.2 %all-gather.11.cloned.1.call-start = ((), (), s32[]{:S(2)}) async-start(), calls=%async_computation.3 | async-start | bytes 1572864 | tf_op jit(solution)/shard_map/all_gather | solution.py:1334
  100.5 11.4 %collective-permute-start.11 = (bf16[512,512]{1,0:T(8,128)(2,1)S(1)}, bf16[512,512]{1,0:T(8,128)(2,1)S(1)}, u32[]{:S(2)}, u32[]{:S(2)}) collective-permute-start(bf16[512,512]{1,0:T(8,128)(2,1)S(1)} %collective-permute-done.10.refs_0_), channel_id=1, source_target_pairs={{0,2},{2,6},{6,10},{10,14},{14,12},{12,8},{8,4},{4,0},{1,3},{3,7},... | collective-permute-start | bytes 1572872 | tf_op jit(solution)/shard_map/ppermute | solution.py:139
  111.9 11.9 %collective-permute-start.12 = (bf16[512,512]{1,0:T(8,128)(2,1)S(1)}, bf16[512,512]{1,0:T(8,128)(2,1)S(1)}, u32[]{:S(2)}, u32[]{:S(2)}) collective-permute-start(bf16[512,512]{1,0:T(8,128)(2,1)S(1)} %collective-permute-done.11.refs_0_), channel_id=1, source_target_pairs={{0,2},{2,6},{6,10},{10,14},{14,12},{12,8},{8,4},{4,0},{1,3},{3,7},... | collective-permute-start | bytes 1572872 | tf_op jit(solution)/shard_map/ppermute | solution.py:139
  113.5 12.0 %collective-permute-start.16 = (bf16[512,512]{1,0:T(8,128)(2,1)S(1)}, bf16[512,512]{1,0:T(8,128)(2,1)S(1)}, u32[]{:S(2)}, u32[]{:S(2)}) collective-permute-start(bf16[512,512]{1,0:T(8,128)(2,1)S(1)} %collective-permute-done.15.refs_1_), channel_id=1, source_target_pairs={{2,0},{6,2},{10,6},{14,10},{12,14},{8,12},{4,8},{0,4},{3,1},{7,3},... | collective-permute-start | bytes 1572872 | tf_op jit(solution)/shard_map/ppermute | solution.py:140
  152.1 20.5 %collective-permute-start.23 = (bf16[400,1024]{1,0:T(8,128)(2,1)S(1)}, bf16[400,1024]{1,0:T(8,128)(2,1)S(1)}, u32[]{:S(2)}, u32[]{:S(2)}) collective-permute-start(bf16[400,1024]{1,0:T(8,128)(2,1)S(1)} %pad_maximum_fusion.3.refs_0_), channel_id=1, source_target_pairs={{0,2},{2,6},{6,10},{10,14},{14,12},{12,8},{8,4},{4,0},{1,3},{3,7},... | collective-permute-start | bytes 2457608 | tf_op jit(solution)/shard_map/ppermute | solution.py:139
  153.8 20.0 %collective-permute-start.24 = (bf16[400,1024]{1,0:T(8,128)(2,1)S(1)}, bf16[400,1024]{1,0:T(8,128)(2,1)S(1)}, u32[]{:S(2)}, u32[]{:S(2)}) collective-permute-start(bf16[400,1024]{1,0:T(8,128)(2,1)S(1)} %pad_maximum_fusion.3.refs_0_), channel_id=1, source_target_pairs={{2,0},{6,2},{10,6},{14,10},{12,14},{8,12},{4,8},{0,4},{3,1},{7,3},... | collective-permute-start | bytes 2457608 | tf_op jit(solution)/shard_map/ppermute | solution.py:140
  173.8 19.1 %collective-permute-start.25 = (bf16[400,1024]{1,0:T(8,128)(2,1)S(1)}, bf16[400,1024]{1,0:T(8,128)(2,1)S(1)}, u32[]{:S(2)}, u32[]{:S(2)}) collective-permute-start(bf16[400,1024]{1,0:T(8,128)(2,1)S(1)} %collective-permute-done.23.refs_0_), channel_id=1, source_target_pairs={{0,2},{2,6},{6,10},{10,14},{14,12},{12,8},{8,4},{4,0},{1,3},{3,7},... | collective-permute-start | bytes 2457608 | tf_op jit(solution)/shard_map/ppermute | solution.py:139
  175.4 19.2 %collective-permute-start.26 = (bf16[400,1024]{1,0:T(8,128)(2,1)S(1)}, bf16[400,1024]{1,0:T(8,128)(2,1)S(1)}, u32[]{:S(2)}, u32[]{:S(2)}) collective-permute-start(bf16[400,1024]{1,0:T(8,128)(2,1)S(1)} %collective-permute-done.24.refs_1_), channel_id=1, source_target_pairs={{2,0},{6,2},{10,6},{14,10},{12,14},{8,12},{4,8},{0,4},{3,1},{7,3},... | collective-permute-start | bytes 2457608 | tf_op jit(solution)/shard_map/ppermute | solution.py:140
  194.6 17.9 %collective-permute-start.27 = (bf16[400,1024]{1,0:T(8,128)(2,1)S(1)}, bf16[400,1024]{1,0:T(8,128)(2,1)S(1)}, u32[]{:S(2)}, u32[]{:S(2)}) collective-permute-start(bf16[400,1024]{1,0:T(8,128)(2,1)S(1)} %collective-permute-done.25.refs_0_), channel_id=1, source_target_pairs={{0,2},{2,6},{6,10},{10,14},{14,12},{12,8},{8,4},{4,0},{1,3},{3,7},... | collective-permute-start | bytes 2457608 | tf_op jit(solution)/shard_map/ppermute | solution.py:139
  196.1 17.8 %collective-permute-start.28 = (bf16[400,1024]{1,0:T(8,128)(2,1)S(1)}, bf16[400,1024]{1,0:T(8,128)(2,1)S(1)}, u32[]{:S(2)}, u32[]{:S(2)}) collective-permute-start(bf16[400,1024]{1,0:T(8,128)(2,1)S(1)} %collective-permute-done.26.refs_1_), channel_id=1, source_target_pairs={{2,0},{6,2},{10,6},{14,10},{12,14},{8,12},{4,8},{0,4},{3,1},{7,3},... | collective-permute-start | bytes 2457608 | tf_op jit(solution)/shard_map/ppermute | solution.py:140
  214.1 18.0 %collective-permute-start.31 = (bf16[192,1024]{1,0:T(8,128)(2,1)S(1)}, bf16[192,1024]{1,0:T(8,128)(2,1)S(1)}, u32[]{:S(2)}, u32[]{:S(2)}) collective-permute-start(bf16[192,1024]{1,0:T(8,128)(2,1)S(1)} %slice.290), channel_id=1, source_target_pairs={{0,2},{2,6},{6,10},{10,14},{14,12},{12,8},{8,4},{4,0},{1,3},{3,7},... | collective-permute-start | bytes 1179656 | tf_op jit(solution)/shard_map/ppermute | solution.py:144
  214.9 17.1 %collective-permute-start.32 = (bf16[192,1024]{1,0:T(8,128)(2,1)S(1)}, bf16[192,1024]{1,0:T(8,128)(2,1)S(1)}, u32[]{:S(2)}, u32[]{:S(2)}) collective-permute-start(bf16[192,1024]{1,0:T(8,128)(2,1)S(1)} %slice.291), channel_id=1, source_target_pairs={{2,0},{6,2},{10,6},{14,10},{12,14},{8,12},{4,8},{0,4},{3,1},{7,3},... | collective-permute-start | bytes 1179656 | tf_op jit(solution)/shard_map/ppermute | solution.py:145
  216.2 15.9 %collective-permute-start.30 = (bf16[208,1024]{1,0:T(8,128)(2,1)S(1)}, bf16[208,1024]{1,0:T(8,128)(2,1)S(1)}, u32[]{:S(2)}, u32[]{:S(2)}) collective-permute-start(bf16[208,1024]{1,0:T(8,128)(2,1)S(1)} %slice.289), channel_id=1, source_target_pairs={{2,0},{6,2},{10,6},{14,10},{12,14},{8,12},{4,8},{0,4},{3,1},{7,3},... | collective-permute-start | bytes 1277960 | tf_op jit(solution)/shard_map/ppermute | solution.py:145
  216.7 15.4 %collective-permute-start.29 = (bf16[192,1024]{1,0:T(8,128)(2,1)S(1)}, bf16[192,1024]{1,0:T(8,128)(2,1)S(1)}, u32[]{:S(2)}, u32[]{:S(2)}) collective-permute-start(bf16[192,1024]{1,0:T(8,128)(2,1)S(1)} %slice.288), channel_id=1, source_target_pairs={{0,2},{2,6},{6,10},{10,14},{14,12},{12,8},{8,4},{4,0},{1,3},{3,7},... | collective-permute-start | bytes 1179656 | tf_op jit(solution)/shard_map/ppermute | solution.py:144
  249.5 18.5 %collective-permute-start.36 = (bf16[400,1024]{1,0:T(8,128)(2,1)S(1)}, bf16[400,1024]{1,0:T(8,128)(2,1)S(1)}, u32[]{:S(2)}, u32[]{:S(2)}) collective-permute-start(bf16[400,1024]{1,0:T(8,128)(2,1)S(1)} %pad_maximum_fusion.6), channel_id=1, source_target_pairs={{2,0},{6,2},{10,6},{14,10},{12,14},{8,12},{4,8},{0,4},{3,1},{7,3},... | collective-permute-start | bytes 2457608 | tf_op jit(solution)/shard_map/ppermute | solution.py:162
  250.0 18.1 %collective-permute-start.35 = (bf16[400,1024]{1,0:T(8,128)(2,1)S(1)}, bf16[400,1024]{1,0:T(8,128)(2,1)S(1)}, u32[]{:S(2)}, u32[]{:S(2)}) collective-permute-start(bf16[400,1024]{1,0:T(8,128)(2,1)S(1)} %pad_maximum_fusion.5), channel_id=1, source_target_pairs={{0,2},{2,6},{6,10},{10,14},{14,12},{12,8},{8,4},{4,0},{1,3},{3,7},... | collective-permute-start | bytes 2457608 | tf_op jit(solution)/shard_map/ppermute | solution.py:161
  268.7 20.9 %collective-permute-start.39 = (bf16[1024,1024]{1,0:T(8,128)(2,1)S(1)}, bf16[1024,1024]{1,0:T(8,128)(2,1)S(1)}, u32[]{:S(2)}, u32[]{:S(2)}) collective-permute-start(bf16[1024,1024]{1,0:T(8,128)(2,1)S(1)} %fusion.15), channel_id=1, source_target_pairs={{0,1},{1,0},{2,3},{3,2},{4,5},{5,4},{6,7},{7,6},{8,9},{9,8},{10,11... | collective-permute-start | bytes 6291464 | tf_op jit(solution)/shard_map/ppermute | solution.py:77
  268.8 20.8 %collective-permute-start.40 = (bf16[512,1024]{1,0:T(8,128)(2,1)S(1)}, bf16[512,1024]{1,0:T(8,128)(2,1)S(1)}, u32[]{:S(2)}, u32[]{:S(2)}) collective-permute-start(bf16[512,1024]{1,0:T(8,128)(2,1)S(1)} %fusion.29), channel_id=1, source_target_pairs={{0,1},{1,0},{2,3},{3,2},{4,5},{5,4},{6,7},{7,6},{8,9},{9,8},{10,11... | collective-permute-start | bytes 3145736 | tf_op jit(solution)/shard_map/ppermute | solution.py:77
  269.3 20.2 %collective-permute-start.38 = (bf16[400,1024]{1,0:T(8,128)(2,1)S(1)}, bf16[400,1024]{1,0:T(8,128)(2,1)S(1)}, u32[]{:S(2)}, u32[]{:S(2)}) collective-permute-start(bf16[400,1024]{1,0:T(8,128)(2,1)S(1)} %add.338), channel_id=1, source_target_pairs={{2,0},{6,2},{10,6},{14,10},{12,14},{8,12},{4,8},{0,4},{3,1},{7,3},... | collective-permute-start | bytes 2457608 | tf_op jit(solution)/shard_map/ppermute | solution.py:162
  269.6 19.9 %collective-permute-start.37 = (bf16[400,1024]{1,0:T(8,128)(2,1)S(1)}, bf16[400,1024]{1,0:T(8,128)(2,1)S(1)}, u32[]{:S(2)}, u32[]{:S(2)}) collective-permute-start(bf16[400,1024]{1,0:T(8,128)(2,1)S(1)} %add.337), channel_id=1, source_target_pairs={{0,2},{2,6},{6,10},{10,14},{14,12},{12,8},{8,4},{4,0},{1,3},{3,7},... | collective-permute-start | bytes 2457608 | tf_op jit(solution)/shard_map/ppermute | solution.py:161
  289.9 19.4 %collective-permute-start.42 = (bf16[400,1024]{1,0:T(8,128)(2,1)S(1)}, bf16[400,1024]{1,0:T(8,128)(2,1)S(1)}, u32[]{:S(2)}, u32[]{:S(2)}) collective-permute-start(bf16[400,1024]{1,0:T(8,128)(2,1)S(1)} %add.340), channel_id=1, source_target_pairs={{2,0},{6,2},{10,6},{14,10},{12,14},{8,12},{4,8},{0,4},{3,1},{7,3},... | collective-permute-start | bytes 2457608 | tf_op jit(solution)/shard_map/ppermute | solution.py:162
  291.2 19.5 %collective-permute-start.41 = (bf16[400,1024]{1,0:T(8,128)(2,1)S(1)}, bf16[400,1024]{1,0:T(8,128)(2,1)S(1)}, u32[]{:S(2)}, u32[]{:S(2)}) collective-permute-start(bf16[400,1024]{1,0:T(8,128)(2,1)S(1)} %add.339), channel_id=1, source_target_pairs={{0,2},{2,6},{6,10},{10,14},{14,12},{12,8},{8,4},{4,0},{1,3},{3,7},... | collective-permute-start | bytes 2457608 | tf_op jit(solution)/shard_map/ppermute | solution.py:161
  336.2 22.4 %collective-permute-start.48 = (bf16[256,512]{1,0:T(8,128)(2,1)S(1)}, bf16[256,512]{1,0:T(8,128)(2,1)S(1)}, u32[]{:S(2)}, u32[]{:S(2)}) collective-permute-start(bf16[256,512]{1,0:T(8,128)(2,1)S(1)} %get-tuple-element.465), channel_id=1, source_target_pairs={{0,2},{2,6},{6,10},{10,14},{14,12},{12,8},{8,4},{4,0},{1,3},{3,7},... | collective-permute-start | bytes 786440 | tf_op jit(solution)/shard_map/ppermute | solution.py:161
  337.6 21.0 %collective-permute-start.49 = (bf16[256,512]{1,0:T(8,128)(2,1)S(1)}, bf16[256,512]{1,0:T(8,128)(2,1)S(1)}, u32[]{:S(2)}, u32[]{:S(2)}) collective-permute-start(bf16[256,512]{1,0:T(8,128)(2,1)S(1)} %get-tuple-element.464), channel_id=1, source_target_pairs={{2,0},{6,2},{10,6},{14,10},{12,14},{8,12},{4,8},{0,4},{3,1},{7,3},... | collective-permute-start | bytes 786440 | tf_op jit(solution)/shard_map/ppermute | solution.py:162
  338.5 52.7 %collective-permute-start.47 = (bf16[384,1024]{1,0:T(8,128)(2,1)S(1)}, bf16[384,1024]{1,0:T(8,128)(2,1)S(1)}, u32[]{:S(2)}, u32[]{:S(2)}) collective-permute-start(bf16[384,1024]{1,0:T(8,128)(2,1)S(1)} %pad_maximum_fusion.11), channel_id=1, source_target_pairs={{2,0},{6,2},{10,6},{14,10},{12,14},{8,12},{4,8},{0,4},{3,1},{7,3},... | collective-permute-start | bytes 2359304 | tf_op jit(solution)/shard_map/ppermute | solution.py:162
  339.4 51.8 %collective-permute-start.46 = (bf16[384,1024]{1,0:T(8,128)(2,1)S(1)}, bf16[384,1024]{1,0:T(8,128)(2,1)S(1)}, u32[]{:S(2)}, u32[]{:S(2)}) collective-permute-start(bf16[384,1024]{1,0:T(8,128)(2,1)S(1)} %pad_maximum_fusion.10), channel_id=1, source_target_pairs={{0,2},{2,6},{6,10},{10,14},{14,12},{12,8},{8,4},{4,0},{1,3},{3,7},... | collective-permute-start | bytes 2359304 | tf_op jit(solution)/shard_map/ppermute | solution.py:161
  355.4 82.7 %collective-permute-start.62 = (bf16[512,1024]{1,0:T(8,128)(2,1)}, bf16[512,1024]{1,0:T(8,128)(2,1)}, u32[]{:S(2)}, u32[]{:S(2)}) collective-permute-start(bf16[512,1024]{1,0:T(8,128)(2,1)} %get-tuple-element.446), channel_id=1, source_target_pairs={{0,16},{16,0},{1,17},{17,1},{2,18},{18,2},{3,19},{19,3},{4,20},{20... | collective-permute-start | bytes 3145736 | tf_op jit(solution)/shard_map/ppermute | solution.py:1175
  358.8 15.5 %collective-permute-start.51 = (bf16[512,512]{1,0:T(8,128)(2,1)S(1)}, bf16[512,512]{1,0:T(8,128)(2,1)S(1)}, u32[]{:S(2)}, u32[]{:S(2)}) collective-permute-start(bf16[512,512]{1,0:T(8,128)(2,1)S(1)} %pad_maximum_fusion.16), channel_id=1, source_target_pairs={{2,0},{6,2},{10,6},{14,10},{12,14},{8,12},{4,8},{0,4},{3,1},{7,3},... | collective-permute-start | bytes 1572872 | tf_op jit(solution)/shard_map/ppermute | solution.py:162
  359.7 14.7 %collective-permute-start.50 = (bf16[512,512]{1,0:T(8,128)(2,1)S(1)}, bf16[512,512]{1,0:T(8,128)(2,1)S(1)}, u32[]{:S(2)}, u32[]{:S(2)}) collective-permute-start(bf16[512,512]{1,0:T(8,128)(2,1)S(1)} %pad_maximum_fusion.15), channel_id=1, source_target_pairs={{0,2},{2,6},{6,10},{10,14},{14,12},{12,8},{8,4},{4,0},{1,3},{3,7},... | collective-permute-start | bytes 1572872 | tf_op jit(solution)/shard_map/ppermute | solution.py:161
  374.5 20.6 %collective-permute-start.55 = (bf16[512,512]{1,0:T(8,128)(2,1)S(1)}, bf16[512,512]{1,0:T(8,128)(2,1)S(1)}, u32[]{:S(2)}, u32[]{:S(2)}) collective-permute-start(bf16[512,512]{1,0:T(8,128)(2,1)S(1)} %add.355), channel_id=1, source_target_pairs={{2,0},{6,2},{10,6},{14,10},{12,14},{8,12},{4,8},{0,4},{3,1},{7,3},... | collective-permute-start | bytes 1572872 | tf_op jit(solution)/shard_map/ppermute | solution.py:162
  375.4 19.7 %collective-permute-start.54 = (bf16[512,512]{1,0:T(8,128)(2,1)S(1)}, bf16[512,512]{1,0:T(8,128)(2,1)S(1)}, u32[]{:S(2)}, u32[]{:S(2)}) collective-permute-start(bf16[512,512]{1,0:T(8,128)(2,1)S(1)} %add.354), channel_id=1, source_target_pairs={{0,2},{2,6},{6,10},{10,14},{14,12},{12,8},{8,4},{4,0},{1,3},{3,7},... | collective-permute-start | bytes 1572872 | tf_op jit(solution)/shard_map/ppermute | solution.py:161
  391.5 40.8 %collective-permute-start.53 = (bf16[384,1024]{1,0:T(8,128)(2,1)S(1)}, bf16[384,1024]{1,0:T(8,128)(2,1)S(1)}, u32[]{:S(2)}, u32[]{:S(2)}) collective-permute-start(bf16[384,1024]{1,0:T(8,128)(2,1)S(1)} %add.353), channel_id=1, source_target_pairs={{2,0},{6,2},{10,6},{14,10},{12,14},{8,12},{4,8},{0,4},{3,1},{7,3},... | collective-permute-start | bytes 2359304 | tf_op jit(solution)/shard_map/ppermute | solution.py:162
  392.6 42.0 %collective-permute-start.52 = (bf16[384,1024]{1,0:T(8,128)(2,1)S(1)}, bf16[384,1024]{1,0:T(8,128)(2,1)S(1)}, u32[]{:S(2)}, u32[]{:S(2)}) collective-permute-start(bf16[384,1024]{1,0:T(8,128)(2,1)S(1)} %add.352), channel_id=1, source_target_pairs={{0,2},{2,6},{6,10},{10,14},{14,12},{12,8},{8,4},{4,0},{1,3},{3,7},... | collective-permute-start | bytes 2359304 | tf_op jit(solution)/shard_map/ppermute | solution.py:161
  395.2 25.0 %collective-permute-start.57 = (bf16[512,512]{1,0:T(8,128)(2,1)S(1)}, bf16[512,512]{1,0:T(8,128)(2,1)S(1)}, u32[]{:S(2)}, u32[]{:S(2)}) collective-permute-start(bf16[512,512]{1,0:T(8,128)(2,1)S(1)} %add.357), channel_id=1, source_target_pairs={{2,0},{6,2},{10,6},{14,10},{12,14},{8,12},{4,8},{0,4},{3,1},{7,3},... | collective-permute-start | bytes 1572872 | tf_op jit(solution)/shard_map/ppermute | solution.py:162
  396.1 25.2 %collective-permute-start.56 = (bf16[512,512]{1,0:T(8,128)(2,1)S(1)}, bf16[512,512]{1,0:T(8,128)(2,1)S(1)}, u32[]{:S(2)}, u32[]{:S(2)}) collective-permute-start(bf16[512,512]{1,0:T(8,128)(2,1)S(1)} %add.356), channel_id=1, source_target_pairs={{0,2},{2,6},{6,10},{10,14},{14,12},{12,8},{8,4},{4,0},{1,3},{3,7},... | collective-permute-start | bytes 1572872 | tf_op jit(solution)/shard_map/ppermute | solution.py:161
  432.3 19.2 %collective-permute-start.66 = (bf16[256,1024]{1,0:T(8,128)(2,1)}, bf16[256,1024]{1,0:T(8,128)(2,1)}, u32[]{:S(2)}, u32[]{:S(2)}) collective-permute-start(bf16[256,1024]{1,0:T(8,128)(2,1)} %get-tuple-element.450), channel_id=1, source_target_pairs={{0,16},{16,0},{1,17},{17,1},{2,18},{18,2},{3,19},{19,3},{4,20},{20... | collective-permute-start | bytes 1572872 | tf_op jit(solution)/shard_map/ppermute | solution.py:1175
  434.6 12.1 %collective-permute-start.63 = (bf16[384,1024]{1,0:T(8,128)(2,1)S(1)}, bf16[384,1024]{1,0:T(8,128)(2,1)}, u32[]{:S(2)}, u32[]{:S(2)}) collective-permute-start(bf16[384,1024]{1,0:T(8,128)(2,1)S(1)} %slice.449), channel_id=1, source_target_pairs={{0,1},{1,0},{2,3},{3,2},{4,5},{5,4},{6,7},{7,6},{8,9},{9,8},{10,11... | collective-permute-start | bytes 2359304 | tf_op jit(solution)/shard_map/ppermute | solution.py:77
  455.3 100.3 %all-gather.9.cloned.1.call-start = ((), (), s32[]{:S(2)}) async-start(), calls=%async_computation.2 | async-start | bytes 3145728 | tf_op jit(solution)/shard_map/all_gather | solution.py:1333
  467.2 11.5 %collective-permute-start.67 = (bf16[192,1024]{1,0:T(8,128)(2,1)}, bf16[192,1024]{1,0:T(8,128)(2,1)}, u32[]{:S(2)}, u32[]{:S(2)}) collective-permute-start(bf16[192,1024]{1,0:T(8,128)(2,1)} %add.379), channel_id=1, source_target_pairs={{0,2},{2,6},{6,10},{10,14},{14,12},{12,8},{8,4},{4,0},{1,3},{3,7},... | collective-permute-start | bytes 1179656 | tf_op jit(solution)/shard_map/ppermute | solution.py:161
  483.2 19.0 %collective-permute-start.71 = (bf16[384,1024]{1,0:T(8,128)(2,1)}, bf16[384,1024]{1,0:T(8,128)(2,1)}, u32[]{:S(2)}, u32[]{:S(2)}) collective-permute-start(bf16[384,1024]{1,0:T(8,128)(2,1)} %add.385), channel_id=1, source_target_pairs={{0,2},{2,6},{6,10},{10,14},{14,12},{12,8},{8,4},{4,0},{1,3},{3,7},... | collective-permute-start | bytes 2359304 | tf_op jit(solution)/shard_map/ppermute | solution.py:161
  485.9 18.5 %collective-permute-start.72 = (bf16[384,1024]{1,0:T(8,128)(2,1)}, bf16[384,1024]{1,0:T(8,128)(2,1)}, u32[]{:S(2)}, u32[]{:S(2)}) collective-permute-start(bf16[384,1024]{1,0:T(8,128)(2,1)} %add.387), channel_id=1, source_target_pairs={{2,0},{6,2},{10,6},{14,10},{12,14},{8,12},{4,8},{0,4},{3,1},{7,3},... | collective-permute-start | bytes 2359304 | tf_op jit(solution)/shard_map/ppermute | solution.py:162
  490.7 11.5 %collective-permute-start.74 = (bf16[96,1024]{1,0:T(8,128)(2,1)}, bf16[96,1024]{1,0:T(8,128)(2,1)S(1)}, u32[]{:S(2)}, u32[]{:S(2)}) collective-permute-start(bf16[96,1024]{1,0:T(8,128)(2,1)} %shard_step.1), channel_id=1, source_target_pairs={{0,16},{16,0},{1,17},{17,1},{2,18},{18,2},{3,19},{19,3},{4,20},{20... | collective-permute-start | bytes 589832 | tf_op jit(solution)/shard_map/ppermute | solution.py:205
  527.6 13.3 %collective-permute-start.89 = (bf16[224,1024]{1,0:T(8,128)(2,1)}, bf16[224,1024]{1,0:T(8,128)(2,1)}, u32[]{:S(2)}, u32[]{:S(2)}) collective-permute-start(bf16[224,1024]{1,0:T(8,128)(2,1)} %collective-permute-done.75.refs_0_), channel_id=1, source_target_pairs={{0,1},{1,0},{2,3},{3,2},{4,5},{5,4},{6,7},{7,6},{8,9},{9,8},{10,11... | collective-permute-start | bytes 1376264 | tf_op jit(solution)/shard_map/ppermute | solution.py:77
  527.6 14.7 %collective-permute-start.90 = (bf16[224,1024]{1,0:T(8,128)(2,1)}, bf16[224,1024]{1,0:T(8,128)(2,1)}, u32[]{:S(2)}, u32[]{:S(2)}) collective-permute-start(bf16[224,1024]{1,0:T(8,128)(2,1)} %collective-permute-done.76.refs_1_), channel_id=1, source_target_pairs={{0,1},{1,0},{2,3},{3,2},{4,5},{5,4},{6,7},{7,6},{8,9},{9,8},{10,11... | collective-permute-start | bytes 1376264 | tf_op jit(solution)/shard_map/ppermute | solution.py:77
  533.8 14.8 %collective-permute-start.87 = (bf16[224,1024]{1,0:T(8,128)(2,1)}, bf16[224,1024]{1,0:T(8,128)(2,1)S(1)}, u32[]{:S(2)}, u32[]{:S(2)}) collective-permute-start(bf16[224,1024]{1,0:T(8,128)(2,1)} %collective-permute-done.77.refs_0_), channel_id=1, source_target_pairs={{0,1},{1,0},{2,3},{3,2},{4,5},{5,4},{6,7},{7,6},{8,9},{9,8},{10,11... | collective-permute-start | bytes 1376264 | tf_op jit(solution)/shard_map/ppermute | solution.py:77
  534.4 14.2 %collective-permute-start.88 = (bf16[224,1024]{1,0:T(8,128)(2,1)}, bf16[224,1024]{1,0:T(8,128)(2,1)}, u32[]{:S(2)}, u32[]{:S(2)}) collective-permute-start(bf16[224,1024]{1,0:T(8,128)(2,1)} %collective-permute-done.78.refs_1_), channel_id=1, source_target_pairs={{0,1},{1,0},{2,3},{3,2},{4,5},{5,4},{6,7},{7,6},{8,9},{9,8},{10,11... | collective-permute-start | bytes 1376264 | tf_op jit(solution)/shard_map/ppermute | solution.py:77
  535.4 26.5 %collective-permute-start.83 = (bf16[112,1024]{1,0:T(8,128)(2,1)}, bf16[112,1024]{1,0:T(8,128)(2,1)S(1)}, u32[]{:S(2)}, u32[]{:S(2)}) collective-permute-start(bf16[112,1024]{1,0:T(8,128)(2,1)} %slice.348), channel_id=1, source_target_pairs={{0,2},{2,6},{6,10},{10,14},{14,12},{12,8},{8,4},{4,0},{1,3},{3,7},... | collective-permute-start | bytes 688136 | tf_op jit(solution)/shard_map/ppermute | solution.py:144
  540.9 21.0 %collective-permute-start.82 = (bf16[112,1024]{1,0:T(8,128)(2,1)S(1)}, bf16[112,1024]{1,0:T(8,128)(2,1)S(1)}, u32[]{:S(2)}, u32[]{:S(2)}) collective-permute-start(bf16[112,1024]{1,0:T(8,128)(2,1)S(1)} %slice.345), channel_id=1, source_target_pairs={{2,0},{6,2},{10,6},{14,10},{12,14},{8,12},{4,8},{0,4},{3,1},{7,3},... | collective-permute-start | bytes 688136 | tf_op jit(solution)/shard_map/ppermute | solution.py:145
  561.9 13.0 %collective-permute-start.84 = (bf16[224,1024]{1,0:T(8,128)(2,1)S(1)}, bf16[224,1024]{1,0:T(8,128)(2,1)S(1)}, u32[]{:S(2)}, u32[]{:S(2)}) collective-permute-start(bf16[224,1024]{1,0:T(8,128)(2,1)S(1)} %constant_dynamic-update-slice_fusion.4.refs_0_), channel_id=1, source_target_pairs={{0,1},{1,0},{2,3},{3,2},{4,5},{5,4},{6,7},{7,6},{8,9},{9,8},{10,11... | collective-permute-start | bytes 1376264 | tf_op jit(solution)/shard_map/ppermute | solution.py:77
  (172 other events, 2286.5 us)
Sparse Core Ops, SparseCore 0:
  70.2 42.9 all-gather.4
  115.3 21.6 all-gather.6
  455.4 19.4 all-gather.10
  476.9 37.9 all-gather.8

commit v4 on v3

--- a/solution.py
+++ b/solution.py
@@ -1293,7 +1293,7 @@
     output = hidden + mix_sum.finish(mix_parts[0])
     dense_new = None
     dense_ring = RingGather(ring, carried)
-    arrived, first_place, earlier = dict(dense_ring.blocks), 0, [(), ()]
+    arrived, first_place, earlier = dict(dense_ring.blocks), 0, [()]
     while arrived:
         later = {}
         if dense_ring.place < ring.half:

time: 597 us -> 590 us (0.988)
  waiting for transfers between devices: 143 us -> 137 us
  transfers between devices with their start and end apart: 95 -> 95, of which waited for: 39 -> 40; matrix products, arithmetic and copies ran while one was open for 20% -> 20% of each run, Pallas kernels for 30% -> 31%
where the time goes in v4:
time: 590 us; the launch traced here: 580 us
  Pallas kernels  197 us (33%)
  waiting for transfers between devices  137 us (23%)
  starting transfers between devices  86.6 us (15%)
  other arithmetic  62.3 us (11%)
  matrix products  43.2 us (7%)
  local copies, waits for them, and re-layouts  37.5 us (6%)
  between operations  16.8 us (3%)
    pallas_call x5, Pallas kernels, attend_back(): pl.pallas_call(functools.partial(attend_back_kernel, first_block, blocks,...  62.1 us
    ppermute x12, waiting for transfers between devices, step(): self.ahead = lax.ppermute(self.ahead, 'chip', ring.forward)  55.1 us
    pallas_call x5, Pallas kernels, run_experts(): pl.pallas_call(functools.partial(expert_kernel, count, tok, spill), grid_...  54.3 us
    pallas_call x5, Pallas kernels, attend(): pl.pallas_call(functools.partial(attend_kernel, first_block, blocks, firs...  41.7 us
    ppermute x16, waiting for transfers between devices, send(): self.behind = lax.ppermute(self.sent[1], 'chip', self.ring.backward)  40 us
    dot_general x7, matrix products, dot_tn(): lax.dot_general(left, right, (((0,), (0,)), ((), ())), preferred_element_...  37.3 us
    pallas_call x5, Pallas kernels, optimize(): pl.pallas_call(functools.partial(optimizer_kernel, blocks, dp_size, grad_...  28.3 us
    ppermute x16, starting transfers between devices, send(): self.ahead = lax.ppermute(self.sent[0], 'chip', self.ring.forward)  23.9 us
  transfers between devices with their start and end apart: 95, of which 40 were waited for; matrix products, arithmetic and copies ran while one was open for 20% of the time, Pallas kernels for 31%

profile of v4, /device:TPU:0, one launch (start us, length us, event | category | flops | bytes accessed | tf_op | source)
XLA Modules:
  0.0 580.4 jit_solution(13630858045051385717)
XLA Ops:
  10.5 2.9 collective-permute-start.2
  13.5 2.0 collective-permute-start.1
  15.6 2.2 copy-done
  21.6 9.4 %collective-permute-done.2.refs_2_ = bf16[384,1024]{1,0:T(8,128)(2,1)S(1)} collective-permute-done((bf16[384,1024]{1,0:T(8,128)(2,1)S(1)}, bf16[384,1024]{1,0:T(8,128)(2,1)S(1)}, u32[]{:S(2)}, u32[]{:S(2)}) %collective-permute-start.2) | collective-permute-done | bytes 786464 | tf_op jit(solution)/shard_map/ppermute | solution.py:139
  34.9 15.0 %collective-permute-done.6.refs_2_ = bf16[384,1024]{1,0:T(8,128)(2,1)} collective-permute-done((bf16[384,1024]{1,0:T(8,128)(2,1)S(1)}, bf16[384,1024]{1,0:T(8,128)(2,1)}, u32[]{:S(2)}, u32[]{:S(2)}) %collective-permute-start.6) | collective-permute-done | bytes 786464 | tf_op jit(solution)/shard_map/ppermute | solution.py:139
  60.0 4.8 project.1
  74.5 2.4 select_convert_fusion
  82.9 7.2 %attend.5 = (f32[6,2,128,512]{3,2,1,0:T(8,128)S(1)}, f32[6,2,8,512]{3,2,1,0:T(8,128)S(1)}) custom-call(s32[16]{0:T(128)S(1)} %concatenate.109.meta_ref, bf16[768,512]{1,0:T(8,128)(2,1)S(1)} %copy-done.43, bf16[512,512]{1,0:T(8,128)(2,1)S(1)} %bitcast.152, bf16[2,128,512]{2,1,0:T(8,128)(2,1)S(1)} %copy-done.47), custom_call_target="tpu_custom_call" | custom-call | flops 4831838208 | bytes 12582912 | tf_op jit(solution)/shard_map/attend/pallas_call | solution.py:488
  90.1 9.8 %attend.6 = (f32[6,2,128,512]{3,2,1,0:T(8,128)S(1)}, f32[6,2,8,512]{3,2,1,0:T(8,128)S(1)}) custom-call(s32[16]{0:T(128)S(1)} %concatenate.109.meta_ref, bf16[768,512]{1,0:T(8,128)(2,1)S(1)} %copy-done.43, bf16[512,512]{1,0:T(8,128)(2,1)S(1)} %collective-permute-done.10.refs_0_, bf16[512,512]{1,0:T(8,128)(2,1)} %collective-permute-done.14.refs_1_, ...), custom_call_target="tpu_custom_call" | custom-call | flops 9663676416 | bytes 12582912 | tf_op jit(solution)/shard_map/attend/pallas_call | solution.py:488
  103.8 4.6 collective-permute-done.18
  114.1 8.7 %attend.7 = (f32[6,2,128,512]{3,2,1,0:T(8,128)S(1)}, f32[6,2,8,512]{3,2,1,0:T(8,128)S(1)}) custom-call(s32[16]{0:T(128)S(1)} %concatenate.109.meta_ref, bf16[768,512]{1,0:T(8,128)(2,1)S(1)} %copy-done.44, bf16[512,512]{1,0:T(8,128)(2,1)S(1)} %collective-permute-done.11.refs_0_, bf16[512,512]{1,0:T(8,128)(2,1)S(1)} %collective-permute-done.15.refs_1_, ...), custom_call_target="tpu_custom_call" | custom-call | flops 9663676416 | bytes 12582912 | tf_op jit(solution)/shard_map/attend/pallas_call | solution.py:488
  126.0 8.7 %attend.8 = (f32[6,2,128,512]{3,2,1,0:T(8,128)S(1)}, f32[6,2,8,512]{3,2,1,0:T(8,128)S(1)}) custom-call(s32[16]{0:T(128)S(1)} %concatenate.109.meta_ref, bf16[768,512]{1,0:T(8,128)(2,1)S(1)} %copy-done.44, bf16[512,512]{1,0:T(8,128)(2,1)S(1)} %collective-permute-done.12.refs_0_, bf16[512,512]{1,0:T(8,128)(2,1)S(1)} %collective-permute-done.16.refs_1_, ...), custom_call_target="tpu_custom_call" | custom-call | flops 9663676416 | bytes 12582912 | tf_op jit(solution)/shard_map/attend/pallas_call | solution.py:488
  134.9 7.3 %attend.9 = (f32[768,512]{1,0:T(8,128)S(1)}, bf16[768,512]{1,0:T(8,128)(2,1)S(1)}, f32[8,768]{1,0:T(8,128)S(1)}) custom-call(s32[16]{0:T(128)S(1)} %concatenate.109.meta_ref, bf16[768,512]{1,0:T(8,128)(2,1)S(1)} %copy-done.44, bf16[512,512]{1,0:T(8,128)(2,1)S(1)} %constant_dynamic-update-slice_fusion.refs_0_, ...), custom_call_target="tpu_custom_call" | custom-call | flops 4831838208 | bytes 12582912 | tf_op jit(solution)/shard_map/attend/pallas_call | solution.py:488
  148.1 2.2 multiply_reduce_fusion.2
  154.2 6.1 %experts.5 = (bf16[384,1024]{1,0:T(8,128)(2,1)S(1)}, bf16[400,1024]{1,0:T(8,128)(2,1)S(1)}, bf16[3072,1024]{1,0:T(8,128)(2,1)}, bf16[3072,1024]{1,0:T(8,128)(2,1...) custom-call(s32[16]{0:T(128)S(1)} %concatenate.109.meta_ref, bf16[400,1024]{1,0:T(8,128)(2,1)S(1)} %pad_maximum_fusion.3.refs_0_, ...), custom_call_target="tpu_custom_call" | custom-call | flops 4831838208 | bytes 14155776 | tf_op jit(solution)/shard_map/experts/pallas_call | solution.py:942
  160.3 12.3 %collective-permute-done.23.refs_0_ = bf16[400,1024]{1,0:T(8,128)(2,1)S(1)} collective-permute-done((bf16[400,1024]{1,0:T(8,128)(2,1)S(1)}, bf16[400,1024]{1,0:T(8,128)(2,1)S(1)}, u32[]{:S(2)}, u32[]{:S(2)}) %collective-permute-start.23) | collective-permute-done | bytes 819232 | tf_op jit(solution)/shard_map/ppermute | solution.py:139
  176.2 14.4 %experts.6 = (bf16[384,1024]{1,0:T(8,128)(2,1)S(1)}, bf16[384,1024]{1,0:T(8,128)(2,1)S(1)}, bf16[400,1024]{1,0:T(8,128)(2,1)S(1)}, bf16[400,1024]{1,0:T(8,128)(2...) custom-call(s32[16]{0:T(128)S(1)} %concatenate.109.meta_ref, ...), custom_call_target="tpu_custom_call", output_to_operand_aliasing={{4}: (9, {}), {5}: (10, {}), {6}: (11, {}), {7}: (12, {})} | custom-call | flops 9663676416 | bytes 22020096 | tf_op jit(solution)/shard_map/experts/pallas_call | solution.py:942
  196.8 14.5 %experts.7 = (bf16[384,1024]{1,0:T(8,128)(2,1)S(1)}, bf16[384,1024]{1,0:T(8,128)(2,1)S(1)}, bf16[400,1024]{1,0:T(8,128)(2,1)S(1)}, bf16[400,1024]{1,0:T(8,128)(2...) custom-call(s32[16]{0:T(128)S(1)} %concatenate.109.meta_ref, ...), custom_call_target="tpu_custom_call", output_to_operand_aliasing={{4}: (9, {}), {5}: (10, {}), {6}: (11, {}), {7}: (12, {})} | custom-call | flops 9663676416 | bytes 22020096 | tf_op jit(solution)/shard_map/experts/pallas_call | solution.py:942
  218.5 13.5 %experts.8 = (bf16[384,1024]{1,0:T(8,128)(2,1)S(1)}, bf16[384,1024]{1,0:T(8,128)(2,1)S(1)}, bf16[400,1024]{1,0:T(8,128)(2,1)S(1)}, bf16[400,1024]{1,0:T(8,128)(2...) custom-call(s32[16]{0:T(128)S(1)} %concatenate.109.meta_ref, ...), custom_call_target="tpu_custom_call", output_to_operand_aliasing={{4}: (9, {}), {5}: (10, {}), {6}: (11, {}), {7}: (12, {})} | custom-call | flops 9663676416 | bytes 22020096 | tf_op jit(solution)/shard_map/experts/pallas_call | solution.py:942
  232.2 5.8 %experts.9 = (bf16[384,1024]{1,0:T(8,128)(2,1)S(1)}, bf16[400,1024]{1,0:T(8,128)(2,1)S(1)}, bf16[3072,1024]{1,0:T(8,128)(2,1)}, bf16[3072,1024]{1,0:T(8,128)(2,1...) custom-call(s32[16]{0:T(128)S(1)} %concatenate.109.meta_ref, ...), custom_call_target="tpu_custom_call", output_to_operand_aliasing={{2}: (7, {}), {3}: (8, {}), {4}: (9, {}), {5}: (10, {})} | custom-call | flops 4831838208 | bytes 14155776 | tf_op jit(solution)/shard_map/experts/pallas_call | solution.py:942
  240.3 9.0 %collective-permute-done.33 = bf16[192,1024]{1,0:T(8,128)(2,1)S(1)} collective-permute-done((bf16[192,1024]{1,0:T(8,128)(2,1)S(1)}, bf16[192,1024]{1,0:T(8,128)(2,1)S(1)}, u32[]{:S(2)}, u32[]{:S(2)}) %collective-permute-start.33) | collective-permute-done | bytes 393248 | tf_op jit(solution)/shard_map/ppermute | solution.py:161
  251.7 9.0 %fusion.15 = bf16[1024,1024]{1,0:T(8,128)(2,1)S(1)} fusion(bf16[3072,1024]{1,0:T(8,128)(2,1)S(1)} %copy-done.51, bf16[3072,2048]{1,0:T(8,128)(2,1)} %get-tuple-element.317), kind=kOutput, calls=%fused_computation.25 | convolution fusion | flops 6443499520 | bytes 14680064 | tf_op jit(solution)/shard_map/dot_general | solution.py:40
  260.7 7.3 %fusion.29 = bf16[512,1024]{1,0:T(8,128)(2,1)S(1)} fusion(bf16[3072,1024]{1,0:T(8,128)(2,1)} %get-tuple-element.319, bf16[3072,1024]{1,0:T(8,128)(2,1)} %get-tuple-element.318), kind=kOutput, calls=%fused_computation.52 | convolution fusion | flops 3221749760 | bytes 10485760 | tf_op jit(solution)/shard_map/dot_general | solution.py:40
  271.3 18.2 %collective-permute-done.38 = bf16[400,1024]{1,0:T(8,128)(2,1)S(1)} collective-permute-done((bf16[400,1024]{1,0:T(8,128)(2,1)S(1)}, bf16[400,1024]{1,0:T(8,128)(2,1)S(1)}, u32[]{:S(2)}, u32[]{:S(2)}) %collective-permute-start.38) | collective-permute-done | bytes 819232 | tf_op jit(solution)/shard_map/ppermute | solution.py:162
  291.2 1.9 collective-permute-start.41
  293.1 9.2 %add_convert_fusion = bf16[1024,1024]{1,0:T(8,128)(2,1)} fusion(bf16[1024,1024]{1,0:T(8,128)(2,1)} %copy-done.132, bf16[3072,1024]{1,0:T(8,128)(2,1)S(1)} %copy-done.51, bf16[3072,2048]{1,0:T(8,128)(2,1)S(1)} %bitcast.155), kind=kOutput, calls=%fused_computation.4 | convolution fusion | flops 6445596672 | bytes 16777216 | tf_op jit(solution)/shard_map/dot_general | solution.py:40
  302.3 6.3 %add_convert_fusion.1 = bf16[512,1024]{1,0:T(8,128)(2,1)} fusion(bf16[512,1024]{1,0:T(8,128)(2,1)S(1)} %collective-permute-done.40, bf16[3072,1024]{1,0:T(8,128)(2,1)S(1)} %bitcast.158, bf16[3072,1024]{1,0:T(8,128)(2,1)} %get-tuple-element.318), kind=kOutput, calls=%fused_computation.24 | convolution fusion | flops 3222798336 | bytes 11534336 | tf_op jit(solution)/shard_map/dot_general | solution.py:40
  316.3 5.6 collective-permute-done.43
  323.8 2.2 collective-permute-done.45
  328.4 7.7 %attend_back.5 = (bf16[512,512]{1,0:T(8,128)(2,1)S(1)}, f32[6,2,128,512]{3,2,1,0:T(8,128)S(1)}) custom-call(s32[16]{0:T(128)S(1)} %concatenate.109.meta_ref, bf16[768,512]{1,0:T(8,128)(2,1)S(1)} %copy-done.45, bf16[768,512]{1,0:T(8,128)(2,1)S(1)} %convolution_convert_fusion.2.do_ref, f32[768,512]{1,0:T(8,128)S(1)} %copy-done.50, ...), custom_call_target="tpu_custom_call" | custom-call | flops 11072962560 | bytes 16777216 | tf_op jit(solution)/shard_map/attend_back/pallas_call | solution.py:538
  340.9 13.3 %attend_back.6 = (bf16[512,512]{1,0:T(8,128)(2,1)S(1)}, bf16[512,512]{1,0:T(8,128)(2,1)S(1)}, f32[6,2,128,512]{3,2,1,0:T(8,128)S(1)}) custom-call(s32[16]{0:T(128)S(1)} %concatenate.109.meta_ref, bf16[768,512]{1,0:T(8,128)(2,1)S(1)} %copy-done.45, bf16[768,512]{1,0:T(8,128)(2,1)S(1)} %convolution_convert_fusion.2.do_ref, f32[768,512]{1,0:T(8,128)S(1)} %copy-done.50, ...), custom_call_target="tpu_custom_call" | custom-call | flops 22145925120 | bytes 16777216 | tf_op jit(solution)/shard_map/attend_back/pallas_call | solution.py:538
  355.4 2.2 collective-permute-start.62
  361.0 13.3 %attend_back.7 = (bf16[512,512]{1,0:T(8,128)(2,1)S(1)}, bf16[512,512]{1,0:T(8,128)(2,1)S(1)}, f32[6,2,128,512]{3,2,1,0:T(8,128)S(1)}) custom-call(s32[16]{0:T(128)S(1)} %concatenate.109.meta_ref, bf16[768,512]{1,0:T(8,128)(2,1)S(1)} %copy-done.45, bf16[768,512]{1,0:T(8,128)(2,1)S(1)} %convolution_convert_fusion.2.do_ref, f32[768,512]{1,0:T(8,128)S(1)} %copy-done.50, ...), custom_call_target="tpu_custom_call" | custom-call | flops 22145925120 | bytes 16777216 | tf_op jit(solution)/shard_map/attend_back/pallas_call | solution.py:538
  376.7 14.4 %attend_back.8 = (bf16[512,512]{1,0:T(8,128)(2,1)S(1)}, bf16[512,512]{1,0:T(8,128)(2,1)S(1)}, f32[6,2,128,512]{3,2,1,0:T(8,128)S(1)}) custom-call(s32[16]{0:T(128)S(1)} %concatenate.109.meta_ref, bf16[768,512]{1,0:T(8,128)(2,1)S(1)} %copy-done.45, bf16[768,512]{1,0:T(8,128)(2,1)S(1)} %convolution_convert_fusion.2.do_ref, f32[768,512]{1,0:T(8,128)S(1)} %copy-done.50, ...), custom_call_target="tpu_custom_call" | custom-call | flops 22145925120 | bytes 16777216 | tf_op jit(solution)/shard_map/attend_back/pallas_call | solution.py:538
  396.1 1.8 collective-permute-start.56
  397.9 13.5 %attend_back.9 = (bf16[512,512]{1,0:T(8,128)(2,1)S(1)}, bf16[768,512]{1,0:T(8,128)(2,1)S(1)}, f32[2,128,512]{2,1,0:T(8,128)S(1)}) custom-call(s32[16]{0:T(128)S(1)} %concatenate.109.meta_ref, bf16[768,512]{1,0:T(8,128)(2,1)S(1)} %copy-done.45, bf16[768,512]{1,0:T(8,128)(2,1)S(1)} %convolution_convert_fusion.2.do_ref, f32[768,512]{1,0:T(8,128)S(1)} %copy-done.50, ...), custom_call_target="tpu_custom_call" | custom-call | flops 11072962560 | bytes 16777216 | tf_op jit(solution)/shard_map/attend_back/pallas_call | solution.py:538
  411.4 8.8 %collective-permute-done.57 = bf16[512,512]{1,0:T(8,128)(2,1)S(1)} collective-permute-done((bf16[512,512]{1,0:T(8,128)(2,1)S(1)}, bf16[512,512]{1,0:T(8,128)(2,1)S(1)}, u32[]{:S(2)}, u32[]{:S(2)}) %collective-permute-start.57) | collective-permute-done | bytes 524320 | tf_op jit(solution)/shard_map/ppermute | solution.py:162
  422.2 3.2 convolution_convert_fusion
  427.1 1.8 fusion.86
  432.3 2.3 collective-permute-start.66
  438.2 4.7 fusion.14
  442.8 3.5 collective-permute-done.61
  447.5 2.1 add.371
  449.6 1.9 add.370
  451.6 3.7 fusion.35
  458.9 2.5 fusion.20
  461.5 4.6 collective-permute-done.65
  472.2 2.1 collective-permute-start.70
  474.3 3.4 collective-permute-done.70
  480.2 1.8 collective-permute-start.73
  487.4 3.3 shard_step.1
  492.1 2.2 fusion.23
  497.2 4.9 collective-permute-done.74
  502.2 2.2 collective-permute-done.72
  506.4 8.4 %collective-permute-done.75.refs_0_ = bf16[224,1024]{1,0:T(8,128)(2,1)} collective-permute-done((bf16[224,1024]{1,0:T(8,128)(2,1)S(1)}, bf16[224,1024]{1,0:T(8,128)(2,1)}, u32[]{:S(2)}, u32[]{:S(2)}) %collective-permute-start.75) | collective-permute-done | bytes 458784 | tf_op jit(solution)/shard_map/ppermute | solution.py:139
  518.2 4.8 optimize.5
  524.8 1.9 collective-permute-start.80
  527.3 6.3 %optimize.6 = (f32[2,512,2048]{2,1,0:T(8,128)}, f32[512,2048]{1,0:T(8,128)}, f32[512,2048]{1,0:T(8,128)}, f32[2,2,256,1024]{3,2,1,0:T(8,128)}, f32[2,256,1024]{2,1,0:T(8,128)}, /*index=5*/f32[2,256,1024]{2,1,0:T(8,128)}) custom-call(s32[16]{0:T(128)} %copy-done.33, ...), custom_call_target="tpu_custom_call", output_to_operand_aliasing={{0}: (11, {}), {1}: (12, {}), {2}: (13, {}), {3}: (14, {}),... | custom-call | flops 7864320 | bytes 11796480 | tf_op jit(solution)/shard_map/optimize/pallas_call | solution.py:847
  533.7 2.0 collective-permute-done.80.refs_0_
  537.9 1.9 add_convert_fusion.2
  542.6 6.2 %optimize.7 = (f32[2,512,2048]{2,1,0:T(8,128)}, f32[512,2048]{1,0:T(8,128)}, f32[512,2048]{1,0:T(8,128)}, f32[2,2,256,1024]{3,2,1,0:T(8,128)}, f32[2,256,1024]{2,1,0:T(8,128)}, /*index=5*/f32[2,256,1024]{2,1,0:T(8,128)}) custom-call(s32[16]{0:T(128)} %copy-done.33, ...), custom_call_target="tpu_custom_call", output_to_operand_aliasing={{0}: (11, {}), {1}: (12, {}), {2}: (13, {}), {3}: (14, {}),... | custom-call | flops 7864320 | bytes 11796480 | tf_op jit(solution)/shard_map/optimize/pallas_call | solution.py:847
  548.9 4.2 convert_element_type.236
  561.9 6.2 %optimize.8 = (f32[2,512,2048]{2,1,0:T(8,128)}, f32[512,2048]{1,0:T(8,128)}, f32[512,2048]{1,0:T(8,128)}, f32[2,2,256,1024]{3,2,1,0:T(8,128)}, f32[2,256,1024]{2,1,0:T(8,128)}, /*index=5*/f32[2,256,1024]{2,1,0:T(8,128)}) custom-call(s32[16]{0:T(128)} %copy-done.33, ...), custom_call_target="tpu_custom_call", output_to_operand_aliasing={{0}: (11, {}), {1}: (12, {}), {2}: (13, {}), {3}: (14, {}),... | custom-call | flops 7864320 | bytes 11796480 | tf_op jit(solution)/shard_map/optimize/pallas_call | solution.py:847
  568.9 4.8 optimize.9
  (595 shorter events, 168.9 us)
Async XLA Ops:
  7.2 138.6 %all-gather.5.cloned.1.call-start = ((), (), s32[]{:S(2)}) async-start(), calls=%async_computation | async-start | bytes 3145728 | tf_op jit(solution)/shard_map/all_gather | solution.py:1064
  10.5 20.6 %collective-permute-start.2 = (bf16[384,1024]{1,0:T(8,128)(2,1)S(1)}, bf16[384,1024]{1,0:T(8,128)(2,1)S(1)}, u32[]{:S(2)}, u32[]{:S(2)}) collective-permute-start(bf16[384,1024]{1,0:T(8,128)(2,1)S(1)} %pad_maximum_fusion.8.refs_1_), channel_id=1, source_target_pairs={{0,2},{2,6},{6,10},{10,14},{14,12},{12,8},{8,4},{4,0},{1,3},{3,7},... | collective-permute-start | bytes 2359304 | tf_op jit(solution)/shard_map/ppermute | solution.py:139
  13.4 19.3 %collective-permute-start.3 = (bf16[384,1024]{1,0:T(8,128)(2,1)S(1)}, bf16[384,1024]{1,0:T(8,128)(2,1)}, u32[]{:S(2)}, u32[]{:S(2)}) collective-permute-start(bf16[384,1024]{1,0:T(8,128)(2,1)S(1)} %pad_maximum_fusion.8.refs_1_), channel_id=1, source_target_pairs={{2,0},{6,2},{10,6},{14,10},{12,14},{8,12},{4,8},{0,4},{3,1},{7,3},... | collective-permute-start | bytes 2359304 | tf_op jit(solution)/shard_map/ppermute | solution.py:140
  13.5 20.2 %collective-permute-start.1 = (bf16[18,512]{1,0:T(8,128)(2,1)S(1)}, bf16[18,512]{1,0:T(8,128)(2,1)S(1)}, u32[]{:S(2)}, u32[]{:S(2)}) collective-permute-start(bf16[18,512]{1,0:T(8,128)(2,1)S(1)} %fusion.53), channel_id=1, source_target_pairs={{0,16},{16,0},{1,17},{17,1},{2,18},{18,2},{3,19},{19,3},{4,20},{20... | collective-permute-start | bytes 55304 | tf_op jit(solution)/shard_map/ppermute | solution.py:205
  15.6 42.0 %collective-permute-start = (s32[1]{0:T(128)}, s32[1]{0:T(128)}, u32[]{:S(2)}, u32[]{:S(2)}) collective-permute-start(s32[1]{0:T(128)} %param.31), channel_id=1, source_target_pairs={{0,1},{1,0},{2,3},{3,2},{4,5},{5,4},{6,7},{7,6},{8,9},{9,8},{10,11... | collective-permute-start | bytes 20 | tf_op jit(solution)/shard_map/ppermute | solution.py:77
  18.0 41.0 %collective-permute-start.5 = (bf16[512,1024]{1,0:T(8,128)(2,1)S(1)}, bf16[512,1024]{1,0:T(8,128)(2,1)}, u32[]{:S(2)}, u32[]{:S(2)}) collective-permute-start(bf16[512,1024]{1,0:T(8,128)(2,1)S(1)} %cast_core_columns.1.refs_0_), channel_id=1, source_target_pairs={{0,16},{16,0},{1,17},{17,1},{2,18},{18,2},{3,19},{19,3},{4,20},{20... | collective-permute-start | bytes 3145736 | tf_op jit(solution)/shard_map/ppermute | solution.py:205
  31.0 18.9 %collective-permute-start.6 = (bf16[384,1024]{1,0:T(8,128)(2,1)S(1)}, bf16[384,1024]{1,0:T(8,128)(2,1)}, u32[]{:S(2)}, u32[]{:S(2)}) collective-permute-start(bf16[384,1024]{1,0:T(8,128)(2,1)S(1)} %collective-permute-done.2.refs_2_), channel_id=1, source_target_pairs={{0,2},{2,6},{6,10},{10,14},{14,12},{12,8},{8,4},{4,0},{1,3},{3,7},... | collective-permute-start | bytes 2359304 | tf_op jit(solution)/shard_map/ppermute | solution.py:139
  32.7 18.6 %collective-permute-start.7 = (bf16[384,1024]{1,0:T(8,128)(2,1)}, bf16[384,1024]{1,0:T(8,128)(2,1)}, u32[]{:S(2)}, u32[]{:S(2)}) collective-permute-start(bf16[384,1024]{1,0:T(8,128)(2,1)} %collective-permute-done.3.refs_3_), channel_id=1, source_target_pairs={{2,0},{6,2},{10,6},{14,10},{12,14},{8,12},{4,8},{0,4},{3,1},{7,3},... | collective-permute-start | bytes 2359304 | tf_op jit(solution)/shard_map/ppermute | solution.py:140
  34.9 24.1 %collective-permute-start.4 = (bf16[384,1024]{1,0:T(8,128)(2,1)}, bf16[384,1024]{1,0:T(8,128)(2,1)}, u32[]{:S(2)}, u32[]{:S(2)}) collective-permute-start(bf16[384,1024]{1,0:T(8,128)(2,1)} %fusion.18.own_ref), channel_id=1, source_target_pairs={{0,1},{1,0},{2,3},{3,2},{4,5},{5,4},{6,7},{7,6},{8,9},{9,8},{10,11... | collective-permute-start | bytes 2359304 | tf_op jit(solution)/shard_map/ppermute | solution.py:77
  50.0 18.1 %collective-permute-start.8 = (bf16[384,1024]{1,0:T(8,128)(2,1)}, bf16[384,1024]{1,0:T(8,128)(2,1)S(1)}, u32[]{:S(2)}, u32[]{:S(2)}) collective-permute-start(bf16[384,1024]{1,0:T(8,128)(2,1)} %collective-permute-done.6.refs_2_), channel_id=1, source_target_pairs={{0,2},{2,6},{6,10},{10,14},{14,12},{12,8},{8,4},{4,0},{1,3},{3,7},... | collective-permute-start | bytes 2359304 | tf_op jit(solution)/shard_map/ppermute | solution.py:139
  51.3 17.5 %collective-permute-start.9 = (bf16[384,1024]{1,0:T(8,128)(2,1)}, bf16[384,1024]{1,0:T(8,128)(2,1)S(1)}, u32[]{:S(2)}, u32[]{:S(2)}) collective-permute-start(bf16[384,1024]{1,0:T(8,128)(2,1)} %collective-permute-done.7.refs_3_), channel_id=1, source_target_pairs={{2,0},{6,2},{10,6},{14,10},{12,14},{8,12},{4,8},{0,4},{3,1},{7,3},... | collective-permute-start | bytes 2359304 | tf_op jit(solution)/shard_map/ppermute | solution.py:140
  70.1 76.3 %all-gather.7.cloned.1.call-start = ((), (), s32[]{:S(2)}) async-start(), calls=%async_computation.1 | async-start | bytes 1572864 | tf_op jit(solution)/shard_map/all_gather | solution.py:1065
  72.5 17.6 %collective-permute-start.10 = (bf16[512,512]{1,0:T(8,128)(2,1)S(1)}, bf16[512,512]{1,0:T(8,128)(2,1)S(1)}, u32[]{:S(2)}, u32[]{:S(2)}) collective-permute-start(bf16[512,512]{1,0:T(8,128)(2,1)S(1)} %bitcast.150), channel_id=1, source_target_pairs={{0,2},{2,6},{6,10},{10,14},{14,12},{12,8},{8,4},{4,0},{1,3},{3,7},... | collective-permute-start | bytes 1572872 | tf_op jit(solution)/shard_map/ppermute | solution.py:139
  74.0 16.0 %collective-permute-start.14 = (bf16[512,512]{1,0:T(8,128)(2,1)S(1)}, bf16[512,512]{1,0:T(8,128)(2,1)}, u32[]{:S(2)}, u32[]{:S(2)}) collective-permute-start(bf16[512,512]{1,0:T(8,128)(2,1)S(1)} %bitcast.151), channel_id=1, source_target_pairs={{2,0},{6,2},{10,6},{14,10},{12,14},{8,12},{4,8},{0,4},{3,1},{7,3},... | collective-permute-start | bytes 1572872 | tf_op jit(solution)/shard_map/ppermute | solution.py:140
  76.9 25.6 %collective-permute-start.19 = (bf16[256,1024]{1,0:T(8,128)(2,1)}, bf16[256,1024]{1,0:T(8,128)(2,1)}, u32[]{:S(2)}, u32[]{:S(2)}) collective-permute-start(bf16[256,1024]{1,0:T(8,128)(2,1)} %select_convert_fusion), channel_id=1, source_target_pairs={{0,16},{16,0},{1,17},{17,1},{2,18},{18,2},{3,19},{19,3},{4,20},{20... | collective-permute-start | bytes 1572872 | tf_op jit(solution)/shard_map/ppermute | solution.py:205
  82.4 466.4 %all-gather.11.cloned.1.call-start = ((), (), s32[]{:S(2)}) async-start(), calls=%async_computation.3 | async-start | bytes 1572864 | tf_op jit(solution)/shard_map/all_gather | solution.py:1334
  100.5 11.4 %collective-permute-start.11 = (bf16[512,512]{1,0:T(8,128)(2,1)S(1)}, bf16[512,512]{1,0:T(8,128)(2,1)S(1)}, u32[]{:S(2)}, u32[]{:S(2)}) collective-permute-start(bf16[512,512]{1,0:T(8,128)(2,1)S(1)} %collective-permute-done.10.refs_0_), channel_id=1, source_target_pairs={{0,2},{2,6},{6,10},{10,14},{14,12},{12,8},{8,4},{4,0},{1,3},{3,7},... | collective-permute-start | bytes 1572872 | tf_op jit(solution)/shard_map/ppermute | solution.py:139
  102.2 11.3 %collective-permute-start.15 = (bf16[512,512]{1,0:T(8,128)(2,1)}, bf16[512,512]{1,0:T(8,128)(2,1)S(1)}, u32[]{:S(2)}, u32[]{:S(2)}) collective-permute-start(bf16[512,512]{1,0:T(8,128)(2,1)} %collective-permute-done.14.refs_1_), channel_id=1, source_target_pairs={{2,0},{6,2},{10,6},{14,10},{12,14},{8,12},{4,8},{0,4},{3,1},{7,3},... | collective-permute-start | bytes 1572872 | tf_op jit(solution)/shard_map/ppermute | solution.py:140
  111.9 11.9 %collective-permute-start.12 = (bf16[512,512]{1,0:T(8,128)(2,1)S(1)}, bf16[512,512]{1,0:T(8,128)(2,1)S(1)}, u32[]{:S(2)}, u32[]{:S(2)}) collective-permute-start(bf16[512,512]{1,0:T(8,128)(2,1)S(1)} %collective-permute-done.11.refs_0_), channel_id=1, source_target_pairs={{0,2},{2,6},{6,10},{10,14},{14,12},{12,8},{8,4},{4,0},{1,3},{3,7},... | collective-permute-start | bytes 1572872 | tf_op jit(solution)/shard_map/ppermute | solution.py:139
  113.5 12.0 %collective-permute-start.16 = (bf16[512,512]{1,0:T(8,128)(2,1)S(1)}, bf16[512,512]{1,0:T(8,128)(2,1)S(1)}, u32[]{:S(2)}, u32[]{:S(2)}) collective-permute-start(bf16[512,512]{1,0:T(8,128)(2,1)S(1)} %collective-permute-done.15.refs_1_), channel_id=1, source_target_pairs={{2,0},{6,2},{10,6},{14,10},{12,14},{8,12},{4,8},{0,4},{3,1},{7,3},... | collective-permute-start | bytes 1572872 | tf_op jit(solution)/shard_map/ppermute | solution.py:140
  152.1 20.5 %collective-permute-start.23 = (bf16[400,1024]{1,0:T(8,128)(2,1)S(1)}, bf16[400,1024]{1,0:T(8,128)(2,1)S(1)}, u32[]{:S(2)}, u32[]{:S(2)}) collective-permute-start(bf16[400,1024]{1,0:T(8,128)(2,1)S(1)} %pad_maximum_fusion.3.refs_0_), channel_id=1, source_target_pairs={{0,2},{2,6},{6,10},{10,14},{14,12},{12,8},{8,4},{4,0},{1,3},{3,7},... | collective-permute-start | bytes 2457608 | tf_op jit(solution)/shard_map/ppermute | solution.py:139
  153.8 20.0 %collective-permute-start.24 = (bf16[400,1024]{1,0:T(8,128)(2,1)S(1)}, bf16[400,1024]{1,0:T(8,128)(2,1)S(1)}, u32[]{:S(2)}, u32[]{:S(2)}) collective-permute-start(bf16[400,1024]{1,0:T(8,128)(2,1)S(1)} %pad_maximum_fusion.3.refs_0_), channel_id=1, source_target_pairs={{2,0},{6,2},{10,6},{14,10},{12,14},{8,12},{4,8},{0,4},{3,1},{7,3},... | collective-permute-start | bytes 2457608 | tf_op jit(solution)/shard_map/ppermute | solution.py:140
  173.8 19.1 %collective-permute-start.25 = (bf16[400,1024]{1,0:T(8,128)(2,1)S(1)}, bf16[400,1024]{1,0:T(8,128)(2,1)S(1)}, u32[]{:S(2)}, u32[]{:S(2)}) collective-permute-start(bf16[400,1024]{1,0:T(8,128)(2,1)S(1)} %collective-permute-done.23.refs_0_), channel_id=1, source_target_pairs={{0,2},{2,6},{6,10},{10,14},{14,12},{12,8},{8,4},{4,0},{1,3},{3,7},... | collective-permute-start | bytes 2457608 | tf_op jit(solution)/shard_map/ppermute | solution.py:139
  175.4 19.2 %collective-permute-start.26 = (bf16[400,1024]{1,0:T(8,128)(2,1)S(1)}, bf16[400,1024]{1,0:T(8,128)(2,1)S(1)}, u32[]{:S(2)}, u32[]{:S(2)}) collective-permute-start(bf16[400,1024]{1,0:T(8,128)(2,1)S(1)} %collective-permute-done.24.refs_1_), channel_id=1, source_target_pairs={{2,0},{6,2},{10,6},{14,10},{12,14},{8,12},{4,8},{0,4},{3,1},{7,3},... | collective-permute-start | bytes 2457608 | tf_op jit(solution)/shard_map/ppermute | solution.py:140
  194.6 17.9 %collective-permute-start.27 = (bf16[400,1024]{1,0:T(8,128)(2,1)S(1)}, bf16[400,1024]{1,0:T(8,128)(2,1)S(1)}, u32[]{:S(2)}, u32[]{:S(2)}) collective-permute-start(bf16[400,1024]{1,0:T(8,128)(2,1)S(1)} %collective-permute-done.25.refs_0_), channel_id=1, source_target_pairs={{0,2},{2,6},{6,10},{10,14},{14,12},{12,8},{8,4},{4,0},{1,3},{3,7},... | collective-permute-start | bytes 2457608 | tf_op jit(solution)/shard_map/ppermute | solution.py:139
  196.1 17.8 %collective-permute-start.28 = (bf16[400,1024]{1,0:T(8,128)(2,1)S(1)}, bf16[400,1024]{1,0:T(8,128)(2,1)S(1)}, u32[]{:S(2)}, u32[]{:S(2)}) collective-permute-start(bf16[400,1024]{1,0:T(8,128)(2,1)S(1)} %collective-permute-done.26.refs_1_), channel_id=1, source_target_pairs={{2,0},{6,2},{10,6},{14,10},{12,14},{8,12},{4,8},{0,4},{3,1},{7,3},... | collective-permute-start | bytes 2457608 | tf_op jit(solution)/shard_map/ppermute | solution.py:140
  214.1 18.0 %collective-permute-start.31 = (bf16[192,1024]{1,0:T(8,128)(2,1)S(1)}, bf16[192,1024]{1,0:T(8,128)(2,1)S(1)}, u32[]{:S(2)}, u32[]{:S(2)}) collective-permute-start(bf16[192,1024]{1,0:T(8,128)(2,1)S(1)} %slice.290), channel_id=1, source_target_pairs={{0,2},{2,6},{6,10},{10,14},{14,12},{12,8},{8,4},{4,0},{1,3},{3,7},... | collective-permute-start | bytes 1179656 | tf_op jit(solution)/shard_map/ppermute | solution.py:144
  214.9 17.1 %collective-permute-start.32 = (bf16[192,1024]{1,0:T(8,128)(2,1)S(1)}, bf16[192,1024]{1,0:T(8,128)(2,1)S(1)}, u32[]{:S(2)}, u32[]{:S(2)}) collective-permute-start(bf16[192,1024]{1,0:T(8,128)(2,1)S(1)} %slice.291), channel_id=1, source_target_pairs={{2,0},{6,2},{10,6},{14,10},{12,14},{8,12},{4,8},{0,4},{3,1},{7,3},... | collective-permute-start | bytes 1179656 | tf_op jit(solution)/shard_map/ppermute | solution.py:145
  216.2 15.9 %collective-permute-start.30 = (bf16[208,1024]{1,0:T(8,128)(2,1)S(1)}, bf16[208,1024]{1,0:T(8,128)(2,1)S(1)}, u32[]{:S(2)}, u32[]{:S(2)}) collective-permute-start(bf16[208,1024]{1,0:T(8,128)(2,1)S(1)} %slice.289), channel_id=1, source_target_pairs={{2,0},{6,2},{10,6},{14,10},{12,14},{8,12},{4,8},{0,4},{3,1},{7,3},... | collective-permute-start | bytes 1277960 | tf_op jit(solution)/shard_map/ppermute | solution.py:145
  216.7 15.4 %collective-permute-start.29 = (bf16[192,1024]{1,0:T(8,128)(2,1)S(1)}, bf16[192,1024]{1,0:T(8,128)(2,1)S(1)}, u32[]{:S(2)}, u32[]{:S(2)}) collective-permute-start(bf16[192,1024]{1,0:T(8,128)(2,1)S(1)} %slice.288), channel_id=1, source_target_pairs={{0,2},{2,6},{6,10},{10,14},{14,12},{12,8},{8,4},{4,0},{1,3},{3,7},... | collective-permute-start | bytes 1179656 | tf_op jit(solution)/shard_map/ppermute | solution.py:144
  238.1 11.2 %collective-permute-start.34 = (bf16[208,1024]{1,0:T(8,128)(2,1)S(1)}, bf16[208,1024]{1,0:T(8,128)(2,1)S(1)}, u32[]{:S(2)}, u32[]{:S(2)}) collective-permute-start(bf16[208,1024]{1,0:T(8,128)(2,1)S(1)} %slice.293), channel_id=1, source_target_pairs={{2,0},{6,2},{10,6},{14,10},{12,14},{8,12},{4,8},{0,4},{3,1},{7,3},... | collective-permute-start | bytes 1277960 | tf_op jit(solution)/shard_map/ppermute | solution.py:162
  249.5 18.5 %collective-permute-start.36 = (bf16[400,1024]{1,0:T(8,128)(2,1)S(1)}, bf16[400,1024]{1,0:T(8,128)(2,1)S(1)}, u32[]{:S(2)}, u32[]{:S(2)}) collective-permute-start(bf16[400,1024]{1,0:T(8,128)(2,1)S(1)} %pad_maximum_fusion.6), channel_id=1, source_target_pairs={{2,0},{6,2},{10,6},{14,10},{12,14},{8,12},{4,8},{0,4},{3,1},{7,3},... | collective-permute-start | bytes 2457608 | tf_op jit(solution)/shard_map/ppermute | solution.py:162
  250.0 18.1 %collective-permute-start.35 = (bf16[400,1024]{1,0:T(8,128)(2,1)S(1)}, bf16[400,1024]{1,0:T(8,128)(2,1)S(1)}, u32[]{:S(2)}, u32[]{:S(2)}) collective-permute-start(bf16[400,1024]{1,0:T(8,128)(2,1)S(1)} %pad_maximum_fusion.5), channel_id=1, source_target_pairs={{0,2},{2,6},{6,10},{10,14},{14,12},{12,8},{8,4},{4,0},{1,3},{3,7},... | collective-permute-start | bytes 2457608 | tf_op jit(solution)/shard_map/ppermute | solution.py:161
  268.7 20.9 %collective-permute-start.39 = (bf16[1024,1024]{1,0:T(8,128)(2,1)S(1)}, bf16[1024,1024]{1,0:T(8,128)(2,1)S(1)}, u32[]{:S(2)}, u32[]{:S(2)}) collective-permute-start(bf16[1024,1024]{1,0:T(8,128)(2,1)S(1)} %fusion.15), channel_id=1, source_target_pairs={{0,1},{1,0},{2,3},{3,2},{4,5},{5,4},{6,7},{7,6},{8,9},{9,8},{10,11... | collective-permute-start | bytes 6291464 | tf_op jit(solution)/shard_map/ppermute | solution.py:77
  268.8 20.8 %collective-permute-start.40 = (bf16[512,1024]{1,0:T(8,128)(2,1)S(1)}, bf16[512,1024]{1,0:T(8,128)(2,1)S(1)}, u32[]{:S(2)}, u32[]{:S(2)}) collective-permute-start(bf16[512,1024]{1,0:T(8,128)(2,1)S(1)} %fusion.29), channel_id=1, source_target_pairs={{0,1},{1,0},{2,3},{3,2},{4,5},{5,4},{6,7},{7,6},{8,9},{9,8},{10,11... | collective-permute-start | bytes 3145736 | tf_op jit(solution)/shard_map/ppermute | solution.py:77
  269.3 20.2 %collective-permute-start.38 = (bf16[400,1024]{1,0:T(8,128)(2,1)S(1)}, bf16[400,1024]{1,0:T(8,128)(2,1)S(1)}, u32[]{:S(2)}, u32[]{:S(2)}) collective-permute-start(bf16[400,1024]{1,0:T(8,128)(2,1)S(1)} %add.338), channel_id=1, source_target_pairs={{2,0},{6,2},{10,6},{14,10},{12,14},{8,12},{4,8},{0,4},{3,1},{7,3},... | collective-permute-start | bytes 2457608 | tf_op jit(solution)/shard_map/ppermute | solution.py:162
  269.6 19.9 %collective-permute-start.37 = (bf16[400,1024]{1,0:T(8,128)(2,1)S(1)}, bf16[400,1024]{1,0:T(8,128)(2,1)S(1)}, u32[]{:S(2)}, u32[]{:S(2)}) collective-permute-start(bf16[400,1024]{1,0:T(8,128)(2,1)S(1)} %add.337), channel_id=1, source_target_pairs={{0,2},{2,6},{6,10},{10,14},{14,12},{12,8},{8,4},{4,0},{1,3},{3,7},... | collective-permute-start | bytes 2457608 | tf_op jit(solution)/shard_map/ppermute | solution.py:161
  289.9 19.4 %collective-permute-start.42 = (bf16[400,1024]{1,0:T(8,128)(2,1)S(1)}, bf16[400,1024]{1,0:T(8,128)(2,1)S(1)}, u32[]{:S(2)}, u32[]{:S(2)}) collective-permute-start(bf16[400,1024]{1,0:T(8,128)(2,1)S(1)} %add.340), channel_id=1, source_target_pairs={{2,0},{6,2},{10,6},{14,10},{12,14},{8,12},{4,8},{0,4},{3,1},{7,3},... | collective-permute-start | bytes 2457608 | tf_op jit(solution)/shard_map/ppermute | solution.py:162
  291.2 19.5 %collective-permute-start.41 = (bf16[400,1024]{1,0:T(8,128)(2,1)S(1)}, bf16[400,1024]{1,0:T(8,128)(2,1)S(1)}, u32[]{:S(2)}, u32[]{:S(2)}) collective-permute-start(bf16[400,1024]{1,0:T(8,128)(2,1)S(1)} %add.339), channel_id=1, source_target_pairs={{0,2},{2,6},{6,10},{10,14},{14,12},{12,8},{8,4},{4,0},{1,3},{3,7},... | collective-permute-start | bytes 2457608 | tf_op jit(solution)/shard_map/ppermute | solution.py:161
  336.2 22.4 %collective-permute-start.48 = (bf16[256,512]{1,0:T(8,128)(2,1)S(1)}, bf16[256,512]{1,0:T(8,128)(2,1)S(1)}, u32[]{:S(2)}, u32[]{:S(2)}) collective-permute-start(bf16[256,512]{1,0:T(8,128)(2,1)S(1)} %get-tuple-element.469), channel_id=1, source_target_pairs={{0,2},{2,6},{6,10},{10,14},{14,12},{12,8},{8,4},{4,0},{1,3},{3,7},... | collective-permute-start | bytes 786440 | tf_op jit(solution)/shard_map/ppermute | solution.py:161
  337.6 21.0 %collective-permute-start.49 = (bf16[256,512]{1,0:T(8,128)(2,1)S(1)}, bf16[256,512]{1,0:T(8,128)(2,1)S(1)}, u32[]{:S(2)}, u32[]{:S(2)}) collective-permute-start(bf16[256,512]{1,0:T(8,128)(2,1)S(1)} %get-tuple-element.468), channel_id=1, source_target_pairs={{2,0},{6,2},{10,6},{14,10},{12,14},{8,12},{4,8},{0,4},{3,1},{7,3},... | collective-permute-start | bytes 786440 | tf_op jit(solution)/shard_map/ppermute | solution.py:162
  338.5 52.7 %collective-permute-start.47 = (bf16[384,1024]{1,0:T(8,128)(2,1)S(1)}, bf16[384,1024]{1,0:T(8,128)(2,1)S(1)}, u32[]{:S(2)}, u32[]{:S(2)}) collective-permute-start(bf16[384,1024]{1,0:T(8,128)(2,1)S(1)} %pad_maximum_fusion.11), channel_id=1, source_target_pairs={{2,0},{6,2},{10,6},{14,10},{12,14},{8,12},{4,8},{0,4},{3,1},{7,3},... | collective-permute-start | bytes 2359304 | tf_op jit(solution)/shard_map/ppermute | solution.py:162
  339.4 51.8 %collective-permute-start.46 = (bf16[384,1024]{1,0:T(8,128)(2,1)S(1)}, bf16[384,1024]{1,0:T(8,128)(2,1)S(1)}, u32[]{:S(2)}, u32[]{:S(2)}) collective-permute-start(bf16[384,1024]{1,0:T(8,128)(2,1)S(1)} %pad_maximum_fusion.10), channel_id=1, source_target_pairs={{0,2},{2,6},{6,10},{10,14},{14,12},{12,8},{8,4},{4,0},{1,3},{3,7},... | collective-permute-start | bytes 2359304 | tf_op jit(solution)/shard_map/ppermute | solution.py:161
  355.4 82.7 %collective-permute-start.62 = (bf16[512,1024]{1,0:T(8,128)(2,1)}, bf16[512,1024]{1,0:T(8,128)(2,1)}, u32[]{:S(2)}, u32[]{:S(2)}) collective-permute-start(bf16[512,1024]{1,0:T(8,128)(2,1)} %get-tuple-element.450), channel_id=1, source_target_pairs={{0,16},{16,0},{1,17},{17,1},{2,18},{18,2},{3,19},{19,3},{4,20},{20... | collective-permute-start | bytes 3145736 | tf_op jit(solution)/shard_map/ppermute | solution.py:1175
  358.8 15.5 %collective-permute-start.51 = (bf16[512,512]{1,0:T(8,128)(2,1)S(1)}, bf16[512,512]{1,0:T(8,128)(2,1)S(1)}, u32[]{:S(2)}, u32[]{:S(2)}) collective-permute-start(bf16[512,512]{1,0:T(8,128)(2,1)S(1)} %pad_maximum_fusion.16), channel_id=1, source_target_pairs={{2,0},{6,2},{10,6},{14,10},{12,14},{8,12},{4,8},{0,4},{3,1},{7,3},... | collective-permute-start | bytes 1572872 | tf_op jit(solution)/shard_map/ppermute | solution.py:162
  359.7 14.7 %collective-permute-start.50 = (bf16[512,512]{1,0:T(8,128)(2,1)S(1)}, bf16[512,512]{1,0:T(8,128)(2,1)S(1)}, u32[]{:S(2)}, u32[]{:S(2)}) collective-permute-start(bf16[512,512]{1,0:T(8,128)(2,1)S(1)} %pad_maximum_fusion.15), channel_id=1, source_target_pairs={{0,2},{2,6},{6,10},{10,14},{14,12},{12,8},{8,4},{4,0},{1,3},{3,7},... | collective-permute-start | bytes 1572872 | tf_op jit(solution)/shard_map/ppermute | solution.py:161
  374.5 20.6 %collective-permute-start.55 = (bf16[512,512]{1,0:T(8,128)(2,1)S(1)}, bf16[512,512]{1,0:T(8,128)(2,1)S(1)}, u32[]{:S(2)}, u32[]{:S(2)}) collective-permute-start(bf16[512,512]{1,0:T(8,128)(2,1)S(1)} %add.355), channel_id=1, source_target_pairs={{2,0},{6,2},{10,6},{14,10},{12,14},{8,12},{4,8},{0,4},{3,1},{7,3},... | collective-permute-start | bytes 1572872 | tf_op jit(solution)/shard_map/ppermute | solution.py:162
  375.4 19.7 %collective-permute-start.54 = (bf16[512,512]{1,0:T(8,128)(2,1)S(1)}, bf16[512,512]{1,0:T(8,128)(2,1)S(1)}, u32[]{:S(2)}, u32[]{:S(2)}) collective-permute-start(bf16[512,512]{1,0:T(8,128)(2,1)S(1)} %add.354), channel_id=1, source_target_pairs={{0,2},{2,6},{6,10},{10,14},{14,12},{12,8},{8,4},{4,0},{1,3},{3,7},... | collective-permute-start | bytes 1572872 | tf_op jit(solution)/shard_map/ppermute | solution.py:161
  391.5 40.8 %collective-permute-start.53 = (bf16[384,1024]{1,0:T(8,128)(2,1)S(1)}, bf16[384,1024]{1,0:T(8,128)(2,1)S(1)}, u32[]{:S(2)}, u32[]{:S(2)}) collective-permute-start(bf16[384,1024]{1,0:T(8,128)(2,1)S(1)} %add.353), channel_id=1, source_target_pairs={{2,0},{6,2},{10,6},{14,10},{12,14},{8,12},{4,8},{0,4},{3,1},{7,3},... | collective-permute-start | bytes 2359304 | tf_op jit(solution)/shard_map/ppermute | solution.py:162
  392.6 42.0 %collective-permute-start.52 = (bf16[384,1024]{1,0:T(8,128)(2,1)S(1)}, bf16[384,1024]{1,0:T(8,128)(2,1)S(1)}, u32[]{:S(2)}, u32[]{:S(2)}) collective-permute-start(bf16[384,1024]{1,0:T(8,128)(2,1)S(1)} %add.352), channel_id=1, source_target_pairs={{0,2},{2,6},{6,10},{10,14},{14,12},{12,8},{8,4},{4,0},{1,3},{3,7},... | collective-permute-start | bytes 2359304 | tf_op jit(solution)/shard_map/ppermute | solution.py:161
  395.2 25.0 %collective-permute-start.57 = (bf16[512,512]{1,0:T(8,128)(2,1)S(1)}, bf16[512,512]{1,0:T(8,128)(2,1)S(1)}, u32[]{:S(2)}, u32[]{:S(2)}) collective-permute-start(bf16[512,512]{1,0:T(8,128)(2,1)S(1)} %add.357), channel_id=1, source_target_pairs={{2,0},{6,2},{10,6},{14,10},{12,14},{8,12},{4,8},{0,4},{3,1},{7,3},... | collective-permute-start | bytes 1572872 | tf_op jit(solution)/shard_map/ppermute | solution.py:162
  396.1 25.2 %collective-permute-start.56 = (bf16[512,512]{1,0:T(8,128)(2,1)S(1)}, bf16[512,512]{1,0:T(8,128)(2,1)S(1)}, u32[]{:S(2)}, u32[]{:S(2)}) collective-permute-start(bf16[512,512]{1,0:T(8,128)(2,1)S(1)} %add.356), channel_id=1, source_target_pairs={{0,2},{2,6},{6,10},{10,14},{14,12},{12,8},{8,4},{4,0},{1,3},{3,7},... | collective-permute-start | bytes 1572872 | tf_op jit(solution)/shard_map/ppermute | solution.py:161
  432.3 19.2 %collective-permute-start.66 = (bf16[256,1024]{1,0:T(8,128)(2,1)}, bf16[256,1024]{1,0:T(8,128)(2,1)}, u32[]{:S(2)}, u32[]{:S(2)}) collective-permute-start(bf16[256,1024]{1,0:T(8,128)(2,1)} %get-tuple-element.454), channel_id=1, source_target_pairs={{0,16},{16,0},{1,17},{17,1},{2,18},{18,2},{3,19},{19,3},{4,20},{20... | collective-permute-start | bytes 1572872 | tf_op jit(solution)/shard_map/ppermute | solution.py:1175
  434.6 12.1 %collective-permute-start.63 = (bf16[384,1024]{1,0:T(8,128)(2,1)S(1)}, bf16[384,1024]{1,0:T(8,128)(2,1)}, u32[]{:S(2)}, u32[]{:S(2)}) collective-permute-start(bf16[384,1024]{1,0:T(8,128)(2,1)S(1)} %slice.449), channel_id=1, source_target_pairs={{0,1},{1,0},{2,3},{3,2},{4,5},{5,4},{6,7},{7,6},{8,9},{9,8},{10,11... | collective-permute-start | bytes 2359304 | tf_op jit(solution)/shard_map/ppermute | solution.py:77
  455.3 93.5 %all-gather.9.cloned.1.call-start = ((), (), s32[]{:S(2)}) async-start(), calls=%async_computation.2 | async-start | bytes 3145728 | tf_op jit(solution)/shard_map/all_gather | solution.py:1333
  467.2 11.5 %collective-permute-start.67 = (bf16[192,1024]{1,0:T(8,128)(2,1)}, bf16[192,1024]{1,0:T(8,128)(2,1)}, u32[]{:S(2)}, u32[]{:S(2)}) collective-permute-start(bf16[192,1024]{1,0:T(8,128)(2,1)} %add.379), channel_id=1, source_target_pairs={{0,2},{2,6},{6,10},{10,14},{14,12},{12,8},{8,4},{4,0},{1,3},{3,7},... | collective-permute-start | bytes 1179656 | tf_op jit(solution)/shard_map/ppermute | solution.py:161
  483.2 19.0 %collective-permute-start.71 = (bf16[384,1024]{1,0:T(8,128)(2,1)}, bf16[384,1024]{1,0:T(8,128)(2,1)}, u32[]{:S(2)}, u32[]{:S(2)}) collective-permute-start(bf16[384,1024]{1,0:T(8,128)(2,1)} %add.385), channel_id=1, source_target_pairs={{0,2},{2,6},{6,10},{10,14},{14,12},{12,8},{8,4},{4,0},{1,3},{3,7},... | collective-permute-start | bytes 2359304 | tf_op jit(solution)/shard_map/ppermute | solution.py:161
  485.9 18.5 %collective-permute-start.72 = (bf16[384,1024]{1,0:T(8,128)(2,1)}, bf16[384,1024]{1,0:T(8,128)(2,1)}, u32[]{:S(2)}, u32[]{:S(2)}) collective-permute-start(bf16[384,1024]{1,0:T(8,128)(2,1)} %add.387), channel_id=1, source_target_pairs={{2,0},{6,2},{10,6},{14,10},{12,14},{8,12},{4,8},{0,4},{3,1},{7,3},... | collective-permute-start | bytes 2359304 | tf_op jit(solution)/shard_map/ppermute | solution.py:162
  490.7 11.5 %collective-permute-start.74 = (bf16[96,1024]{1,0:T(8,128)(2,1)}, bf16[96,1024]{1,0:T(8,128)(2,1)S(1)}, u32[]{:S(2)}, u32[]{:S(2)}) collective-permute-start(bf16[96,1024]{1,0:T(8,128)(2,1)} %shard_step.1), channel_id=1, source_target_pairs={{0,16},{16,0},{1,17},{17,1},{2,18},{18,2},{3,19},{19,3},{4,20},{20... | collective-permute-start | bytes 589832 | tf_op jit(solution)/shard_map/ppermute | solution.py:205
  526.8 15.8 %collective-permute-start.89 = (bf16[224,1024]{1,0:T(8,128)(2,1)}, bf16[224,1024]{1,0:T(8,128)(2,1)}, u32[]{:S(2)}, u32[]{:S(2)}) collective-permute-start(bf16[224,1024]{1,0:T(8,128)(2,1)} %collective-permute-done.77.refs_0_), channel_id=1, source_target_pairs={{0,1},{1,0},{2,3},{3,2},{4,5},{5,4},{6,7},{7,6},{8,9},{9,8},{10,11... | collective-permute-start | bytes 1376264 | tf_op jit(solution)/shard_map/ppermute | solution.py:77
  526.8 15.8 %collective-permute-start.90 = (bf16[224,1024]{1,0:T(8,128)(2,1)}, bf16[224,1024]{1,0:T(8,128)(2,1)}, u32[]{:S(2)}, u32[]{:S(2)}) collective-permute-start(bf16[224,1024]{1,0:T(8,128)(2,1)} %collective-permute-done.78.refs_1_), channel_id=1, source_target_pairs={{0,1},{1,0},{2,3},{3,2},{4,5},{5,4},{6,7},{7,6},{8,9},{9,8},{10,11... | collective-permute-start | bytes 1376264 | tf_op jit(solution)/shard_map/ppermute | solution.py:77
  536.6 18.5 %collective-permute-start.85 = (bf16[112,1024]{1,0:T(8,128)(2,1)}, bf16[112,1024]{1,0:T(8,128)(2,1)S(1)}, u32[]{:S(2)}, u32[]{:S(2)}) collective-permute-start(bf16[112,1024]{1,0:T(8,128)(2,1)} %slice.348), channel_id=1, source_target_pairs={{0,2},{2,6},{6,10},{10,14},{14,12},{12,8},{8,4},{4,0},{1,3},{3,7},... | collective-permute-start | bytes 688136 | tf_op jit(solution)/shard_map/ppermute | solution.py:144
  540.7 14.4 %collective-permute-start.84 = (bf16[112,1024]{1,0:T(8,128)(2,1)S(1)}, bf16[112,1024]{1,0:T(8,128)(2,1)S(1)}, u32[]{:S(2)}, u32[]{:S(2)}) collective-permute-start(bf16[112,1024]{1,0:T(8,128)(2,1)S(1)} %slice.345), channel_id=1, source_target_pairs={{2,0},{6,2},{10,6},{14,10},{12,14},{8,12},{4,8},{0,4},{3,1},{7,3},... | collective-permute-start | bytes 688136 | tf_op jit(solution)/shard_map/ppermute | solution.py:145
  555.2 12.9 %collective-permute-start.86 = (bf16[224,1024]{1,0:T(8,128)(2,1)S(1)}, bf16[224,1024]{1,0:T(8,128)(2,1)S(1)}, u32[]{:S(2)}, u32[]{:S(2)}) collective-permute-start(bf16[224,1024]{1,0:T(8,128)(2,1)S(1)} %constant_dynamic-update-slice_fusion.4.refs_0_), channel_id=1, source_target_pairs={{0,1},{1,0},{2,3},{3,2},{4,5},{5,4},{6,7},{7,6},{8,9},{9,8},{10,11... | collective-permute-start | bytes 1376264 | tf_op jit(solution)/shard_map/ppermute | solution.py:77
  (172 other events, 2289.3 us)
Sparse Core Ops, SparseCore 0:
  70.2 42.9 all-gather.4
  115.3 21.6 all-gather.6
  455.4 19.4 all-gather.10
  476.9 37.9 all-gather.8
